TPU v7x, 32 devices: a whole 2x2x4 slice. The times are simulated.
32 devices in a mesh: ty: 2 (over x), tx: 4 (over y, core), items: 4 (over z).
Axes of the slice: x: 2, y: 2, z: 4, core: 2. Of those that a mesh axis runs over, the one named last changes fastest.
Arguments:
- inputs: float32 [128, 32, 3072], P('items', 'ty', 'tx'), may hold values from -300 to 300
- regions: int32 [128, 32, 32], P('items', 'ty', 'tx'), may hold values from 0 to 8, as said below
- lead_step_index: int32 [128], P('items'), may hold values from 0 to 13
- running_channel_mean: float32 [96], replicated, may hold values from -3 to 3
- running_channel_variance: float32 [96], replicated, may hold values from 0.5 to 4
- query_key_value_weight: float32 [96, 288], replicated, may hold values from -0.625 to 0.625
- query_value_bias: float32 [2, 96], replicated, may hold values from -3 to 3
- log_cosine_scale: float32 [3], replicated, may hold values from 1.8 to 2.6
- bias_net_weight1: float32 [2, 512], replicated, may hold values from -4 to 4
- bias_net_bias1: float32 [512], replicated, may hold values from -3 to 3
- bias_net_weight2: float32 [512, 3], replicated, may hold values from -0.125 to 0.125
- output_weight: float32 [96, 96], replicated, may hold values from -0.625 to 0.625
- projection_bias: float32 [96], replicated, may hold values from -3 to 3
- up_weight: float32 [96, 384], replicated, may hold values from -0.625 to 0.625
- up_bias: float32 [384], replicated, may hold values from -3 to 3
- down_weight: float32 [96, 384], replicated, may hold values from -0.3125 to 0.3125
- down_bias: float32 [96], replicated, may hold values from -3 to 3
- conditioned_norm_values: float32 [2, 4, 96], replicated, may hold values from -2 to 2
- cotangent: float32 [128, 32, 3072], P('items', 'ty', 'tx'), may hold values from -6 to 6
Outputs:
- outputs: float32 [128, 32, 3072], P('items', 'ty', 'tx')
- grad_inputs: float32 [128, 32, 3072], P('items', 'ty', 'tx')
- grad_w_qkv: float32 [96, 288], replicated
- grad_qv_bias: float32 [2, 96], replicated
- grad_logit_scale: float32 [3], replicated
- grad_cpb_w1: float32 [2, 512], replicated
- grad_cpb_b1: float32 [512], replicated
- grad_cpb_w2: float32 [512, 3], replicated
- grad_w_out: float32 [96, 96], replicated
- grad_b_out: float32 [96], replicated
- grad_w_up: float32 [96, 384], replicated
- grad_b_up: float32 [384], replicated
- grad_w_down: float32 [96, 384], replicated
- grad_b_down: float32 [96], replicated
- grad_norm_params: float32 [2, 4, 96], replicated
- new_mean: float32 [96], replicated
- new_var: float32 [96], replicated
Inputs may be any that keep to these rules, and one draw needn't show every extreme that they name: regions[b, r, c] = 3 * p + q. Along rows, an item is either wrapped (p = 0 for all rows) or cut (p = 0 for r < 24, 1 for r < 28, 2 for the rest); q likewise along columns with 32. Each item chooses for each dimension; some item is cut along both.
All inputs are finite; a program needn't handle non-finite values.
Results may differ from a plain program's by a relative error of at most 0.0003.
Values sent between devices are 32-bit elements; how exact they have to be, the bound alone decides.
No kernel may reach another device: no remote copies, remote signals or barrier semaphores. Data moves between devices by JAX's collectives and lax.ppermute only.
A program may use at most 128 MiB of HBM per device.

v0:
```python
from functools import partial

import jax
import jax.numpy as jnp
from jax import lax
from jax.sharding import PartitionSpec as P

ATTENTION_HEADS = 3
HEAD_DIM = 32
WINDOW = 8
SHIFT = 4
LEAD_STEPS = 14


precise_product = lax.Precision.HIGHEST
masked_score = -1000000000.0
norm_eps = 1e-05
unit_eps = 1e-06
momentum = 0.1


def from_behind(block, axis, distance):
    devices = range(lax.axis_size(axis))
    route = [((i - distance) % len(devices), i) for i in devices]
    return lax.ppermute(block, axis, route)


def windows_of(grid_field):
    batch_items, tile_rows, tile_cols = grid_field.shape[:3]
    trailing = grid_field.shape[3:]
    blocks = grid_field.reshape(
        (batch_items, tile_rows // WINDOW, WINDOW, tile_cols // WINDOW, WINDOW) + trailing
    )
    return jnp.moveaxis(blocks, 3, 2).reshape((-1, WINDOW * WINDOW) + trailing)


def grid_of(window_field, batch_items, tile_rows, tile_cols):
    trailing = window_field.shape[2:]
    blocks = window_field.reshape(
        (batch_items, tile_rows // WINDOW, tile_cols // WINDOW, WINDOW, WINDOW) + trailing
    )
    return jnp.moveaxis(blocks, 3, 2).reshape((batch_items, tile_rows, tile_cols) + trailing)


def relative_index():
    places = jnp.arange(WINDOW * WINDOW, dtype=jnp.int32)
    place_row = places // WINDOW
    place_col = places % WINDOW
    offset_row = place_row[:, None] - place_row[None, :] + WINDOW - 1
    offset_col = place_col[:, None] - place_col[None, :] + WINDOW - 1
    return offset_row * (2 * WINDOW - 1) + offset_col


def coordinate_table():
    offsets = jnp.arange((2 * WINDOW - 1) ** 2, dtype=jnp.int32)
    along_rows = (offsets // (2 * WINDOW - 1) - (WINDOW - 1)).astype(jnp.float32)
    along_cols = (offsets % (2 * WINDOW - 1) - (WINDOW - 1)).astype(jnp.float32)
    stacked = jnp.stack([along_rows, along_cols], -1) * (8.0 / (WINDOW - 1))
    return jnp.sign(stacked) * jnp.log2(jnp.abs(stacked) + 1.0) / 3.0


def position_bias_window(bias_net_weight1, bias_net_bias1, bias_net_weight2):
    hidden_units = jax.nn.gelu(
        jnp.dot(coordinate_table(), bias_net_weight1, precision=precise_product) + bias_net_bias1,
        approximate=False,
    )
    bias_table = 16.0 * jax.nn.sigmoid(
        jnp.dot(hidden_units, bias_net_weight2, precision=precise_product)
    )
    offset_ids = jnp.arange((2 * WINDOW - 1) ** 2, dtype=jnp.int32)
    one_hot = (relative_index().reshape(-1)[:, None] == offset_ids[None, :]).astype(jnp.float32)
    spread_out = jnp.dot(one_hot, bias_table, precision=precise_product)
    return jnp.transpose(
        spread_out.reshape(WINDOW * WINDOW, WINDOW * WINDOW, ATTENTION_HEADS), (2, 0, 1)
    )


def unit_rows(field):
    return field * lax.rsqrt(jnp.sum(field * field, -1, keepdims=True) + unit_eps)


def heads_of(field):
    return field.reshape(field.shape[:-1] + (ATTENTION_HEADS, HEAD_DIM))


def project_heads(windowed, query_key_value_weight, query_value_bias):
    feature_count = windowed.shape[-1]
    joined = jnp.einsum("wtc,ce->wte", windowed, query_key_value_weight, precision=precise_product)
    queries = joined[..., :feature_count] + query_value_bias[0]
    keys_raw = joined[..., feature_count : 2 * feature_count]
    values = joined[..., 2 * feature_count :] + query_value_bias[1]
    return (unit_rows(heads_of(queries)), unit_rows(heads_of(keys_raw)), heads_of(values))


def score_block(query_dir, key_dir, scale_head, relative_bias, same_region):
    cosine = jnp.einsum("wihd,wjhd->whij", query_dir, key_dir, precision=precise_product)
    scores = jnp.where(
        same_region, cosine * scale_head[None, :, None, None] + relative_bias[None], masked_score
    )
    return (cosine, scores)


def cond_norm(field, lead_time_value, params):
    centre = jnp.mean(field, -1, keepdims=True)
    centred = field - centre
    spread = jnp.mean(centred * centred, -1, keepdims=True)
    gain = 1.0 + params[0] + lead_time_value * params[1]
    return centred * lax.rsqrt(spread + norm_eps) * gain + params[2] + lead_time_value * params[3]


def post_block(
    back_rolled,
    normed,
    output_weight,
    projection_bias,
    up_weight,
    up_bias,
    down_weight,
    down_bias,
    conditioned_norm_values,
    lead_time_value,
):
    attn_out = (
        jnp.einsum("brcd,de->brce", back_rolled, output_weight, precision=precise_product)
        + projection_bias
    )
    first_sum = normed + cond_norm(attn_out, lead_time_value, conditioned_norm_values[0])
    hidden_units = jax.nn.gelu(
        jnp.einsum("brcd,de->brce", first_sum, up_weight, precision=precise_product) + up_bias,
        approximate=False,
    )
    branch = (
        jnp.einsum("brce,de->brcd", hidden_units, down_weight, precision=precise_product)
        + down_bias
    )
    return first_sum + cond_norm(branch, lead_time_value, conditioned_norm_values[1])


def roll_minus(grid_field):
    incoming = from_behind(grid_field[:, :SHIFT], "ty", -1)
    grid_field = jnp.concatenate([grid_field[:, SHIFT:], incoming], 1)
    incoming = from_behind(grid_field[:, :, :SHIFT], "tx", -1)
    return jnp.concatenate([grid_field[:, :, SHIFT:], incoming], 2)


def roll_plus(grid_field):
    incoming = from_behind(grid_field[:, -SHIFT:], "ty", 1)
    grid_field = jnp.concatenate([incoming, grid_field[:, :-SHIFT]], 1)
    incoming = from_behind(grid_field[:, :, -SHIFT:], "tx", 1)
    return jnp.concatenate([incoming, grid_field[:, :, :-SHIFT]], 2)


def shards(
    inputs,
    regions,
    lead_step_index,
    running_channel_mean,
    running_channel_variance,
    query_key_value_weight,
    query_value_bias,
    log_cosine_scale,
    bias_net_weight1,
    bias_net_bias1,
    bias_net_weight2,
    output_weight,
    projection_bias,
    up_weight,
    up_bias,
    down_weight,
    down_bias,
    conditioned_norm_values,
    cotangent,
):
    batch_items, tile_rows, flat_cols = inputs.shape
    feature_count = query_key_value_weight.shape[0]
    tile_cols = flat_cols // feature_count
    inputs = inputs.reshape(batch_items, tile_rows, tile_cols, feature_count)
    cotangent = cotangent.reshape(batch_items, tile_rows, tile_cols, feature_count)
    token_count = batch_items * tile_rows * tile_cols * lax.axis_size(("ty", "tx", "items"))
    chan_total = lax.psum(jnp.sum(inputs, (0, 1, 2)), ("ty", "tx", "items"))
    chan_mean = chan_total / token_count
    centred = inputs - chan_mean
    chan_var = lax.psum(jnp.sum(centred * centred, (0, 1, 2)), ("ty", "tx", "items")) / token_count
    inv_std = lax.rsqrt(chan_var + norm_eps)
    normed = centred * inv_std
    lead_time_value = ((lead_step_index + 1).astype(jnp.float32) / LEAD_STEPS).reshape(-1, 1, 1, 1)
    shifted = roll_minus(normed)
    (query_dir, key_dir, values), heads_pull = jax.vjp(
        project_heads, windows_of(shifted), query_key_value_weight, query_value_bias
    )
    relative_bias, bias_net_pullback = jax.vjp(
        position_bias_window, bias_net_weight1, bias_net_bias1, bias_net_weight2
    )
    region_win = windows_of(regions)
    same_region = region_win[:, None, :, None] == region_win[:, None, None, :]
    scale_head = jnp.exp(log_cosine_scale)
    cosine, scores = score_block(query_dir, key_dir, scale_head, relative_bias, same_region)
    row_top = jnp.max(scores, -1, keepdims=True)
    log_total = row_top + jnp.log(jnp.sum(jnp.exp(scores - row_top), -1, keepdims=True))
    attn_probs = jnp.exp(scores - log_total)
    mixed_win = jnp.einsum("whij,wjhd->wihd", attn_probs, values, precision=precise_product)
    window_count = mixed_win.shape[0]
    mixed_out = grid_of(
        mixed_win.reshape(window_count, WINDOW * WINDOW, ATTENTION_HEADS * HEAD_DIM),
        batch_items,
        tile_rows,
        tile_cols,
    )
    back_rolled = roll_plus(mixed_out)
    outputs, post_pull = jax.vjp(
        partial(post_block, lead_time_value=lead_time_value),
        back_rolled,
        normed,
        output_weight,
        projection_bias,
        up_weight,
        up_bias,
        down_weight,
        down_bias,
        conditioned_norm_values,
    )
    d_back, d_normed, g_w_out, g_b_out, g_w_up, g_b_up, g_w_down, g_b_down, g_norm = post_pull(
        cotangent
    )
    d_mixed = windows_of(roll_minus(d_back)).reshape(
        window_count, WINDOW * WINDOW, ATTENTION_HEADS, HEAD_DIM
    )
    cosine, scores = score_block(query_dir, key_dir, scale_head, relative_bias, same_region)
    attn_probs = jnp.exp(scores - log_total)
    d_values = jnp.einsum("whij,wihd->wjhd", attn_probs, d_mixed, precision=precise_product)
    d_probs = jnp.einsum("wihd,wjhd->whij", d_mixed, values, precision=precise_product)
    score_gradient = attn_probs * (d_probs - jnp.sum(attn_probs * d_probs, -1, keepdims=True))
    g_scale = jnp.sum(score_gradient * cosine, (0, 2, 3)) * scale_head
    d_cosine = score_gradient * scale_head[None, :, None, None]
    d_query = jnp.einsum("whij,wjhd->wihd", d_cosine, key_dir, precision=precise_product)
    d_key = jnp.einsum("whij,wihd->wjhd", d_cosine, query_dir, precision=precise_product)
    d_windowed, g_w_qkv, g_qv_bias = heads_pull((d_query, d_key, d_values))
    grad_bias_net_weight1, grad_bias_net_bias1, grad_bias_net_weight2 = bias_net_pullback(
        jnp.sum(score_gradient, 0)
    )
    d_normed = d_normed + roll_plus(grid_of(d_windowed, batch_items, tile_rows, tile_cols))
    sum_grad = jnp.sum(d_normed, (0, 1, 2))
    sum_cross = jnp.sum(d_normed * normed, (0, 1, 2))
    (
        g_w_out,
        g_b_out,
        g_w_up,
        g_b_up,
        g_w_down,
        g_b_down,
        g_norm,
        g_w_qkv,
        g_qv_bias,
        g_scale,
        grad_bias_net_weight1,
        grad_bias_net_bias1,
        grad_bias_net_weight2,
        sum_grad,
        sum_cross,
    ) = lax.psum(
        (
            g_w_out,
            g_b_out,
            g_w_up,
            g_b_up,
            g_w_down,
            g_b_down,
            g_norm,
            g_w_qkv,
            g_qv_bias,
            g_scale,
            grad_bias_net_weight1,
            grad_bias_net_bias1,
            grad_bias_net_weight2,
            sum_grad,
            sum_cross,
        ),
        ("ty", "tx", "items"),
    )
    grad_inputs = inv_std * (d_normed - sum_grad / token_count - normed * (sum_cross / token_count))
    new_mean = (1.0 - momentum) * running_channel_mean + momentum * chan_mean
    new_var = (1.0 - momentum) * running_channel_variance + momentum * chan_var * (
        token_count / (token_count - 1.0)
    )
    outputs = outputs.reshape(batch_items, tile_rows, flat_cols)
    grad_inputs = grad_inputs.reshape(batch_items, tile_rows, flat_cols)
    return (
        outputs,
        grad_inputs,
        g_w_qkv,
        g_qv_bias,
        g_scale,
        grad_bias_net_weight1,
        grad_bias_net_bias1,
        grad_bias_net_weight2,
        g_w_out,
        g_b_out,
        g_w_up,
        g_b_up,
        g_w_down,
        g_b_down,
        g_norm,
        new_mean,
        new_var,
    )


def solution(mesh):
    placed = (
        P("items", "ty", "tx"),
        P("items", "ty", "tx"),
        P("items"),
        P(),
        P(),
        P(),
        P(),
        P(),
        P(),
        P(),
        P(),
        P(),
        P(),
        P(),
        P(),
        P(),
        P(),
        P(),
        P("items", "ty", "tx"),
    )
    return jax.shard_map(
        shards,
        mesh=mesh,
        in_specs=placed,
        out_specs=(
            P("items", "ty", "tx"),
            P("items", "ty", "tx"),
            P(),
            P(),
            P(),
            P(),
            P(),
            P(),
            P(),
            P(),
            P(),
            P(),
            P(),
            P(),
            P(),
            P(),
            P(),
        ),
        check_vma=False,
    )
```

profile of v0, /device:TPU:0, one launch (start us, length us, event | category | flops | bytes accessed | tf_op | source)
XLA Modules:
  0.0 590.4 jit_solution(1961910714824930536)
XLA Ops:
  11.9 42.0 %psum.119 = f32[96]{0:T(128)S(1)} all-reduce(f32[96]{0:T(128)S(1)} %reduce_sum.399), channel_id=1, replica_groups=mesh['ty'=2,'tx'=4,'items'=4] {'ty','tx','items'}, use_global_device_ids=true, to_apply=%region_2.0 | all-reduce | flops 96 | bytes 768 | tf_op jit(solution)/shard_map/psum | solution.py:180
  56.2 40.2 %psum.120 = f32[96]{0:T(128)S(1)} all-reduce(f32[96]{0:T(128)S(1)} %reduce_sum.405), channel_id=1, replica_groups=mesh['ty'=2,'tx'=4,'items'=4] {'ty','tx','items'}, use_global_device_ids=true, to_apply=%region_5.0 | all-reduce | flops 96 | bytes 768 | tf_op jit(solution)/shard_map/psum | solution.py:183
  103.5 8.1 %collective-permute-done = f32[32,4,8,96]{3,0,2,1:T(8,128)S(1)} collective-permute-done((f32[32,4,8,96]{3,0,2,1:T(8,128)S(1)}, f32[32,4,8,96]{3,0,2,1:T(8,128)S(1)}, u32[]{:S(2)}, u32[]{:S(2)}) %collective-permute-start) | collective-permute-done | bytes 393248 | tf_op jit(solution)/shard_map/ppermute | solution.py:25
  146.4 10.6 %fusion.18 = (f32[64,3,64]{2,1,0:T(4,128)S(1)}, f32[64,3,64,64]{2,3,1,0:T(8,128)S(1)}) fusion(f32[3,64,64]{1,2,0:T(8,128)S(1)} %bitcast.176, f32[3]{0:T(128)S(1)} %exp.15, pred[64,64,64]{1,2,0:T(8,128)(4,1)S(1)} %copy-done.20, f32[64,64,3,32]{1,3,2,0:T(8,128)S(1)} %bitcast.159, f32[64,64,3]{1,2,0:T(4,128)S(1)} %get-tuple-element.119, ...), kind=kOutput, calls=%fused_computation.43 | convolution fusion | flops 305909760 | bytes 6750220 | tf_op jit(solution)/shard_map/wihd,wjhd->whij/dot_general | solution.py:96
  162.6 11.3 %convolution_bitcast_fusion = f32[64,64,3,32]{1,3,2,0:T(8,128)} fusion(f32[64,64,3,32]{1,3,2,0:T(8,128)S(1)} %bitcast.165, f32[64,3,64,64]{2,3,1,0:T(8,128)} %copy-done.2, f32[64,3,64]{2,1,0:T(4,128)S(1)} %log_add_fusion, f32[3,64,64]{1,2,0:T(8,128)S(1)} %bitcast.178, f32[3]{0:T(128)S(1)} %exp.15, pred[64,64,64]{1,2,0:T(8,128)(4,1)} %broadcast_compare_fusion), kind=kOutput, calls=%fused_computation.93 | convolution fusion | flops 305135616 | bytes 6651916 | tf_op jit(solution)/shard_map/whij,wjhd->wihd/dot_general | solution.py:201
  173.9 7.6 %copy.167 = f32[64,64,3,32]{3,2,1,0:T(4,128)} copy(f32[64,64,3,32]{1,3,2,0:T(8,128)} %convolution_bitcast_fusion) | data formatting | bytes 3145728 | tf_op jit(solution)/shard_map/whij,wjhd->wihd/transpose | solution.py:201
  181.4 7.9 %reshape_transpose_reshape_reshape.3 = f32[32,16,8,96]{3,2,1,0:T(8,128)S(1)} reshape(f32[64,64,3,32]{3,2,1,0:T(4,128)} %copy.167) | data formatting | bytes 3145728 | tf_op jit(solution)/shard_map/reshape;transpose;reshape;reshape | solution.py:42
  194.6 10.1 %collective-permute-done.2 = f32[32,4,8,96]{3,0,2,1:T(8,128)S(1)} collective-permute-done((f32[32,4,8,96]{3,0,2,1:T(8,128)S(1)}, f32[32,4,8,96]{3,0,2,1:T(8,128)S(1)}, u32[]{:S(2)}, u32[]{:S(2)}) %collective-permute-start.2) | collective-permute-done | bytes 393248 | tf_op jit(solution)/shard_map/ppermute | solution.py:25
  212.9 8.6 %collective-permute-done.3 = f32[32,16,4,96]{3,0,2,1:T(8,128)} collective-permute-done((f32[32,16,4,96]{3,0,2,1:T(8,128)}, f32[32,16,4,96]{3,0,2,1:T(8,128)}, u32[]{:S(2)}, u32[]{:S(2)}) %collective-permute-start.3) | collective-permute-done | bytes 786464 | tf_op jit(solution)/shard_map/ppermute | solution.py:25
  228.8 8.7 %convert_reduce_fusion.1 = (u32[16,8,384]{2,1,0:T(8,128)S(1)}, u32[16,8,384]{2,1,0:T(8,128)S(1)}, f32[32,16,8,384]{3,2,1,0:T(8,128)S(1)}) fusion(f32[384]{0:T(512)S(1)} %copy-done.71, f32[96,384]{1,0:T(8,128)S(1)} %copy-done, f32[32,16,8,96]{3,0,2,1:T(8,128)S(1)} %add_add_fusion.5), kind=kOutput, calls=%fused_computation.6 | convolution fusion | flops 1830715392 | bytes 8406528 | tf_op jit(solution)/shard_map/jvp(brcd,de->brce)/dot_general | solution.py:129
  237.5 14.3 %multiply_multiply_fusion.5 = (f32[32,16,8,384]{3,2,1,0:T(8,128)S(1)}, f32[32,16,8,384]{3,2,1,0:T(8,128)S(1)}) fusion(f32[32,16,8,384]{3,2,1,0:T(8,128)S(1)} %get-tuple-element.102, f32[384]{0:T(512)S(1)} %copy-done.71, u32[16,8,384]{2,1,0:T(8,128)S(1)} %get-tuple-element.18, u32[16,8,384]{2,1,0:T(8,128)S(1)} %get-tuple-element.17), kind=kLoop, calls=%fused_computation.35 | loop fusion | flops 106954752 | bytes 19269120 | tf_op jit(solution)/shard_map/jvp()/mul | solution.py:128
  270.7 9.8 %fusion.118 = (f32[384]{0:T(512)}, f32[32,16,8,384]{3,2,1,0:T(8,128)S(1)}) fusion(f32[32,16,8,384]{3,2,1,0:T(8,128)S(1)} %get-tuple-element.63, f32[96,384]{1,0:T(8,128)S(1)} %copy-done.50, f32[32,16,8,96]{3,0,2,1:T(8,128)S(1)} %get-tuple-element.55, f32[32,16,8,384]{3,2,1,0:T(8,128)S(1)} %get-tuple-element.102, f32[384]{0:T(512)S(1)} %copy-done.71), kind=kOutput, calls=%fused_computation.251 | convolution fusion | flops 1835531904 | bytes 20597760 | tf_op jit(solution)/shard_map/transpose(jvp(brce,de->brcd))/dot_general | solution.py:133
  314.7 8.6 %fusion.48 = f32[96,384]{1,0:T(8,128)} fusion(f32[32,16,8,96]{3,0,2,1:T(8,128)S(1)} %copy-done.32, f32[32,16,8,384]{3,2,1,0:T(8,128)S(1)} %bitcast.164), kind=kOutput, calls=%fused_computation.111 | convolution fusion | flops 1811939328 | bytes 8011776 | tf_op jit(solution)/shard_map/transpose(jvp(brce,de->brcd))/dot_general | solution.py:133
  323.3 8.8 %fusion.45 = f32[96,384]{1,0:T(8,128)} fusion(f32[32,16,8,96]{3,0,2,1:T(8,128)S(1)} %copy-done.26, f32[32,16,8,384]{3,2,1,0:T(8,128)S(1)} %bitcast.168), kind=kOutput, calls=%fused_computation.110 | convolution fusion | flops 1811939328 | bytes 8011776 | tf_op jit(solution)/shard_map/transpose(jvp(brcd,de->brce))/dot_general | solution.py:129
  339.5 8.0 %copy.178 = f32[64,64,3,32]{1,3,2,0:T(8,128)} copy(f32[64,64,3,32]{3,2,1,0:T(4,128)} %reshape_reshape_transpose_reshape.3) | data formatting | bytes 3145728 | tf_op jit(solution)/shard_map/reshape;reshape;transpose;reshape | solution.py:225
  347.5 16.7 %bitcast_reduce_fusion = (f32[3,32]{1,0:T(4,128)}, f32[64,3,32,64]{3,2,1,0:T(8,128)}) fusion(f32[64,64,3,32]{1,3,2,0:T(8,128)} %copy.178, f32[64,3,64,64]{2,3,1,0:T(8,128)} %copy-done.2, f32[64,3,64]{2,1,0:T(4,128)S(1)} %log_add_fusion, f32[3,64,64]{1,2,0:T(8,128)S(1)} %bitcast.179, f32[3]{0:T(128)S(1)} %exp.15, pred[64,64,64]{1,2,0:T(8,128)(4,1)S(1)} %copy-done.21), kind=kOutput, calls=%fused_computation.50 | convolution fusion | flops 305528736 | bytes 6652300 | tf_op jit(solution)/shard_map/whij,wihd->wjhd/dot_general | solution.py:230
  364.2 10.9 %multiply_reduce_fusion.1 = (f32[64,3,64]{2,1,0:T(4,128)S(1)}, f32[64,3,64,64]{2,3,1,0:T(8,128)S(1)}) fusion(f32[64,3,64]{2,1,0:T(4,128)S(1)} %log_add_fusion, f32[3,64,64]{1,2,0:T(8,128)S(1)} %bitcast.180, f32[64,3,64,64]{2,3,1,0:T(8,128)S(1)} %bitcast.152, f32[3]{0:T(128)S(1)} %exp.15, pred[64,64,64]{1,2,0:T(8,128)(4,1)S(1)} %copy-done.21, ...), kind=kOutput, calls=%fused_computation.14 | convolution fusion | flops 306696192 | bytes 9846796 | tf_op jit(solution)/shard_map/wihd,wjhd->whij/dot_general | solution.py:231
  380.5 12.3 %fusion.20 = (f32[64,64,3]{1,2,0:T(4,128)}, f32[64,3,32,64]{3,2,1,0:T(8,128)}) fusion(f32[64,64,3,32]{1,3,2,0:T(8,128)S(1)} %bitcast.160, f32[64,3,64,64]{2,3,1,0:T(8,128)S(1)} %get-tuple-element.56, f32[3]{0:T(128)S(1)} %exp.15, f32[64,64,3,32]{1,3,2,0:T(8,128)S(1)} %bitcast.155, f32[64,64,3]{1,2,0:T(4,128)S(1)} %copy-done.35), kind=kOutput, calls=%fused_computation.49 | convolution fusion | flops 303943680 | bytes 7962636 | tf_op jit(solution)/shard_map/whij,wihd->wjhd/dot_general | solution.py:236
  392.8 8.8 %fusion.19 = (f32[64,64,3]{1,2,0:T(4,128)}, f32[64,3,32,64]{3,2,1,0:T(8,128)}) fusion(f32[64,64,3,32]{1,3,2,0:T(8,128)S(1)} %bitcast.156, f32[64,3,64,64]{2,3,1,0:T(8,128)S(1)} %get-tuple-element.56, f32[3]{0:T(128)S(1)} %exp.15, f32[64,64,3,32]{1,3,2,0:T(8,128)S(1)} %bitcast.161, f32[64,64,3]{1,2,0:T(4,128)S(1)} %copy-done.37), kind=kOutput, calls=%fused_computation.46 | convolution fusion | flops 303943680 | bytes 7962636 | tf_op jit(solution)/shard_map/whij,wjhd->wihd/dot_general | solution.py:235
  422.2 8.9 %fusion.15 = f32[64,64,96]{2,1,0:T(8,128)S(1)} fusion(f32[64,64,96]{2,1,0:T(8,128)} %copy.185, f32[64,64,96]{2,1,0:T(8,128)} %copy.183, f32[64,64,96]{2,1,0:T(8,128)S(1)} %copy-done.27, f32[96,288]{1,0:T(8,128)S(1)} %copy-done.45), kind=kOutput, calls=%fused_computation.39 | convolution fusion | flops 1361313792 | bytes 6402048 | tf_op jit(solution)/shard_map/transpose(jvp(wtc,ce->wte))/dot_general | solution.py:88
  437.4 9.7 %fusion.51 = f32[96,288]{1,0:T(8,128)} fusion(f32[64,64,96]{2,1,0:T(8,128)S(1)} %bitcast.170, f32[64,64,96]{2,1,0:T(8,128)} %copy.185, f32[64,64,96]{2,1,0:T(8,128)} %copy.183, f32[64,64,96]{2,1,0:T(8,128)} %copy.180), kind=kOutput, calls=%fused_computation.112 | convolution fusion | flops 1361313792 | bytes 6402048 | tf_op jit(solution)/shard_map/transpose(jvp(wtc,ce->wte))/dot_general | solution.py:88
  455.3 10.8 %collective-permute-done.7 = f32[32,16,4,96]{3,0,2,1:T(8,128)} collective-permute-done((f32[32,16,4,96]{3,0,2,1:T(8,128)}, f32[32,16,4,96]{3,0,2,1:T(8,128)}, u32[]{:S(2)}, u32[]{:S(2)}) %collective-permute-start.7) | collective-permute-done | bytes 786464 | tf_op jit(solution)/shard_map/ppermute | solution.py:25
  468.9 40.1 %all-reduce.15 = (f32[96]{0:T(128)S(1)}, f32[96]{0:T(128)S(1)}, f32[2,96]{1,0:T(2,128)}, f32[3]{0:T(128)}, f32[2,512]{1,0:T(2,128)}, /*index=5*/f32[512]{0:T(512...) all-reduce(f32[96]{0:T(128)S(1)} %get-tuple-element.28, ...), channel_id=1, replica_groups=mesh['ty'=2,'tx'=4,'items'=4] {'ty','tx','items'}, use_global_device_ids=true, to_apply=%region_24.25 | all-reduce | flops 14019 | bytes 112152 | tf_op jit(solution)/shard_map/psum | solution.py:260
  515.3 63.3 %all-reduce.19.cloned.1.call-done = (f32[96,288]{1,0:T(8,128)}, f32[96,384]{1,0:T(8,128)}, f32[96,384]{1,0:T(8,128)}) async-done(((f32[96,288]{1,0:T(8,128)}, f32[96,384]{1,0:T(8,128)}, f32[96,384]{1,0:T(8,128)}), (f32[96,288]{1,0:T(8,128)}, f32[96,384]{1,0:T(8,128)}, f32[96,384]{1,0:T(8,128)})) %all-reduce.19.cloned.1.call-update) | async-done | bytes 405520 | tf_op jit(solution)/shard_map/psum | solution.py:260
  (319 shorter events, 188.6 us)
Async XLA Ops:
  7.2 221.6 %copy-start = (f32[96,384]{1,0:T(8,128)S(1)}, f32[96,384]{1,0:T(8,128)}, u32[]{:S(2)}) copy-start(f32[96,384]{1,0:T(8,128)} %param.32) | copy-start | bytes 442372
  7.2 46.7 %copy-start.77 = (f32[96]{0:T(128)S(1)}, f32[96]{0:T(128)}, u32[]{:S(2)}) copy-start(f32[96]{0:T(128)} %param.22) | copy-start | bytes 1156
  7.2 89.2 %copy-start.78 = (f32[96]{0:T(128)S(1)}, f32[96]{0:T(128)}, u32[]{:S(2)}) copy-start(f32[96]{0:T(128)} %param.23) | copy-start | bytes 1156
  7.2 571.4 %all-reduce.19.cloned.1.call-start = ((), (), s32[]{:S(2)}) async-start(), calls=%async_computation | async-start | bytes 884736 | tf_op jit(solution)/shard_map/psum | solution.py:260
  9.5 88.7 %copy-start.11 = (f32[32,16,8,96]{3,2,1,0:T(8,128)}, f32[32,16,8,96]{3,2,1,0:T(8,128)S(1)}, u32[]{:S(2)}) copy-start(f32[32,16,8,96]{3,2,1,0:T(8,128)S(1)} %reshape.663) | copy-start | bytes 4718596
  54.4 172.5 %copy-start.52 = (f32[96]{0:T(128)}, f32[96]{0:T(128)S(1)}, u32[]{:S(2)}) copy-start(f32[96]{0:T(128)S(1)} %get-tuple-element.91) | copy-start | bytes 1156
  54.5 46.1 %copy-start.79 = (f32[2,512]{1,0:T(2,128)S(1)}, f32[2,512]{1,0:T(2,128)}, u32[]{:S(2)}) copy-start(f32[2,512]{1,0:T(2,128)} %param.27) | copy-start | bytes 12292
  54.5 46.1 %copy-start.80 = (f32[512]{0:T(512)S(1)}, f32[512]{0:T(512)}, u32[]{:S(2)}) copy-start(f32[512]{0:T(512)} %param.28) | copy-start | bytes 6148
  98.2 13.4 %collective-permute-start = (f32[32,4,8,96]{3,0,2,1:T(8,128)S(1)}, f32[32,4,8,96]{3,0,2,1:T(8,128)S(1)}, u32[]{:S(2)}, u32[]{:S(2)}) collective-permute-start(f32[32,4,8,96]{3,0,2,1:T(8,128)S(1)} %slice.135), channel_id=1, source_target_pairs={{16,0},{0,16},{17,1},{1,17},{18,2},{2,18},{19,3},{3,19},{20,4},{4,... | collective-permute-start | bytes 1179656 | tf_op jit(solution)/shard_map/ppermute | solution.py:25
  111.8 12.5 %collective-permute-start.1 = (f32[32,16,4,96]{3,0,2,1:T(8,128)S(1)}, f32[32,16,4,96]{3,0,2,1:T(8,128)}, u32[]{:S(2)}, u32[]{:S(2)}) collective-permute-start(f32[32,16,4,96]{3,0,2,1:T(8,128)S(1)} %get-tuple-element.75), channel_id=1, source_target_pairs={{4,0},{8,4},{12,8},{0,12},{5,1},{9,5},{13,9},{1,13},{6,2},{10,6},{... | collective-permute-start | bytes 2359304 | tf_op jit(solution)/shard_map/ppermute | solution.py:25
  190.6 14.0 %collective-permute-start.2 = (f32[32,4,8,96]{3,0,2,1:T(8,128)S(1)}, f32[32,4,8,96]{3,0,2,1:T(8,128)S(1)}, u32[]{:S(2)}, u32[]{:S(2)}) collective-permute-start(f32[32,4,8,96]{3,0,2,1:T(8,128)S(1)} %copy.203), channel_id=1, source_target_pairs={{16,0},{0,16},{17,1},{1,17},{18,2},{2,18},{19,3},{3,19},{20,4},{4,... | collective-permute-start | bytes 1179656 | tf_op jit(solution)/shard_map/ppermute | solution.py:25
  206.8 14.7 %collective-permute-start.3 = (f32[32,16,4,96]{3,0,2,1:T(8,128)}, f32[32,16,4,96]{3,0,2,1:T(8,128)}, u32[]{:S(2)}, u32[]{:S(2)}) collective-permute-start(f32[32,16,4,96]{3,0,2,1:T(8,128)} %get-tuple-element.72), channel_id=1, source_target_pairs={{12,0},{0,4},{4,8},{8,12},{13,1},{1,5},{5,9},{9,13},{14,2},{2,6},{... | collective-permute-start | bytes 2359304 | tf_op jit(solution)/shard_map/ppermute | solution.py:25
  228.8 38.0 %copy-start.25 = (f32[32,16,8,96]{3,0,2,1:T(8,128)}, f32[32,16,8,96]{3,0,2,1:T(8,128)S(1)}, u32[]{:S(2)}) copy-start(f32[32,16,8,96]{3,0,2,1:T(8,128)S(1)} %add_add_fusion.5) | copy-start | bytes 4718596
  297.5 15.4 %collective-permute-start.4 = (f32[32,4,8,96]{3,0,2,1:T(8,128)}, f32[32,4,8,96]{3,0,2,1:T(8,128)}, u32[]{:S(2)}, u32[]{:S(2)}) collective-permute-start(f32[32,4,8,96]{3,0,2,1:T(8,128)} %slice.146), channel_id=1, source_target_pairs={{16,0},{0,16},{17,1},{1,17},{18,2},{2,18},{19,3},{3,19},{20,4},{4,... | collective-permute-start | bytes 1179656 | tf_op jit(solution)/shard_map/ppermute | solution.py:25
  314.4 17.6 %collective-permute-start.5 = (f32[32,16,4,96]{3,0,2,1:T(8,128)S(1)}, f32[32,16,4,96]{3,0,2,1:T(8,128)S(1)}, u32[]{:S(2)}, u32[]{:S(2)}) collective-permute-start(f32[32,16,4,96]{3,0,2,1:T(8,128)S(1)} %get-tuple-element.71), channel_id=1, source_target_pairs={{4,0},{8,4},{12,8},{0,12},{5,1},{9,5},{13,9},{1,13},{6,2},{10,6},{... | collective-permute-start | bytes 2359304 | tf_op jit(solution)/shard_map/ppermute | solution.py:25
  339.5 24.8 %slice-start = ((s8[6291456]{0:T(1024)(128)(4,1)}), s8[2097152]{0:T(1024)(128)(4,1)S(1)}, s32[]{:S(2)}) async-start(s8[6291456]{0:T(1024)(128)(4,1)} %bitcast.151), calls=%async_computation.1 | async-start | bytes 4194304
  347.5 16.8 %slice-start.1 = ((s8[6291456]{0:T(1024)(128)(4,1)}), s8[4194304]{0:T(1024)(128)(4,1)S(1)}, s32[]{:S(2)}) async-start(s8[6291456]{0:T(1024)(128)(4,1)} %bitcast.151), calls=%async_computation.2 | async-start | bytes 8388608
  347.5 16.8 %copy-start.17 = (f32[64,64,3,32]{1,3,2,0:T(8,128)S(1)}, f32[64,64,3,32]{1,3,2,0:T(8,128)}, u32[]{:S(2)}) copy-start(f32[64,64,3,32]{1,3,2,0:T(8,128)} %copy.178) | copy-start | bytes 4718596
  347.5 16.8 %copy-start.19 = (f32[64,64,96]{1,2,0:T(8,128)S(1)}, f32[64,64,96]{1,2,0:T(8,128)}, u32[]{:S(2)}) copy-start(f32[64,64,96]{1,2,0:T(8,128)} %copy-done.18) | copy-start | bytes 4718596
  432.8 14.4 %collective-permute-start.6 = (f32[32,4,8,96]{3,0,2,1:T(8,128)S(1)}, f32[32,4,8,96]{3,0,2,1:T(8,128)S(1)}, u32[]{:S(2)}, u32[]{:S(2)}) collective-permute-start(f32[32,4,8,96]{3,0,2,1:T(8,128)S(1)} %copy.205), channel_id=1, source_target_pairs={{16,0},{0,16},{17,1},{1,17},{18,2},{2,18},{19,3},{3,19},{20,4},{4,... | collective-permute-start | bytes 1179656 | tf_op jit(solution)/shard_map/ppermute | solution.py:25
  449.5 16.6 %copy-start.13 = (f32[32,16,8,96]{3,2,1,0:T(8,128)S(1)}, f32[32,16,8,96]{3,2,1,0:T(8,128)}, u32[]{:S(2)}) copy-start(f32[32,16,8,96]{3,2,1,0:T(8,128)} %copy-done.11) | copy-start | bytes 4718596
  449.5 16.5 %copy-start.53 = (f32[96]{0:T(128)S(1)}, f32[96]{0:T(128)}, u32[]{:S(2)}) copy-start(f32[96]{0:T(128)} %copy-done.52) | copy-start | bytes 1156
  450.8 15.3 %collective-permute-start.7 = (f32[32,16,4,96]{3,0,2,1:T(8,128)}, f32[32,16,4,96]{3,0,2,1:T(8,128)}, u32[]{:S(2)}, u32[]{:S(2)}) collective-permute-start(f32[32,16,4,96]{3,0,2,1:T(8,128)} %get-tuple-element.68), channel_id=1, source_target_pairs={{12,0},{0,4},{4,8},{8,12},{13,1},{1,5},{5,9},{9,13},{14,2},{2,6},{... | collective-permute-start | bytes 2359304 | tf_op jit(solution)/shard_map/ppermute | solution.py:25
  512.2 71.1 %copy-start.1 = (f32[96,384]{1,0:T(8,128)S(1)}, f32[96,384]{1,0:T(8,128)}, u32[]{:S(2)}) copy-start(f32[96,384]{1,0:T(8,128)} %param.32) | copy-start | bytes 442372
  (76 other events, 458.4 us)
Sparse Core Ops, SparseCore 0:
  451.3 127.2 all-reduce.18
where the time goes:
time: 597 us; the launch traced here: 590 us
  matrix products  165 us (28%)
  blocking collectives  122 us (20%)
  waiting for transfers between devices  108 us (18%)
  local copies, waits for them, and re-layouts  87.2 us (15%)
  other arithmetic  84 us (14%)
  between operations  15.7 us (3%)
  starting transfers between devices  8.33 us (1%)
    psum x1, waiting for transfers between devices, shards(): lax.psum((g_w_out, g_b_out, g_w_up, g_b_up, g_w_down, g_b_down, g_norm, g...  63.3 us
    ppermute x8, waiting for transfers between devices, from_behind(): return lax.ppermute(block, axis, route)  45 us
    psum x1, blocking collectives, shards(): chan_total = lax.psum(jnp.sum(inputs, (0, 1, 2)), ('ty', 'tx', 'items'))  42 us
    psum x1, blocking collectives, shards(): lax.psum(jnp.sum(centred * centred, (0, 1, 2)), ('ty', 'tx', 'items'))  40.2 us
    psum x1, blocking collectives, shards(): lax.psum((g_w_out, g_b_out, g_w_up, g_b_up, g_w_down, g_b_down, g_norm, g...  40.1 us
    dot_general x3, matrix products, project_heads(): jnp.einsum('wtc,ce->wte', windowed, query_key_value_weight, precision=pre...  24.4 us
    dot_general x3, matrix products, post_block(): jnp.einsum('brce,de->brcd', hidden_units, down_weight, precision=precise_...  24.2 us
    dot_general x3, matrix products, post_block(): jnp.einsum('brcd,de->brce', first_sum, up_weight, precision=precise_product)  23.6 us
  transfers between devices with their start and end apart: 9, of which 7 were waited for; matrix products, arithmetic and copies ran while one was open for 12% of the time, Pallas kernels for 0%

commit v1 on v0

v1 whole, which is shorter than its diff:
```python
from functools import partial

import jax
import jax.numpy as jnp
from jax import lax
from jax.experimental import pallas as pl
from jax.experimental.pallas import tpu as pltpu
from jax.sharding import PartitionSpec as P

HEADS = 3
HEAD_DIM = 32
WIDTH = 96
HIDDEN = 384
WINDOW = 8
SHIFT = 4
LEAD_STEPS = 14
PLACES = WINDOW * WINDOW
SPAN = 2 * WINDOW - 1
PAIR = 2 * PLACES
LANES = 128

masked_score = -1000000000.0
norm_eps = 1e-05
unit_eps = 1e-06
momentum = 0.1
axes_all = ("ty", "tx", "items")

f32 = jnp.float32
bf16 = jnp.bfloat16

normal_slope = 0.28
normal_poly = (
    0.11652074430372011,
    0.06749697235753221,
    0.26890961436457633,
    -0.23699279280357777,
    0.389873590681989,
    -0.10580813816203069,
)


def dot(a, b):
    return lax.dot_general(a, b, (((1,), (0,)), ((), ())), preferred_element_type=f32)


def dot_rows(a, b):
    return lax.dot_general(a, b, (((1,), (1,)), ((), ())), preferred_element_type=f32)


def split(x):
    hi = x.astype(bf16)
    return hi, (x - hi.astype(f32)).astype(bf16)


def normal_parts(u):
    a = jnp.abs(u)
    t = 1.0 / (1.0 + normal_slope * a)
    bell = jnp.exp(-0.5 * u * u)
    poly = normal_poly[-1] * t + normal_poly[-2]
    for c in normal_poly[-3::-1]:
        poly = poly * t + c
    tail = poly * t * bell
    return jnp.where(u < 0, tail, 1.0 - tail), bell * 0.3989422804014327


def stats_kernel(x_ref, out_ref):
    items, rows, flat = x_ref.shape
    cols = flat // WIDTH
    count = items * rows * cols

    def fold(v):
        total = v[:, :WIDTH]
        for j in range(1, cols):
            total = total + v[:, j * WIDTH : (j + 1) * WIDTH]
        return jnp.sum(total, 0, keepdims=True)

    def add(i, acc):
        return acc + x_ref[i, 0:8, :] + x_ref[i, 8:16, :]

    zero = jnp.zeros((8, flat), f32)
    mean = fold(lax.fori_loop(0, items, add, zero)) * (1.0 / count)
    spread = jnp.concatenate([mean] * cols, 1)

    def add_square(i, acc):
        lo = x_ref[i, 0:8, :] - spread
        hi = x_ref[i, 8:16, :] - spread
        return acc + lo * lo + hi * hi

    square = fold(lax.fori_loop(0, items, add_square, zero))
    out_ref[...] = jnp.concatenate(
        [mean, square, jnp.zeros((6, WIDTH), f32)], 0
    )


def local_stats(x):
    return pl.pallas_call(
        stats_kernel,
        out_shape=jax.ShapeDtypeStruct((8, WIDTH), f32),
        compiler_params=pltpu.CompilerParams(vmem_limit_bytes=32 * 1024 * 1024),
    )(x)


def stack_rows(hi, lo):
    return jnp.concatenate([hi, lo], 0)


def block_kernel(
    step_items,
    flags_ref,
    lead_ref,
    x_own,
    x_right,
    x_down,
    x_corner,
    ct_own,
    ct_right,
    ct_down,
    ct_corner,
    affine_ref,
    w_qkv_ref,
    w_out_ref,
    w_up_ref,
    w_down_ref,
    cols_ref,
    up_bias_ref,
    scale_ref,
    bias_ref,
    out_lo,
    out_ld,
    out_ro,
    out_rd,
    dn_lo,
    dn_ld,
    dn_ro,
    dn_rd,
    g_qkv_ref,
    g_out_ref,
    g_up_ref,
    g_down_ref,
    sums_ref,
    dpos_ref,
    dcos_ref,
    qkv_f,
    out_f,
    up_f,
    down_f,
    down_b,
    up_b,
    out_b,
    qkv_b,
    down_f_hi,
    up_b_hi,
    qkv_b_hi,
):
    step = pl.program_id(0)
    last = pl.num_programs(0) - 1

    def packed(w):
        hi, lo = split(w)
        return jnp.concatenate(
            [jnp.concatenate([hi, hi], 1), jnp.concatenate([lo, jnp.zeros_like(lo)], 1)], 0
        )

    @pl.when(step == 0)
    def _():
        w = w_qkv_ref[...]
        qkv_f[...] = packed(w.T)
        hi, lo = split(w)
        qkv_b[...] = stack_rows(hi, lo)
        qkv_b_hi[...] = hi
        w = w_out_ref[...]
        out_f[...] = packed(w.T)
        out_b[...] = packed(w)
        w = w_up_ref[...]
        up_f[...] = packed(w.T)
        hi, lo = split(w)
        up_b[...] = stack_rows(hi, lo)
        up_b_hi[...] = hi
        w = w_down_ref[...]
        down_b[...] = packed(w.T)
        hi, lo = split(w)
        down_f[...] = stack_rows(hi, lo)
        down_f_hi[...] = hi
        g_qkv_ref[...] = jnp.zeros_like(g_qkv_ref)
        g_out_ref[...] = jnp.zeros_like(g_out_ref)
        g_up_ref[...] = jnp.zeros_like(g_up_ref)
        g_down_ref[...] = jnp.zeros_like(g_down_ref)
        sums_ref[...] = jnp.zeros_like(sums_ref)
        dpos_ref[...] = jnp.zeros_like(dpos_ref)
        dcos_ref[...] = jnp.zeros_like(dcos_ref)

    first_half = lax.broadcasted_iota(jnp.int32, (1, PAIR), 1) < PLACES

    def narrow(weight, x_hi, x_lo):
        r = dot(weight, stack_rows(x_hi, x_lo))
        m = weight.shape[0] // 2
        return r[:m] + r[m:]

    def wide(weight, weight_hi, x_hi, x_lo):
        r = dot(weight, x_hi)
        m = weight_hi.shape[0]
        return (r[:m] + r[m:]) + dot(weight_hi, x_lo)

    def halves(v):
        m = v.shape[0] // 2
        return jnp.where(first_half, v[:m], v[m:])

    def col(i):
        return cols_ref[i]

    def per_item(fn):
        return jnp.concatenate([fn(m) for m in range(step_items)], 1)

    def spread_cols(i):
        c = col(i)
        return jnp.concatenate([c] * step_items, 1)

    def gather(own, right, down, corner, m):
        top_l = own[m, SHIFT : SHIFT + WINDOW, HIDDEN:]
        top_r = right[m, 0:WINDOW, :]
        low_l = jnp.concatenate([own[m, SHIFT + WINDOW :, HIDDEN:], down[m]], 0)
        low_r = jnp.concatenate([right[m, WINDOW:, :], corner[m]], 0)
        tiles = [
            part[:, j * WIDTH : (j + 1) * WIDTH]
            for part in (top_l, top_r, low_l, low_r)
            for j in range(4)
        ]
        return jnp.concatenate(tiles, 0).T

    def scatter(value, lo, ld, ro, rd, m):
        rows = value.T
        parts = [
            jnp.concatenate([rows[(4 * s + j) * 8 : (4 * s + j + 1) * 8] for j in range(4)], 1)
            for s in range(4)
        ]
        lo[m, 0:WINDOW] = parts[0]
        ro[m, 0:WINDOW] = parts[1]
        lo[m, WINDOW:] = parts[2][:SHIFT]
        ro[m, WINDOW:] = parts[3][:SHIFT]
        ld[m] = parts[2][SHIFT:]
        rd[m] = parts[3][SHIFT:]

    def mean_rows(v):
        return jnp.sum(v, 0, keepdims=True) * (1.0 / WIDTH)

    def layer_norm(v):
        centred = v - mean_rows(v)
        rstd = lax.rsqrt(mean_rows(centred * centred) + norm_eps)
        return centred * rstd, rstd

    items = [step * step_items + m for m in range(step_items)]
    leads = [lead_ref[i] for i in items]
    raw = per_item(lambda m: gather(x_own, x_right, x_down, x_corner, m))
    mean = jnp.concatenate([affine_ref[0]] * step_items, 1)
    inv_std = jnp.concatenate([affine_ref[1]] * step_items, 1)
    normed = (raw - mean) * inv_std
    n_hi, n_lo = split(normed)

    joined = narrow(qkv_f[...], n_hi, n_lo)
    query = joined[:WIDTH] + spread_cols(0)
    key = joined[WIDTH : 2 * WIDTH]
    value = joined[2 * WIDTH :] + spread_cols(1)

    def unit(v):
        rows, inverses = [], []
        for h in range(HEADS):
            part = v[h * HEAD_DIM : (h + 1) * HEAD_DIM]
            inverse = lax.rsqrt(jnp.sum(part * part, 0, keepdims=True) + unit_eps)
            rows.append(part * inverse)
            inverses.append(inverse)
        return rows, inverses

    q_rows, q_inv = unit(query)
    k_rows, k_inv = unit(key)
    v_rows = [value[h * HEAD_DIM : (h + 1) * HEAD_DIM] for h in range(HEADS)]

    def of_item(v, m):
        return v[:, m * PAIR : (m + 1) * PAIR]

    def three(a_hi, a_lo, b_hi, b_lo):
        left = jnp.concatenate([a_hi, a_lo, a_hi], 0)
        right = jnp.concatenate([b_hi, b_hi, b_lo], 0)
        return halves(dot(left.T, right))

    def side_by_side(v):
        other = pltpu.roll(v, PLACES, 1)
        v_hi, v_lo = split(v)
        o_hi, o_lo = split(other)
        top = jnp.concatenate([jnp.where(first_half, v_hi, o_lo), v_hi], 1)
        low = jnp.concatenate([jnp.where(first_half, o_hi, v_lo), o_hi], 1)
        return jnp.concatenate([top, low], 0)[:, : 3 * PLACES]

    def over_keys(both, e_hi, e_lo):
        return halves(dot(both, jnp.concatenate([e_hi, e_hi, e_lo], 0)))

    def over_queries(v_hi, v_lo, e_hi, e_lo):
        zero = jnp.zeros_like(v_hi)

        def apart(x):
            return jnp.concatenate(
                [jnp.where(first_half, x, zero), jnp.where(first_half, zero, x)], 0
            )

        a_hi, a_lo = apart(v_hi), apart(v_lo)
        left = jnp.concatenate(
            [
                jnp.concatenate([a_hi, a_hi], 1),
                jnp.concatenate([a_lo, jnp.zeros_like(a_lo)], 1),
            ],
            0,
        )
        weights = jnp.concatenate([e_hi, e_lo], 1)
        r = dot_rows(left, jnp.concatenate([weights, weights], 0))
        return halves(r[:PLACES] + r[PLACES:])

    kept = []
    mixed_items = []
    for m in range(step_items):
        mixed_heads = []
        for h in range(HEADS):
            q_hi, q_lo = split(of_item(q_rows[h], m))
            k_hi, k_lo = split(of_item(k_rows[h], m))
            cosine = three(k_hi, k_lo, q_hi, q_lo)
            flag0 = flags_ref[2 * items[m]]
            flag1 = flags_ref[2 * items[m] + 1]
            offset = jnp.where(first_half, bias_ref[flag0, h], bias_ref[flag1, h])
            expo = jnp.exp(cosine * scale_ref[h] + offset)
            inverse = 1.0 / jnp.sum(expo, 0, keepdims=True)
            e_hi, e_lo = split(expo)
            mixed = over_keys(side_by_side(of_item(v_rows[h], m)), e_hi, e_lo) * inverse
            mixed_heads.append(mixed)
            kept.append((q_hi, q_lo, k_hi, k_lo, cosine, expo, e_hi, e_lo, inverse, mixed))
        mixed_items.append(jnp.concatenate(mixed_heads, 0))
    mixed = jnp.concatenate(mixed_items, 1)

    o_hi, o_lo = split(mixed)
    attn_hat, attn_rstd = layer_norm(narrow(out_f[...], o_hi, o_lo) + spread_cols(2))

    def gain(base):
        return per_item(lambda m: 1.0 + col(base) + leads[m] * col(base + 1))

    def shift(base):
        return per_item(lambda m: col(base + 2) + leads[m] * col(base + 3))

    gain0 = gain(4)
    first = normed + attn_hat * gain0 + shift(4)
    f_hi, f_lo = split(first)

    up_bias = jnp.concatenate([up_bias_ref[...]] * step_items, 1)
    u = narrow(up_f[...], f_hi, f_lo) + up_bias
    phi, bell = normal_parts(u)
    hidden = u * phi
    slope = phi + u * bell
    h_hi, h_lo = split(hidden)
    branch = wide(down_f[...], down_f_hi[...], h_hi, h_lo) + spread_cols(3)
    hat, rstd = layer_norm(branch)
    gain1 = gain(8)
    out = first + hat * gain1 + shift(8)
    for m in range(step_items):
        scatter(of_item(out, m), out_lo, out_ld, out_ro, out_rd, m)

    def norm_back(g, hat, rstd, gain, base):
        weighted = g * hat
        for m in range(step_items):
            a, b = of_item(weighted, m), of_item(g, m)
            sums_ref[base] += a
            sums_ref[base + 1] += leads[m] * a
            sums_ref[base + 2] += b
            sums_ref[base + 3] += leads[m] * b
        e = g * gain
        return (e - mean_rows(e) - hat * mean_rows(e * hat)) * rstd

    def add_items(v):
        total = of_item(v, 0)
        for m in range(1, step_items):
            total = total + of_item(v, m)
        return total

    ones_rows = jnp.where(
        lax.broadcasted_iota(jnp.int32, (LANES - WIDTH, step_items * PAIR), 0) == 0, 1.0, 0.0
    ).astype(bf16)
    zero_rows = jnp.zeros((LANES - WIDTH, step_items * PAIR), bf16)

    def outer(a_hi, a_lo, b_hi, b_lo):
        right = jnp.concatenate([b_hi, ones_rows, b_lo, zero_rows], 0)
        r = dot_rows(stack_rows(a_hi, a_lo), right)
        m = a_hi.shape[0]
        return (r[:m, :LANES] + r[m:, :LANES]) + r[:m, LANES:]

    cot = per_item(lambda m: gather(ct_own, ct_right, ct_down, ct_corner, m))
    d_branch = norm_back(cot, hat, rstd, gain1, 4)
    sums_ref[8] += add_items(d_branch)
    z_hi, z_lo = split(d_branch)
    g_down_ref[...] += outer(h_hi, h_lo, z_hi, z_lo)
    d_pre = narrow(down_b[...], z_hi, z_lo) * slope
    p_hi, p_lo = split(d_pre)
    g_up_ref[...] += outer(p_hi, p_lo, f_hi, f_lo)
    d_first = cot + wide(up_b[...], up_b_hi[...], p_hi, p_lo)
    d_attn = norm_back(d_first, attn_hat, attn_rstd, gain0, 0)
    a_hi, a_lo = split(d_attn)
    g_out_ref[...] += outer(a_hi, a_lo, o_hi, o_lo)
    d_mixed = narrow(out_b[...], a_hi, a_lo)

    d_items = []
    for m in range(step_items):
        dq_rows, dk_rows, dv_rows = [], [], []
        for h in range(HEADS):
            q_hi, q_lo, k_hi, k_lo, cosine, expo, e_hi, e_lo, inverse, mixed_h = kept[m * HEADS + h]
            q_dir, k_dir = of_item(q_rows[h], m), of_item(k_rows[h], m)
            v_hi, v_lo = split(of_item(v_rows[h], m))
            d_out = of_item(d_mixed, m)[h * HEAD_DIM : (h + 1) * HEAD_DIM] * inverse
            d_hi, d_lo = split(d_out)
            delta = jnp.sum(d_out * mixed_h, 0, keepdims=True)
            d_scores = expo * (three(v_hi, v_lo, d_hi, d_lo) - delta)
            dpos_ref[h] += d_scores
            folded = d_scores * cosine
            total = folded[0:8]
            for i in range(1, PLACES // 8):
                total = total + folded[8 * i : 8 * i + 8]
            dcos_ref[h] += total
            s_hi, s_lo = split(d_scores)
            dv = over_queries(d_hi, d_lo, e_hi, e_lo)
            dk = over_queries(q_hi, q_lo, s_hi, s_lo) * scale_ref[h]
            dq = over_keys(side_by_side(k_dir), s_hi, s_lo) * scale_ref[h]
            dq = (dq - q_dir * jnp.sum(q_dir * dq, 0, keepdims=True)) * of_item(q_inv[h], m)
            dk = (dk - k_dir * jnp.sum(k_dir * dk, 0, keepdims=True)) * of_item(k_inv[h], m)
            dq_rows.append(dq)
            dk_rows.append(dk)
            dv_rows.append(dv)
        d_items.append(jnp.concatenate(dq_rows + dk_rows + dv_rows, 0))
    d_joined = jnp.concatenate(d_items, 1)
    j_hi, j_lo = split(d_joined)
    g_qkv_ref[...] += outer(j_hi, j_lo, n_hi, n_lo)
    d_normed = d_first + wide(qkv_b[...], qkv_b_hi[...], j_hi, j_lo)
    sums_ref[9] += add_items(d_normed)
    sums_ref[10] += add_items(d_normed * normed)
    for m in range(step_items):
        scatter(of_item(d_normed, m), dn_lo, dn_ld, dn_ro, dn_rd, m)


def run_block(flags, lead, x_parts, ct_parts, affine, weights, cols, up_bias, scale, bias):
    items = x_parts[0].shape[0]
    step_items = 2
    steps = items // step_items
    half = HIDDEN

    def rows(n, width):
        return pl.BlockSpec((step_items, n, width), lambda i: (i, 0, 0))

    def whole(shape):
        return pl.BlockSpec(shape, lambda i: (0,) * len(shape))

    smem = pl.BlockSpec(memory_space=pltpu.SMEM)
    part_specs = [
        rows(16, 2 * half),
        rows(12, half),
        rows(4, half),
        rows(4, half),
    ]
    side_shapes = [(12, half), (4, half), (12, half), (4, half)]
    side_out = [jax.ShapeDtypeStruct((items,) + s, f32) for s in side_shapes]
    side_specs = [rows(*s) for s in side_shapes]
    acc_shapes = [
        (3 * WIDTH, LANES),
        (WIDTH, LANES),
        (HIDDEN, LANES),
        (HIDDEN, LANES),
        (11, WIDTH, LANES),
        (HEADS, PLACES, LANES),
        (HEADS, 8, LANES),
    ]
    w_qkv, w_out, w_up, w_down = weights
    return pl.pallas_call(
        partial(block_kernel, step_items),
        grid=(steps,),
        in_specs=[smem, smem]
        + part_specs
        + part_specs
        + [whole(affine.shape)]
        + [whole(w.shape) for w in weights]
        + [whole(cols.shape), whole(up_bias.shape), smem, whole(bias.shape)],
        out_specs=side_specs + side_specs + [whole(s) for s in acc_shapes],
        out_shape=side_out + side_out + [jax.ShapeDtypeStruct(s, f32) for s in acc_shapes],
        scratch_shapes=[
            pltpu.VMEM((6 * WIDTH, 2 * WIDTH), bf16),
            pltpu.VMEM((2 * WIDTH, 2 * WIDTH), bf16),
            pltpu.VMEM((2 * HIDDEN, 2 * WIDTH), bf16),
            pltpu.VMEM((2 * WIDTH, HIDDEN), bf16),
            pltpu.VMEM((2 * HIDDEN, 2 * WIDTH), bf16),
            pltpu.VMEM((2 * WIDTH, HIDDEN), bf16),
            pltpu.VMEM((2 * WIDTH, 2 * WIDTH), bf16),
            pltpu.VMEM((2 * WIDTH, 3 * WIDTH), bf16),
            pltpu.VMEM((WIDTH, HIDDEN), bf16),
            pltpu.VMEM((WIDTH, HIDDEN), bf16),
            pltpu.VMEM((WIDTH, 3 * WIDTH), bf16),
        ],
        compiler_params=pltpu.CompilerParams(
            dimension_semantics=("arbitrary",), vmem_limit_bytes=56 * 1024 * 1024
        ),
    )(
        flags,
        lead,
        *x_parts,
        *ct_parts,
        affine,
        w_qkv,
        w_out,
        w_up,
        w_down,
        cols,
        up_bias,
        scale,
        bias,
    )


def input_grad_kernel(x_ref, own_ref, right_ref, down_ref, corner_ref, c_ref, out_ref):
    inv_std = c_ref[0:1]
    a = c_ref[1:2]
    b = c_ref[2:3]
    mean = c_ref[3:4]
    half = HIDDEN
    for m in range(x_ref.shape[0]):
        for rows, left, right in (
            (slice(0, SHIFT), corner_ref[m], down_ref[m]),
            (slice(SHIFT, 16), right_ref[m], own_ref[m]),
        ):
            for lanes, d in ((slice(0, half), left), (slice(half, 2 * half), right)):
                x = x_ref[m, rows, lanes]
                out_ref[m, rows, lanes] = (
                    inv_std[:, lanes] * d - a[:, lanes] - (x - mean[:, lanes]) * b[:, lanes]
                )


def input_grad(x, own, right, down, corner, coefficients):
    items, rows, flat = x.shape
    step_items = 8 if items % 8 == 0 else 1
    half = HIDDEN

    def spec(n, width):
        return pl.BlockSpec((step_items, n, width), lambda i: (i, 0, 0))

    return pl.pallas_call(
        input_grad_kernel,
        grid=(items // step_items,),
        in_specs=[
            spec(rows, flat),
            spec(12, half),
            spec(12, half),
            spec(4, half),
            spec(4, half),
            pl.BlockSpec(coefficients.shape, lambda i: (0, 0)),
        ],
        out_specs=spec(rows, flat),
        out_shape=jax.ShapeDtypeStruct(x.shape, f32),
    )(x, own, right, down, corner, coefficients)


def place_coordinates():
    places = jnp.arange(PLACES, dtype=jnp.int32)
    return places % WINDOW, places // WINDOW


def coordinate_table():
    offsets = jnp.arange(SPAN * SPAN, dtype=jnp.int32)
    along_rows = (offsets // SPAN - (WINDOW - 1)).astype(f32)
    along_cols = (offsets % SPAN - (WINDOW - 1)).astype(f32)
    stacked = jnp.stack([along_rows, along_cols], -1) * (8.0 / (WINDOW - 1))
    return jnp.sign(stacked) * jnp.log2(jnp.abs(stacked) + 1.0) / 3.0


def position_bias(weight1, bias1, weight2):
    precise = lax.Precision.HIGHEST
    hidden_units = jax.nn.gelu(
        jnp.dot(coordinate_table(), weight1, precision=precise) + bias1, approximate=False
    )
    table = 16.0 * jax.nn.sigmoid(jnp.dot(hidden_units, weight2, precision=precise))
    row, col = place_coordinates()
    index = (row[None, :] - row[:, None] + WINDOW - 1) * SPAN + (
        col[None, :] - col[:, None] + WINDOW - 1
    )
    offset_ids = jnp.arange(SPAN * SPAN, dtype=jnp.int32)
    one_hot = (index.reshape(-1)[:, None] == offset_ids[None, :]).astype(f32)
    spread_out = lax.dot_general(
        table, one_hot, (((0,), (1,)), ((), ())), precision=precise
    )
    return spread_out.reshape(HEADS, PLACES, PLACES)


def mask_tables():
    row, col = place_coordinates()
    apart_r = (row[None, :] < SHIFT) != (row[:, None] < SHIFT)
    apart_c = (col[None, :] < SHIFT) != (col[:, None] < SHIFT)
    none = jnp.zeros_like(apart_r)
    return jnp.stack([none, apart_c, apart_r, apart_r | apart_c])


def take_from(block, dy, dx):
    rows, cols = lax.axis_size("ty"), lax.axis_size("tx")
    route = []
    for i in range(rows * cols):
        y, x = divmod(i, cols)
        route.append((((y + dy) % rows) * cols + (x + dx) % cols, i))
    return lax.ppermute(block, ("ty", "tx"), route)


def reduce_all(v):
    n = lax.axis_size(axes_all)
    step = 1
    while step < n:
        v = v + lax.ppermute(v, axes_all, [(i, i ^ step) for i in range(n)])
        step *= 2
    return v


def shards(
    inputs,
    regions,
    lead_step_index,
    running_channel_mean,
    running_channel_variance,
    query_key_value_weight,
    query_value_bias,
    log_cosine_scale,
    bias_net_weight1,
    bias_net_bias1,
    bias_net_weight2,
    output_weight,
    projection_bias,
    up_weight,
    up_bias,
    down_weight,
    down_bias,
    conditioned_norm_values,
    cotangent,
):
    items, tile_rows, flat = inputs.shape
    tile_cols = flat // WIDTH
    half = flat // 2
    devices = lax.axis_size(axes_all)
    local_count = items * tile_rows * tile_cols
    token_count = local_count * devices

    def halo(field):
        return (
            field,
            take_from(field[:, SHIFT:, :half], 0, 1),
            take_from(field[:, :SHIFT, half:], 1, 0),
            take_from(field[:, :SHIFT, :half], 1, 1),
        )

    stats = local_stats(inputs)
    x_parts = halo(inputs)
    ct_parts = halo(cotangent)
    mine = jnp.broadcast_to(stats[None, :2], (devices, 2, WIDTH))
    every = lax.all_to_all(mine, axes_all, 0, 0, tiled=True)
    chan_mean = jnp.mean(every[:, 0], 0)
    apart = every[:, 0] - chan_mean
    chan_var = (
        jnp.sum(every[:, 1], 0) + local_count * jnp.sum(apart * apart, 0)
    ) / token_count
    inv_std = lax.rsqrt(chan_var + norm_eps)

    row_cut = regions[:, ::WINDOW, 0] != regions[:, WINDOW - 1 :: WINDOW, 0]
    col_cut = regions[:, ::WINDOW, 0] != regions[:, ::WINDOW, WINDOW - 1]
    flags = (2 * row_cut.astype(jnp.int32) + col_cut.astype(jnp.int32)).reshape(-1)
    lead = (lead_step_index + 1).astype(f32) / LEAD_STEPS

    scale = jnp.exp(log_cosine_scale)
    pos_bias, bias_pull = jax.vjp(
        position_bias, bias_net_weight1, bias_net_bias1, bias_net_weight2
    )
    ceiling = (scale + 16.0)[:, None, None]
    tables = jnp.where(mask_tables()[:, None], masked_score, pos_bias[None] - ceiling[None])
    tables = jnp.concatenate([tables, tables], -1)

    def spread(rows):
        return jnp.broadcast_to(rows[..., None], rows.shape + (LANES,))

    cols = spread(
        jnp.concatenate(
            [
                query_value_bias,
                projection_bias[None],
                down_bias[None],
                conditioned_norm_values.reshape(8, WIDTH),
            ],
            0,
        )
    )
    affine = spread(jnp.stack([chan_mean, inv_std]))
    results = run_block(
        flags,
        lead,
        x_parts,
        ct_parts,
        affine,
        (query_key_value_weight, output_weight, up_weight, down_weight),
        cols,
        spread(up_bias),
        scale,
        tables,
    )
    out_parts, dn_parts = results[:4], results[4:8]
    g_qkv, g_out, g_up, g_down, sums, d_pos, d_cos = results[8:]

    def home(parts):
        own, down, right, corner = parts
        return (own, take_from(right, 0, -1), take_from(down, -1, 0), take_from(corner, -1, -1))

    dn_own, dn_right, dn_down, dn_corner = home(dn_parts)
    out_own, out_right, out_down, out_corner = home(out_parts)
    outputs = jnp.concatenate(
        [
            jnp.concatenate([out_corner, out_down], 2),
            jnp.concatenate([out_right, out_own], 2),
        ],
        1,
    )

    d_pos = d_pos[:, :, :PLACES] + d_pos[:, :, PLACES:]
    g_w1, g_b1, g_w2 = bias_pull(d_pos)
    sums = jnp.sum(sums, -1)
    pieces = [
        g_qkv,
        g_out,
        g_up,
        g_down,
        sums,
        jnp.sum(d_cos, (1, 2)) * scale,
        g_w1,
        g_b1,
        g_w2,
    ]
    sizes = [p.size for p in pieces]
    total = sum(sizes)
    padded = -(-total // 1024) * 1024
    flat_sum = jnp.concatenate([p.reshape(-1) for p in pieces] + [jnp.zeros(padded - total, f32)])
    flat_sum = reduce_all(flat_sum.reshape(-1, LANES)).reshape(-1)
    back, at = [], 0
    for p in pieces:
        back.append(flat_sum[at : at + p.size].reshape(p.shape))
        at += p.size
    g_qkv, g_out, g_up, g_down, sums, g_scale, g_w1, g_b1, g_w2 = back

    sum_grad = sums[9] / token_count
    sum_cross = sums[10] / token_count
    coefficients = jnp.stack(
        [inv_std, inv_std * sum_grad, inv_std * inv_std * sum_cross, chan_mean]
    )
    coefficients = jnp.tile(coefficients, (1, tile_cols))
    grad_inputs = input_grad(inputs, dn_own, dn_right, dn_down, dn_corner, coefficients)
    new_mean = (1.0 - momentum) * running_channel_mean + momentum * chan_mean
    new_var = (1.0 - momentum) * running_channel_variance + momentum * chan_var * (
        token_count / (token_count - 1.0)
    )
    return (
        outputs,
        grad_inputs,
        g_qkv[:, :WIDTH].T,
        jnp.stack([g_qkv[:WIDTH, WIDTH], g_qkv[2 * WIDTH :, WIDTH]]),
        g_scale,
        g_w1,
        g_b1,
        g_w2,
        g_out[:, :WIDTH].T,
        g_out[:, WIDTH],
        g_up[:, :WIDTH].T,
        g_up[:, WIDTH],
        g_down[:, :WIDTH].T,
        sums[8],
        sums[:8].reshape(2, 4, WIDTH),
        new_mean,
        new_var,
    )


def solution(mesh):
    tiled = P("items", "ty", "tx")
    placed = (tiled, tiled, P("items")) + (P(),) * 15 + (tiled,)
    return jax.shard_map(
        shards,
        mesh=mesh,
        in_specs=placed,
        out_specs=(tiled, tiled) + (P(),) * 15,
        check_vma=False,
    )
```

time: 597 us -> 241 us (0.40)
  matrix products: 165 us -> 7.77 us
  blocking collectives: 122 us -> 0 us
  Pallas kernels: 0 us -> 91.7 us
  other arithmetic: 84 us -> 8.61 us
  local copies, waits for them, and re-layouts: 87.2 us -> 25.6 us
  waiting for transfers between devices: 108 us -> 82.9 us
  between operations: 15.7 us -> 1.22 us
  starting transfers between devices: 8.33 us -> 22.5 us
    dot_general x25 -> x7, matrix products: 165 us -> 7.77 us  [the longest x2 3.61 us: position_bias(): lax.dot_general(table, one_hot, (((0,), (1,)), ((), ())), precision=precise)]
    psum x3 -> x0, blocking collectives: 122 us -> none  [the longest x1 42 us: shards(): chan_total = lax.psum(jnp.sum(inputs, (0, 1, 2)), ('ty', 'tx', 'items'))]
    pallas_call x0 -> x3, Pallas kernels: none -> 91.7 us  [the longest x1 86.8 us: run_block(): pl.pallas_call(partial(block_kernel, step_items), grid=(steps,), in_specs...]
    psum x1 -> x0, waiting for transfers between devices: 63.3 us -> none  [shards(): lax.psum((g_w_out, g_b_out, g_w_up, g_b_up, g_w_down, g_b_down, g_norm, g...]
    reduce_sum x22 -> x5, other arithmetic: 45.5 us -> 0.45 us  [the longest x1 0.27 us: shards(): sums = jnp.sum(sums, -1)]
    ppermute x8 -> x17, waiting for transfers between devices: 45 us -> 82.9 us  [the longest x5 58.4 us: reduce_all(): v = v + lax.ppermute(v, axes_all, [(i, i ^ step) for i in range(n)])]
    another operation x3, local copies, waits for them, and re-layouts: 21.8 us -> 0.69 us  [the longest x2 0.68 us: shards(): coefficients = jnp.tile(coefficients, (1, tile_cols))]
    mul x6 -> x2, other arithmetic: 19.9 us -> 0.52 us  [the longest x1 0.52 us: shards(): inv_std * sum_grad]
  transfers between devices with their start and end apart: 9 -> 18, of which waited for: 7 -> 9; matrix products, arithmetic and copies ran while one was open for 12% -> 12% of each run, Pallas kernels for 0% -> 0%
where the time goes in v1:
time: 241 us; the launch traced here: 240 us
  Pallas kernels  91.7 us (38%)
  waiting for transfers between devices  82.9 us (34%)
  local copies, waits for them, and re-layouts  25.6 us (11%)
  starting transfers between devices  22.5 us (9%)
  other arithmetic  8.61 us (4%)
  matrix products  7.77 us (3%)
    pallas_call x1, Pallas kernels, run_block(): pl.pallas_call(partial(block_kernel, step_items), grid=(steps,), in_specs...  86.8 us
    ppermute x5, waiting for transfers between devices, reduce_all(): v = v + lax.ppermute(v, axes_all, [(i, i ^ step) for i in range(n)])  58.4 us
    ppermute x12, waiting for transfers between devices, take_from(): return lax.ppermute(block, ('ty', 'tx'), route)  24.5 us
    ppermute x12, starting transfers between devices, take_from(): return lax.ppermute(block, ('ty', 'tx'), route)  9.53 us
    all_to_all x1, starting transfers between devices, shards(): every = lax.all_to_all(mine, axes_all, 0, 0, tiled=True)  7.43 us
    unnamed x74, local copies, waits for them, and re-layouts  7.29 us
    ppermute x5, starting transfers between devices, reduce_all(): v = v + lax.ppermute(v, axes_all, [(i, i ^ step) for i in range(n)])  5.58 us
  transfers between devices with their start and end apart: 18, of which 9 were waited for; matrix products, arithmetic and copies ran while one was open for 12% of the time, Pallas kernels for 0%

profile of v1, /device:TPU:0, one launch (start us, length us, event | category | flops | bytes accessed | tf_op | source)
XLA Modules:
  0.0 240.3 jit_solution(10117314849127397898)
XLA Ops:
  0.7 1.4 copy-done.1
  3.4 7.4 %all-to-all-start = ((f32[32,2,96]{2,1,0:T(2,128)}), f32[32,2,96]{2,1,0:T(2,128)}, u32[]{:S(2)}, u32[]{:S(2)}) async-start(f32[32,2,96]{2,1,0:T(2,128)} %broadcast_in_dim.34), calls=%async_computation | async-start | bytes 65536 | tf_op jit(solution)/shard_map/all_to_all | solution.py:656
  10.9 1.8 collective-permute-start.1
  13.6 1.9 fusion.32
  15.5 1.5 collective-permute-start.4
  19.2 1.6 fusion.9
  21.4 2.2 fusion.1
  31.5 4.3 %collective-permute-done.3 = f32[32,12,384]{2,0,1:T(8,128)S(1)} collective-permute-done((f32[32,12,384]{2,0,1:T(8,128)S(1)}, f32[32,12,384]{2,0,1:T(8,128)S(1)}, u32[]{:S(2)}, u32[]{:S(2)}) %collective-permute-start.3) | collective-permute-done | bytes 589856 | tf_op jit(solution)/shard_map/ppermute | solution.py:604
  39.6 86.8 %shard_map.315 = (f32[32,12,384]{2,1,0:T(8,128)}, f32[32,4,384]{2,1,0:T(4,128)}, f32[32,12,384]{2,1,0:T(8,128)}, f32[32,4,384]{2,1,0:T(4,128)}, f32[32,12,384]{2...) custom-call(s32[64]{0:T(128)} %add.203.flags_ref, ...), custom_call_target="tpu_custom_call" | custom-call | tf_op jit(solution)/shard_map/pallas_call | solution.py:473
  127.6 1.4 fusion.5
  132.0 1.4 concatenate.23
  133.3 1.5 collective-permute-start.12
  134.9 15.0 %collective-permute-done.12 = f32[1192,128]{1,0:T(8,128)S(1)} collective-permute-done((f32[1192,128]{1,0:T(8,128)S(1)}, f32[1192,128]{1,0:T(8,128)S(1)}, u32[]{:S(2)}, u32[]{:S(2)}) %collective-permute-start.12) | collective-permute-done | bytes 610336 | tf_op jit(solution)/shard_map/ppermute | solution.py:611
  149.9 2.3 collective-permute-start.13
  152.2 27.4 %collective-permute-done.13 = f32[1192,128]{1,0:T(8,128)S(1)} collective-permute-done((f32[1192,128]{1,0:T(8,128)S(1)}, f32[1192,128]{1,0:T(8,128)S(1)}, u32[]{:S(2)}, u32[]{:S(2)}) %collective-permute-start.13) | collective-permute-done | bytes 610336 | tf_op jit(solution)/shard_map/ppermute | solution.py:611
  179.8 2.0 collective-permute-done.14
  182.9 1.8 collective-permute-start.8
  184.7 13.9 %collective-permute-done.15 = f32[1192,128]{1,0:T(8,128)S(1)} collective-permute-done((f32[1192,128]{1,0:T(8,128)S(1)}, f32[1192,128]{1,0:T(8,128)S(1)}, u32[]{:S(2)}, u32[]{:S(2)}) %collective-permute-start.15) | collective-permute-done | bytes 610336 | tf_op jit(solution)/shard_map/ppermute | solution.py:611
  200.9 3.3 %collective-permute-done.9 = f32[32,12,384]{2,0,1:T(8,128)S(1)} collective-permute-done((f32[32,12,384]{2,0,1:T(8,128)S(1)}, f32[32,12,384]{2,0,1:T(8,128)S(1)}, u32[]{:S(2)}, u32[]{:S(2)}) %collective-permute-start.9) | collective-permute-done | bytes 589856 | tf_op jit(solution)/shard_map/ppermute | solution.py:604
  206.6 4.1 %collective-permute-done.8 = f32[32,12,384]{2,0,1:T(8,128)S(1)} collective-permute-done((f32[32,12,384]{2,0,1:T(8,128)S(1)}, f32[32,12,384]{2,0,1:T(8,128)S(1)}, u32[]{:S(2)}, u32[]{:S(2)}) %collective-permute-start.8) | collective-permute-done | bytes 589856 | tf_op jit(solution)/shard_map/ppermute | solution.py:604
  211.0 7.4 %collective-permute-done.6 = f32[32,4,384]{2,1,0:T(4,128)S(1)} collective-permute-done((f32[32,4,384]{2,1,0:T(4,128)S(1)}, f32[32,4,384]{2,1,0:T(4,128)S(1)}, u32[]{:S(2)}, u32[]{:S(2)}) %collective-permute-start.6) | collective-permute-done | bytes 196640 | tf_op jit(solution)/shard_map/ppermute | solution.py:604
  218.4 5.5 %collective-permute-done.7 = f32[32,4,384]{2,1,0:T(4,128)S(1)} collective-permute-done((f32[32,4,384]{2,1,0:T(4,128)S(1)}, f32[32,4,384]{2,1,0:T(4,128)S(1)}, u32[]{:S(2)}, u32[]{:S(2)}) %collective-permute-start.7) | collective-permute-done | bytes 196640 | tf_op jit(solution)/shard_map/ppermute | solution.py:604
  223.9 1.4 maximum_maximum_fusion
  236.1 4.2 %shard_map.316 = f32[32,16,768]{2,1,0:T(8,128)} custom-call(f32[32,16,768]{2,1,0:T(8,128)} %x_ref.3, f32[32,12,384]{2,1,0:T(8,128)} %get-tuple-element.36.own_ref, f32[32,12,384]{2,1,0:T(8,128)} %copy.93.right_ref, f32[32,4,384]{2,1,0:T(4,128)} %copy-done.8, f32[32,4,384]{2,1,0:T(4,128)} %copy-done.9, f32[4,768]{1,0:T(4,128)} %tile.10.c_ref), custom_call_target="tpu_custom_call" | custom-call | tf_op jit(solution)/shard_map/pallas_call | solution.py:543
  (169 shorter events, 37.8 us)
Async XLA Ops:
  0.7 20.2 %copy-start = (f32[512,3]{0,1:T(4,128)S(1)}, f32[512,3]{0,1:T(4,128)}, u32[]{:S(2)}) copy-start(f32[512,3]{0,1:T(4,128)} %param.29) | copy-start | bytes 18436
  3.4 24.2 %all-to-all-start = ((f32[32,2,96]{2,1,0:T(2,128)}), f32[32,2,96]{2,1,0:T(2,128)}, u32[]{:S(2)}, u32[]{:S(2)}) async-start(f32[32,2,96]{2,1,0:T(2,128)} %broadcast_in_dim.34), calls=%async_computation | async-start | bytes 65536 | tf_op jit(solution)/shard_map/all_to_all | solution.py:656
  10.9 26.1 %collective-permute-start.1 = (f32[32,4,384]{2,1,0:T(4,128)S(1)}, f32[32,4,384]{2,1,0:T(4,128)}, u32[]{:S(2)}, u32[]{:S(2)}) collective-permute-start(f32[32,4,384]{2,1,0:T(4,128)S(1)} %get-tuple-element.138), channel_id=1, source_target_pairs={{16,0},{20,4},{24,8},{28,12},{0,16},{4,20},{8,24},{12,28},{17,1},{... | collective-permute-start | bytes 589832 | tf_op jit(solution)/shard_map/ppermute | solution.py:604
  12.7 24.4 %collective-permute-start.2 = (f32[32,4,384]{2,1,0:T(4,128)S(1)}, f32[32,4,384]{2,1,0:T(4,128)}, u32[]{:S(2)}, u32[]{:S(2)}) collective-permute-start(f32[32,4,384]{2,1,0:T(4,128)S(1)} %get-tuple-element.137), channel_id=1, source_target_pairs={{20,0},{24,4},{28,8},{16,12},{4,16},{8,20},{12,24},{0,28},{21,1},{... | collective-permute-start | bytes 589832 | tf_op jit(solution)/shard_map/ppermute | solution.py:604
  15.5 21.5 %collective-permute-start.4 = (f32[32,4,384]{2,1,0:T(4,128)}, f32[32,4,384]{2,1,0:T(4,128)}, u32[]{:S(2)}, u32[]{:S(2)}) collective-permute-start(f32[32,4,384]{2,1,0:T(4,128)} %get-tuple-element.136), channel_id=1, source_target_pairs={{16,0},{20,4},{24,8},{28,12},{0,16},{4,20},{8,24},{12,28},{17,1},{... | collective-permute-start | bytes 589832 | tf_op jit(solution)/shard_map/ppermute | solution.py:604
  18.0 11.0 %collective-permute-start = (f32[32,12,384]{2,0,1:T(8,128)}, f32[32,12,384]{2,0,1:T(8,128)S(1)}, u32[]{:S(2)}, u32[]{:S(2)}) collective-permute-start(f32[32,12,384]{2,0,1:T(8,128)} %copy.100), channel_id=1, source_target_pairs={{4,0},{8,4},{12,8},{0,12},{20,16},{24,20},{28,24},{16,28},{5,1},{9... | collective-permute-start | bytes 1769480 | tf_op jit(solution)/shard_map/ppermute | solution.py:604
  18.8 17.0 %collective-permute-start.3 = (f32[32,12,384]{2,0,1:T(8,128)S(1)}, f32[32,12,384]{2,0,1:T(8,128)S(1)}, u32[]{:S(2)}, u32[]{:S(2)}) collective-permute-start(f32[32,12,384]{2,0,1:T(8,128)S(1)} %copy.101), channel_id=1, source_target_pairs={{4,0},{8,4},{12,8},{0,12},{20,16},{24,20},{28,24},{16,28},{5,1},{9... | collective-permute-start | bytes 1769480 | tf_op jit(solution)/shard_map/ppermute | solution.py:604
  29.0 8.0 %collective-permute-start.5 = (f32[32,4,384]{2,1,0:T(4,128)S(1)}, f32[32,4,384]{2,1,0:T(4,128)S(1)}, u32[]{:S(2)}, u32[]{:S(2)}) collective-permute-start(f32[32,4,384]{2,1,0:T(4,128)S(1)} %copy-done.10), channel_id=1, source_target_pairs={{20,0},{24,4},{28,8},{16,12},{4,16},{8,20},{12,24},{0,28},{21,1},{... | collective-permute-start | bytes 589832 | tf_op jit(solution)/shard_map/ppermute | solution.py:604
  133.3 16.5 %collective-permute-start.12 = (f32[1192,128]{1,0:T(8,128)S(1)}, f32[1192,128]{1,0:T(8,128)S(1)}, u32[]{:S(2)}, u32[]{:S(2)}) collective-permute-start(f32[1192,128]{1,0:T(8,128)S(1)} %bitcast.45), channel_id=1, source_target_pairs={{0,1},{1,0},{2,3},{3,2},{4,5},{5,4},{6,7},{7,6},{8,9},{9,8},{10,11... | collective-permute-start | bytes 1830920 | tf_op jit(solution)/shard_map/ppermute | solution.py:611
  149.9 32.5 %copy-start.6 = (f32[32,12,384]{2,1,0:T(8,128)S(1)}, f32[32,12,384]{2,1,0:T(8,128)}, u32[]{:S(2)}) copy-start(f32[32,12,384]{2,1,0:T(8,128)} %get-tuple-element.37) | copy-start | bytes 1769476
  149.9 29.7 %collective-permute-start.13 = (f32[1192,128]{1,0:T(8,128)S(1)}, f32[1192,128]{1,0:T(8,128)S(1)}, u32[]{:S(2)}, u32[]{:S(2)}) collective-permute-start(f32[1192,128]{1,0:T(8,128)S(1)} %bitcast_add_fusion), channel_id=1, source_target_pairs={{0,2},{1,3},{2,0},{3,1},{4,6},{5,7},{6,4},{7,5},{8,10},{9,11},{10,... | collective-permute-start | bytes 1830920 | tf_op jit(solution)/shard_map/ppermute | solution.py:611
  179.8 2.1 collective-permute-start.14
  181.9 16.7 %collective-permute-start.15 = (f32[1192,128]{1,0:T(8,128)S(1)}, f32[1192,128]{1,0:T(8,128)S(1)}, u32[]{:S(2)}, u32[]{:S(2)}) collective-permute-start(f32[1192,128]{1,0:T(8,128)S(1)} %add.223), channel_id=1, source_target_pairs={{0,8},{1,9},{2,10},{3,11},{4,12},{5,13},{6,14},{7,15},{8,0},{9,1},... | collective-permute-start | bytes 1830920 | tf_op jit(solution)/shard_map/ppermute | solution.py:611
  182.6 21.5 %collective-permute-start.9 = (f32[32,12,384]{2,0,1:T(8,128)S(1)}, f32[32,12,384]{2,0,1:T(8,128)S(1)}, u32[]{:S(2)}, u32[]{:S(2)}) collective-permute-start(f32[32,12,384]{2,0,1:T(8,128)S(1)} %copy.91), channel_id=1, source_target_pairs={{12,0},{0,4},{4,8},{8,12},{28,16},{16,20},{20,24},{24,28},{13,1},{... | collective-permute-start | bytes 1769480 | tf_op jit(solution)/shard_map/ppermute | solution.py:604
  182.7 17.3 %copy-start.27 = (f32[32,4,384]{2,1,0:T(4,128)S(1)}, f32[32,4,384]{2,1,0:T(4,128)}, u32[]{:S(2)}) copy-start(f32[32,4,384]{2,1,0:T(4,128)} %get-tuple-element.32) | copy-start | bytes 589828
  182.7 21.5 %copy-start.25 = (f32[32,4,384]{2,1,0:T(4,128)S(1)}, f32[32,4,384]{2,1,0:T(4,128)}, u32[]{:S(2)}) copy-start(f32[32,4,384]{2,1,0:T(4,128)} %get-tuple-element.38) | copy-start | bytes 589828
  182.9 27.8 %copy-start.24 = (f32[32,4,384]{2,1,0:T(4,128)S(1)}, f32[32,4,384]{2,1,0:T(4,128)}, u32[]{:S(2)}) copy-start(f32[32,4,384]{2,1,0:T(4,128)} %get-tuple-element.39) | copy-start | bytes 589828
  182.9 27.7 %collective-permute-start.8 = (f32[32,12,384]{2,0,1:T(8,128)S(1)}, f32[32,12,384]{2,0,1:T(8,128)S(1)}, u32[]{:S(2)}, u32[]{:S(2)}) collective-permute-start(f32[32,12,384]{2,0,1:T(8,128)S(1)} %copy.89), channel_id=1, source_target_pairs={{12,0},{0,4},{4,8},{8,12},{28,16},{16,20},{20,24},{24,28},{13,1},{... | collective-permute-start | bytes 1769480 | tf_op jit(solution)/shard_map/ppermute | solution.py:604
  198.7 25.2 %copy-start.4 = (f32[32,12,384]{2,1,0:T(8,128)S(1)}, f32[32,12,384]{2,1,0:T(8,128)}, u32[]{:S(2)}) copy-start(f32[32,12,384]{2,1,0:T(8,128)} %get-tuple-element.35) | copy-start | bytes 1769476
  198.7 26.6 %collective-permute-start.16 = (f32[1192,128]{1,0:T(8,128)S(1)}, f32[1192,128]{1,0:T(8,128)S(1)}, u32[]{:S(2)}, u32[]{:S(2)}) collective-permute-start(f32[1192,128]{1,0:T(8,128)S(1)} %add.224), channel_id=1, source_target_pairs={{0,16},{1,17},{2,18},{3,19},{4,20},{5,21},{6,22},{7,23},{8,24},{9,... | collective-permute-start | bytes 1830920 | tf_op jit(solution)/shard_map/ppermute | solution.py:611
  200.0 18.4 %collective-permute-start.6 = (f32[32,4,384]{2,1,0:T(4,128)S(1)}, f32[32,4,384]{2,1,0:T(4,128)S(1)}, u32[]{:S(2)}, u32[]{:S(2)}) collective-permute-start(f32[32,4,384]{2,1,0:T(4,128)S(1)} %copy-done.27), channel_id=1, source_target_pairs={{28,0},{16,4},{20,8},{24,12},{12,16},{0,20},{4,24},{8,28},{29,1},{... | collective-permute-start | bytes 589832 | tf_op jit(solution)/shard_map/ppermute | solution.py:604
  200.0 23.9 %collective-permute-start.7 = (f32[32,4,384]{2,1,0:T(4,128)S(1)}, f32[32,4,384]{2,1,0:T(4,128)S(1)}, u32[]{:S(2)}, u32[]{:S(2)}) collective-permute-start(f32[32,4,384]{2,1,0:T(4,128)S(1)} %copy-done.26), channel_id=1, source_target_pairs={{16,0},{20,4},{24,8},{28,12},{0,16},{4,20},{8,24},{12,28},{17,1},{... | collective-permute-start | bytes 589832 | tf_op jit(solution)/shard_map/ppermute | solution.py:604
  204.1 31.2 %collective-permute-start.10 = (f32[32,4,384]{2,1,0:T(4,128)S(1)}, f32[32,4,384]{2,1,0:T(4,128)S(1)}, u32[]{:S(2)}, u32[]{:S(2)}) collective-permute-start(f32[32,4,384]{2,1,0:T(4,128)S(1)} %copy-done.25), channel_id=1, source_target_pairs={{16,0},{20,4},{24,8},{28,12},{0,16},{4,20},{8,24},{12,28},{17,1},{... | collective-permute-start | bytes 589832 | tf_op jit(solution)/shard_map/ppermute | solution.py:604
  210.6 24.7 %collective-permute-start.11 = (f32[32,4,384]{2,1,0:T(4,128)S(1)}, f32[32,4,384]{2,1,0:T(4,128)S(1)}, u32[]{:S(2)}, u32[]{:S(2)}) collective-permute-start(f32[32,4,384]{2,1,0:T(4,128)S(1)} %copy-done.24), channel_id=1, source_target_pairs={{28,0},{16,4},{20,8},{24,12},{12,16},{0,20},{4,24},{8,28},{29,1},{... | collective-permute-start | bytes 589832 | tf_op jit(solution)/shard_map/ppermute | solution.py:604
  (27 other events, 116.2 us)

commit v2 on v1

v2 whole, which is shorter than its diff:
```python
from functools import partial

import jax
import jax.numpy as jnp
import numpy as np
from jax import lax
from jax.experimental import pallas as pl
from jax.experimental.pallas import tpu as pltpu
from jax.sharding import PartitionSpec as P

HEADS = 3
HEAD_DIM = 32
WIDTH = 96
HIDDEN = 384
WINDOW = 8
SHIFT = 4
LEAD_STEPS = 14
PLACES = WINDOW * WINDOW
SPAN = 2 * WINDOW - 1
PAIR = 2 * PLACES
LANES = 128
OFFSETS = 256
PAYLOAD = 903

masked_score = -1000000000.0
norm_eps = 1e-05
unit_eps = 1e-06
momentum = 0.1
axes_all = ("ty", "tx", "items")

f32 = jnp.float32
bf16 = jnp.bfloat16

in_order = pltpu.CompilerParams(
    dimension_semantics=("arbitrary",), vmem_limit_bytes=60 * 1024 * 1024
)


def block_of(items):
    return next(n for n in (8, 4, 2, 1) if items % n == 0)


def whole(a):
    return pl.BlockSpec(a.shape, lambda i: (0,) * len(a.shape))


normal_slope = 0.28
normal_poly = (
    0.11652074430372011,
    0.06749697235753221,
    0.26890961436457633,
    -0.23699279280357777,
    0.389873590681989,
    -0.10580813816203069,
)


def dot(a, b):
    return lax.dot_general(a, b, (((1,), (0,)), ((), ())), preferred_element_type=f32)


def dot_rows(a, b):
    return lax.dot_general(a, b, (((1,), (1,)), ((), ())), preferred_element_type=f32)


def split(x):
    hi = x.astype(bf16)
    return hi, (x - hi.astype(f32)).astype(bf16)


def normal_parts(u):
    a = jnp.abs(u)
    t = 1.0 / (1.0 + normal_slope * a)
    bell = jnp.exp(-0.5 * u * u)
    poly = normal_poly[-1] * t + normal_poly[-2]
    for c in normal_poly[-3::-1]:
        poly = poly * t + c
    tail = poly * t * bell
    return jnp.where(u < 0, tail, 1.0 - tail), bell * 0.3989422804014327


def pack_kernel(items, x_ref, ct_ref, stats_ref, right_ref, down_ref, corner_ref, sums_ref):
    step = pl.program_id(0)
    step_items, rows, flat = x_ref.shape
    cols = flat // WIDTH
    half = flat // 2

    for part, ref in enumerate((x_ref, ct_ref)):
        right_ref[:, 12 * part : 12 * part + 12, :] = ref[:, SHIFT:, :half]
        down_ref[:, 4 * part : 4 * part + 4, :] = ref[:, :SHIFT, half:]
        corner_ref[:, 4 * part : 4 * part + 4, :] = ref[:, :SHIFT, :half]

    def fold(v):
        total = v[:, :WIDTH]
        for j in range(1, cols):
            total = total + v[:, j * WIDTH : (j + 1) * WIDTH]
        return jnp.sum(total, 0, keepdims=True)

    def total(fn):
        acc = jnp.zeros((8, flat), f32)
        for i in range(step_items):
            acc = acc + fn(x_ref[i, 0:8, :]) + fn(x_ref[i, 8:16, :])
        return acc

    @pl.when(step == 0)
    def _():
        pivot = fold(total(lambda v: v)) * (1.0 / (step_items * rows * cols))
        sums_ref[0] = jnp.broadcast_to(jnp.concatenate([pivot] * cols, 1), (8, flat))
        sums_ref[1] = jnp.zeros((8, flat), f32)
        sums_ref[2] = jnp.zeros((8, flat), f32)

    pivot = sums_ref[0]
    sums_ref[1] += total(lambda v: v - pivot)
    sums_ref[2] += total(lambda v: (v - pivot) * (v - pivot))

    @pl.when(step == pl.num_programs(0) - 1)
    def _():
        count = items * rows * cols
        offset = fold(sums_ref[1]) * (1.0 / count)
        square = fold(sums_ref[2]) - count * offset * offset
        pad = jnp.zeros((1, LANES - WIDTH), f32)
        row = jnp.concatenate([sums_ref[0, 0:1, :WIDTH] + offset, pad, square, pad], 1)
        stats_ref[...] = jnp.broadcast_to(row[None], stats_ref.shape)


def pack(x, ct, devices):
    items, rows, flat = x.shape
    half = flat // 2
    step_items = block_of(items)

    def spec(n, width):
        return pl.BlockSpec((step_items, n, width), lambda i: (i, 0, 0))

    return pl.pallas_call(
        partial(pack_kernel, items),
        grid=(items // step_items,),
        in_specs=[spec(rows, flat)] * 2,
        out_specs=[
            pl.BlockSpec((devices, 1, 2 * LANES), lambda i: (0, 0, 0)),
            spec(24, half),
            spec(8, half),
            spec(8, half),
        ],
        out_shape=[
            jax.ShapeDtypeStruct((devices, 1, 2 * LANES), f32),
            jax.ShapeDtypeStruct((items, 24, half), f32),
            jax.ShapeDtypeStruct((items, 8, half), f32),
            jax.ShapeDtypeStruct((items, 8, half), f32),
        ],
        scratch_shapes=[pltpu.VMEM((3, 8, flat), f32)],
        compiler_params=in_order,
    )(x, ct)


def offset_constants():
    coords = np.zeros((8, OFFSETS), np.float32)
    o = np.arange(SPAN * SPAN)
    for k, along in enumerate((o // SPAN - (WINDOW - 1), o % SPAN - (WINDOW - 1))):
        u = along.astype(np.float32) * np.float32(8.0 / (WINDOW - 1))
        coords[k, : SPAN * SPAN] = np.sign(u) * np.log2(np.abs(u) + np.float32(1.0)) / np.float32(3.0)
    coords[2, : SPAN * SPAN] = 1.0
    key_row, lane = np.divmod(np.arange(WINDOW * LANES), LANES)
    across, row = np.divmod(lane, WINDOW)
    target = (row - key_row + WINDOW - 1) * SPAN + across
    target = np.where(across < SPAN, target, -1).astype(np.int32)
    return jnp.asarray(coords), jnp.asarray(np.broadcast_to(target, (8, target.size)).copy())


def exact(a, b, dims):
    return lax.dot_general(
        a, b, (dims, ((), ())), preferred_element_type=f32, precision=lax.Precision.HIGHEST
    )


def bias_net(net, coords):
    units = net.shape[1]
    columns = jnp.concatenate([net, jnp.zeros((LANES - 8, units), f32)], 0).T

    def column(i):
        return jnp.broadcast_to(columns[:, i : i + 1], (units, OFFSETS))

    u = column(0) * coords[0:1] + column(1) * coords[1:2] + column(2)
    phi, bell = normal_parts(u)
    return column, u * phi, phi + u * bell


def head_rows(net):
    return jnp.concatenate([net[3:6], jnp.zeros((5, net.shape[1]), f32)], 0)


def one_hot(target):
    rows = lax.broadcasted_iota(jnp.int32, (OFFSETS, WINDOW * LANES), 0)
    return jnp.where(rows == target[0:1], 1.0, 0.0)


def prepare_kernel(
    w_qkv_ref,
    w_out_ref,
    w_up_ref,
    w_down_ref,
    rows_ref,
    up_bias_ref,
    log_scale_ref,
    net_ref,
    coords_ref,
    target_ref,
    qkv_f,
    out_f,
    up_f,
    down_f,
    down_b,
    up_b,
    out_b,
    qkv_b,
    cols_ref,
    up_cols_ref,
    scale_ref,
    bias_ref,
):
    def packed(w):
        hi, lo = split(w)
        return jnp.concatenate(
            [jnp.concatenate([hi, hi], 1), jnp.concatenate([lo, jnp.zeros_like(lo)], 1)], 0
        )

    def stacked(w):
        hi, lo = split(w)
        return jnp.concatenate([hi, lo], 0)

    qkv_f[...] = packed(w_qkv_ref[...].T)
    qkv_b[...] = stacked(w_qkv_ref[...])
    out_f[...] = packed(w_out_ref[...].T)
    out_b[...] = packed(w_out_ref[...])
    up_f[...] = packed(w_up_ref[...].T)
    up_b[...] = stacked(w_up_ref[...])
    down_b[...] = packed(w_down_ref[...].T)
    down_f[...] = stacked(w_down_ref[...])

    for i in range(cols_ref.shape[0]):
        cols_ref[i] = jnp.broadcast_to(rows_ref[i : i + 1], (LANES, WIDTH)).T
    up_cols_ref[...] = jnp.broadcast_to(up_bias_ref[...], (LANES, HIDDEN)).T

    lanes = lax.broadcasted_iota(jnp.int32, (1, LANES), 1)
    net = net_ref[...]
    _, hidden, _ = bias_net(net, coords_ref[...])
    table = 16.0 / (1.0 + jnp.exp(-exact(head_rows(net), hidden, ((1,), (0,)))))
    tiles = exact(table, one_hot(target_ref[...]), ((1,), (0,)))
    place = lax.broadcasted_iota(jnp.int32, (PLACES, LANES), 0)
    other = lax.broadcasted_iota(jnp.int32, (PLACES, LANES), 1) % PLACES
    apart_r = (place % WINDOW < SHIFT) != (other % WINDOW < SHIFT)
    apart_c = (place // WINDOW < SHIFT) != (other // WINDOW < SHIFT)
    for h in range(HEADS):
        scale = jnp.exp(jnp.full((1, LANES), log_scale_ref[h], f32))
        scale_ref[h : h + 1, :] = scale
        tile = jnp.concatenate(
            [tiles[h : h + 1, r * LANES : (r + 1) * LANES] for r in range(WINDOW)], 0
        )
        columns = []
        for j in range(WINDOW):
            turned = pltpu.roll(tile, (72 + 8 * j) % LANES, 1)
            columns.append(jnp.where(lanes < PLACES, turned, pltpu.roll(turned, PLACES, 1)))
        bias = jnp.concatenate(columns, 0) - (scale + 16.0)
        bias_ref[0, h] = bias
        bias_ref[1, h] = jnp.where(apart_c, masked_score, bias)
        bias_ref[2, h] = jnp.where(apart_r, masked_score, bias)
        bias_ref[3, h] = jnp.where(apart_r | apart_c, masked_score, bias)


def prepare(weights, rows, up_bias, log_scale, net, coords, target):
    smem = pl.BlockSpec(memory_space=pltpu.SMEM)
    shapes = [
        ((6 * WIDTH, 2 * WIDTH), bf16),
        ((2 * WIDTH, 2 * WIDTH), bf16),
        ((2 * HIDDEN, 2 * WIDTH), bf16),
        ((2 * WIDTH, HIDDEN), bf16),
        ((2 * HIDDEN, 2 * WIDTH), bf16),
        ((2 * WIDTH, HIDDEN), bf16),
        ((2 * WIDTH, 2 * WIDTH), bf16),
        ((2 * WIDTH, 3 * WIDTH), bf16),
        ((rows.shape[0], WIDTH, LANES), f32),
        ((HIDDEN, LANES), f32),
        ((8, LANES), f32),
        ((4, HEADS, PLACES, LANES), f32),
    ]
    shapes = [jax.ShapeDtypeStruct(s, t) for s, t in shapes]
    return pl.pallas_call(
        prepare_kernel,
        grid=(1,),
        in_specs=[whole(a) for a in (*weights, rows, up_bias)]
        + [smem]
        + [whole(a) for a in (net, coords, target)],
        out_specs=[whole(a) for a in shapes],
        out_shape=shapes,
        compiler_params=in_order,
    )(*weights, rows, up_bias, log_scale, net, coords, target)


def stack_rows(hi, lo):
    return jnp.concatenate([hi, lo], 0)


def block_kernel(
    step_items,
    token_count,
    flags_ref,
    lead_ref,
    x_own,
    x_right,
    x_down,
    x_corner,
    ct_own,
    stats_ref,
    running_ref,
    qkv_f,
    out_f,
    up_f,
    down_f,
    down_b,
    up_b,
    out_b,
    qkv_b,
    cols_ref,
    up_cols_ref,
    scale_ref,
    bias_ref,
    net_ref,
    coords_ref,
    target_ref,
    out_keep,
    dn_keep,
    send_right,
    send_down,
    send_corner,
    grads_ref,
    norm_ref,
    affine_ref,
    g_qkv_ref,
    g_out_ref,
    g_up_ref,
    g_down_ref,
    sums_ref,
    dpos_ref,
    dcos_ref,
    flat_ref,
):
    step = pl.program_id(0)

    @pl.when(step == 0)
    def _():
        every = stats_ref[...]
        devices = every.shape[0]
        means, squares = every[:, 0, :LANES], every[:, 0, LANES:]
        mean = jnp.sum(means, 0, keepdims=True) * (1.0 / devices)
        apart = means - mean
        var = (
            jnp.sum(squares, 0, keepdims=True) * (1.0 / token_count)
            + jnp.sum(apart * apart, 0, keepdims=True) * (1.0 / devices)
        )
        inv_std = lax.rsqrt(var + norm_eps)
        affine_ref[0] = jnp.broadcast_to(mean, (LANES, LANES)).T[:WIDTH]
        affine_ref[1] = jnp.broadcast_to(inv_std, (LANES, LANES)).T[:WIDTH]
        pad = jnp.zeros((1, LANES - WIDTH), f32)
        running = jnp.concatenate([running_ref[...], jnp.concatenate([pad, pad], 0)], 1)
        norm_ref[0:1] = mean
        norm_ref[1:2] = inv_std
        norm_ref[2:3] = (1.0 - momentum) * running[0:1] + momentum * mean
        norm_ref[3:4] = (1.0 - momentum) * running[1:2] + momentum * var * (
            token_count / (token_count - 1.0)
        )
        norm_ref[4:8] = jnp.zeros((4, LANES), f32)
        g_qkv_ref[...] = jnp.zeros_like(g_qkv_ref)
        g_out_ref[...] = jnp.zeros_like(g_out_ref)
        g_up_ref[...] = jnp.zeros_like(g_up_ref)
        g_down_ref[...] = jnp.zeros_like(g_down_ref)
        sums_ref[...] = jnp.zeros_like(sums_ref)
        dpos_ref[...] = jnp.zeros_like(dpos_ref)
        dcos_ref[...] = jnp.zeros_like(dcos_ref)

    first_half = lax.broadcasted_iota(jnp.int32, (1, PAIR), 1) < PLACES

    def narrow(weight, x_hi, x_lo):
        r = dot(weight, stack_rows(x_hi, x_lo))
        m = weight.shape[0] // 2
        return r[:m] + r[m:]

    def wide(weight, x_hi, x_lo):
        r = dot(weight[...], x_hi)
        m = weight.shape[0] // 2
        return (r[:m] + r[m:]) + dot(weight[:m], x_lo)

    def halves(v):
        m = v.shape[0] // 2
        return jnp.where(first_half, v[:m], v[m:])

    def col(i):
        return cols_ref[i]

    def per_item(fn):
        return jnp.concatenate([fn(m) for m in range(step_items)], 1)

    def spread_cols(i):
        c = col(i)
        return jnp.concatenate([c] * step_items, 1)

    def gather(own, part, m):
        right, down = 12 * part, 4 * part
        top_l = own[m, SHIFT : SHIFT + WINDOW, :]
        top_r = x_right[m, right : right + WINDOW, :]
        low_l = jnp.concatenate([own[m, SHIFT + WINDOW :, :], x_down[m, down : down + SHIFT, :]], 0)
        low_r = jnp.concatenate(
            [x_right[m, right + WINDOW : right + 12, :], x_corner[m, down : down + SHIFT, :]], 0
        )
        tiles = [
            side[:, j * WIDTH : (j + 1) * WIDTH]
            for side in (top_l, top_r, low_l, low_r)
            for j in range(4)
        ]
        return jnp.concatenate(tiles, 0).T

    def scatter(value, keep, part, m):
        rows = value.T
        sides = [
            jnp.concatenate([rows[(4 * s + j) * 8 : (4 * s + j + 1) * 8] for j in range(4)], 1)
            for s in range(4)
        ]
        right, down = 12 * part, 4 * part
        keep[m, 0:WINDOW, :] = sides[0]
        keep[m, WINDOW:, :] = sides[2][:SHIFT]
        send_right[m, right : right + WINDOW, :] = sides[1]
        send_right[m, right + WINDOW : right + 12, :] = sides[3][:SHIFT]
        send_down[m, down : down + SHIFT, :] = sides[2][SHIFT:]
        send_corner[m, down : down + SHIFT, :] = sides[3][SHIFT:]

    def mean_rows(v):
        return jnp.sum(v, 0, keepdims=True) * (1.0 / WIDTH)

    def layer_norm(v):
        centred = v - mean_rows(v)
        rstd = lax.rsqrt(mean_rows(centred * centred) + norm_eps)
        return centred * rstd, rstd

    items = [step * step_items + m for m in range(step_items)]
    leads = [(lead_ref[i] + 1).astype(f32) * (1.0 / LEAD_STEPS) for i in items]
    raw = per_item(lambda m: gather(x_own, 0, m))
    mean = jnp.concatenate([affine_ref[0]] * step_items, 1)
    inv_std = jnp.concatenate([affine_ref[1]] * step_items, 1)
    normed = (raw - mean) * inv_std
    n_hi, n_lo = split(normed)

    joined = narrow(qkv_f[...], n_hi, n_lo)
    query = joined[:WIDTH] + spread_cols(0)
    key = joined[WIDTH : 2 * WIDTH]
    value = joined[2 * WIDTH :] + spread_cols(1)

    def unit(v):
        rows, inverses = [], []
        for h in range(HEADS):
            part = v[h * HEAD_DIM : (h + 1) * HEAD_DIM]
            inverse = lax.rsqrt(jnp.sum(part * part, 0, keepdims=True) + unit_eps)
            rows.append(part * inverse)
            inverses.append(inverse)
        return rows, inverses

    q_rows, q_inv = unit(query)
    k_rows, k_inv = unit(key)
    v_rows = [value[h * HEAD_DIM : (h + 1) * HEAD_DIM] for h in range(HEADS)]

    def of_item(v, m):
        return v[:, m * PAIR : (m + 1) * PAIR]

    def three(a_hi, a_lo, b_hi, b_lo):
        left = jnp.concatenate([a_hi, a_lo, a_hi], 0)
        right = jnp.concatenate([b_hi, b_hi, b_lo], 0)
        return halves(dot(left.T, right))

    def side_by_side(v):
        other = pltpu.roll(v, PLACES, 1)
        v_hi, v_lo = split(v)
        o_hi, o_lo = split(other)
        top = jnp.concatenate([jnp.where(first_half, v_hi, o_lo), v_hi], 1)
        low = jnp.concatenate([jnp.where(first_half, o_hi, v_lo), o_hi], 1)
        return jnp.concatenate([top, low], 0)[:, : 3 * PLACES]

    def over_keys(both, e_hi, e_lo):
        return halves(dot(both, jnp.concatenate([e_hi, e_hi, e_lo], 0)))

    def over_queries(v_hi, v_lo, e_hi, e_lo):
        zero = jnp.zeros_like(v_hi)

        def apart(x):
            return jnp.concatenate(
                [jnp.where(first_half, x, zero), jnp.where(first_half, zero, x)], 0
            )

        a_hi, a_lo = apart(v_hi), apart(v_lo)
        left = jnp.concatenate(
            [
                jnp.concatenate([a_hi, a_hi], 1),
                jnp.concatenate([a_lo, jnp.zeros_like(a_lo)], 1),
            ],
            0,
        )
        weights = jnp.concatenate([e_hi, e_lo], 1)
        r = dot_rows(left, jnp.concatenate([weights, weights], 0))
        return halves(r[:PLACES] + r[PLACES:])

    pairs = [(m, h) for m in range(step_items) for h in range(HEADS)]
    q_parts = [split(of_item(q_rows[h], m)) for m, h in pairs]
    k_parts = [split(of_item(k_rows[h], m)) for m, h in pairs]
    cosines = [three(*k, *q) for k, q in zip(k_parts, q_parts)]
    expos, inverses = [], []
    for (m, h), cosine in zip(pairs, cosines):
        flag0 = flags_ref[2 * items[m]]
        flag1 = flags_ref[2 * items[m] + 1]
        offset = jnp.where(first_half, bias_ref[flag0, h], bias_ref[flag1, h])
        expo = jnp.exp(cosine * scale_ref[h : h + 1, :] + offset)
        expos.append(expo)
        inverses.append(1.0 / jnp.sum(expo, 0, keepdims=True))
    e_parts = [split(e) for e in expos]
    mixes = [
        over_keys(side_by_side(of_item(v_rows[h], m)), *e) * inverse
        for (m, h), e, inverse in zip(pairs, e_parts, inverses)
    ]
    mixed = jnp.concatenate(
        [jnp.concatenate(mixes[HEADS * m : HEADS * (m + 1)], 0) for m in range(step_items)], 1
    )

    o_hi, o_lo = split(mixed)
    attn_hat, attn_rstd = layer_norm(narrow(out_f[...], o_hi, o_lo) + spread_cols(2))

    def gain(base):
        return per_item(lambda m: 1.0 + col(base) + leads[m] * col(base + 1))

    def shift(base):
        return per_item(lambda m: col(base + 2) + leads[m] * col(base + 3))

    gain0 = gain(4)
    first = normed + attn_hat * gain0 + shift(4)
    f_hi, f_lo = split(first)

    up_bias = jnp.concatenate([up_cols_ref[...]] * step_items, 1)
    u = narrow(up_f[...], f_hi, f_lo) + up_bias
    phi, bell = normal_parts(u)
    hidden = u * phi
    slope = phi + u * bell
    h_hi, h_lo = split(hidden)
    branch = wide(down_f, h_hi, h_lo) + spread_cols(3)
    hat, rstd = layer_norm(branch)
    gain1 = gain(8)
    out = first + hat * gain1 + shift(8)
    for m in range(step_items):
        scatter(of_item(out, m), out_keep, 0, m)

    def norm_back(g, hat, rstd, gain, base):
        weighted = g * hat
        for m in range(step_items):
            a, b = of_item(weighted, m), of_item(g, m)
            sums_ref[base] += a
            sums_ref[base + 1] += leads[m] * a
            sums_ref[base + 2] += b
            sums_ref[base + 3] += leads[m] * b
        e = g * gain
        return (e - mean_rows(e) - hat * mean_rows(e * hat)) * rstd

    def add_items(v):
        total = of_item(v, 0)
        for m in range(1, step_items):
            total = total + of_item(v, m)
        return total

    ones_rows = jnp.where(
        lax.broadcasted_iota(jnp.int32, (LANES - WIDTH, step_items * PAIR), 0) == 0, 1.0, 0.0
    ).astype(bf16)
    zero_rows = jnp.zeros((LANES - WIDTH, step_items * PAIR), bf16)

    def outer(a_hi, a_lo, b_hi, b_lo):
        right = jnp.concatenate([b_hi, ones_rows, b_lo, zero_rows], 0)
        r = dot_rows(stack_rows(a_hi, a_lo), right)
        m = a_hi.shape[0]
        return (r[:m, :LANES] + r[m:, :LANES]) + r[:m, LANES:]

    cot = per_item(lambda m: gather(ct_own, 1, m))
    d_branch = norm_back(cot, hat, rstd, gain1, 4)
    sums_ref[8] += add_items(d_branch)
    z_hi, z_lo = split(d_branch)
    g_down_ref[...] += outer(h_hi, h_lo, z_hi, z_lo)
    d_pre = narrow(down_b[...], z_hi, z_lo) * slope
    p_hi, p_lo = split(d_pre)
    g_up_ref[...] += outer(p_hi, p_lo, f_hi, f_lo)
    d_first = cot + wide(up_b, p_hi, p_lo)
    d_attn = norm_back(d_first, attn_hat, attn_rstd, gain0, 0)
    a_hi, a_lo = split(d_attn)
    g_out_ref[...] += outer(a_hi, a_lo, o_hi, o_lo)
    d_mixed = narrow(out_b[...], a_hi, a_lo)

    d_outs = [
        of_item(d_mixed, m)[h * HEAD_DIM : (h + 1) * HEAD_DIM] * inverse
        for (m, h), inverse in zip(pairs, inverses)
    ]
    d_parts = [split(d) for d in d_outs]
    d_probs = [
        three(*split(of_item(v_rows[h], m)), *d) for (m, h), d in zip(pairs, d_parts)
    ]
    s_parts = []
    for n, (m, h) in enumerate(pairs):
        delta = jnp.sum(d_outs[n] * mixes[n], 0, keepdims=True)
        d_scores = expos[n] * (d_probs[n] - delta)
        dpos_ref[h] += d_scores
        folded = d_scores * cosines[n]
        total = folded[0:8]
        for i in range(1, PLACES // 8):
            total = total + folded[8 * i : 8 * i + 8]
        dcos_ref[h] += total
        s_parts.append(split(d_scores))
    dv_rows = [over_queries(*d, *e) for d, e in zip(d_parts, e_parts)]
    dk_rows = [over_queries(*q, *d) for q, d in zip(q_parts, s_parts)]
    dq_rows = [
        over_keys(side_by_side(of_item(k_rows[h], m)), *d) for (m, h), d in zip(pairs, s_parts)
    ]

    def unit_back(grads, rows, inverse):
        out = []
        for n, (m, h) in enumerate(pairs):
            d = grads[n] * scale_ref[h : h + 1, :]
            row = of_item(rows[h], m)
            d = d - row * jnp.sum(row * d, 0, keepdims=True)
            out.append(d * of_item(inverse[h], m))
        return out

    dq_rows = unit_back(dq_rows, q_rows, q_inv)
    dk_rows = unit_back(dk_rows, k_rows, k_inv)
    d_joined = jnp.concatenate(
        [
            jnp.concatenate(
                [d for rows in (dq_rows, dk_rows, dv_rows) for d in rows[HEADS * m : HEADS * (m + 1)]], 0
            )
            for m in range(step_items)
        ],
        1,
    )
    j_hi, j_lo = split(d_joined)
    g_qkv_ref[...] += outer(j_hi, j_lo, n_hi, n_lo)
    d_normed = d_first + wide(qkv_b, j_hi, j_lo)
    sums_ref[9] += add_items(d_normed)
    sums_ref[10] += add_items(d_normed * normed)
    for m in range(step_items):
        scatter(of_item(d_normed, m), dn_keep, 1, m)

    @pl.when(step == pl.num_programs(0) - 1)
    def _():
        def lane_sums(v):
            return jnp.sum(v.T, 0, keepdims=True)

        flat_ref[...] = jnp.zeros_like(flat_ref)
        g = g_qkv_ref[...].T
        flat_ref[0:96, :] = g[:WIDTH, :LANES]
        flat_ref[96:192, :] = g[:WIDTH, LANES : 2 * LANES]
        qv = g[WIDTH : WIDTH + 1]
        g_out = g_out_ref[...].T
        flat_ref[192:288, :] = jnp.concatenate([g_out[:WIDTH], g[:WIDTH, 2 * LANES :]], 1)
        g_up = g_up_ref[...].T
        g_down = g_down_ref[...].T
        for k in range(3):
            lanes = slice(k * LANES, (k + 1) * LANES)
            flat_ref[288 + 96 * k : 384 + 96 * k, :] = g_up[:WIDTH, lanes]
            flat_ref[576 + 96 * k : 672 + 96 * k, :] = g_down[:WIDTH, lanes]
            flat_ref[876 + k : 877 + k, :] = g_up[WIDTH : WIDTH + 1, lanes]
        totals = [lane_sums(sums_ref[i]) for i in range(11)]
        for i in range(8):
            flat_ref[864 + i : 865 + i, :WIDTH] = totals[i]
        flat_ref[872:873, :WIDTH] = totals[8]
        flat_ref[873:874, :WIDTH] = g_out[WIDTH : WIDTH + 1]
        flat_ref[874:875, :WIDTH] = qv[:, :WIDTH]
        flat_ref[875:876, :WIDTH] = qv[:, 2 * WIDTH :]
        lane = lax.broadcasted_iota(jnp.int32, (1, LANES), 1)
        scales = jnp.zeros((1, LANES), f32)
        for h in range(HEADS):
            total = jnp.sum(jnp.sum(dcos_ref[h], 0, keepdims=True), 1, keepdims=True)
            scales = jnp.where(lane == WIDTH + h, total * scale_ref[h : h + 1, :], scales)
        flat_ref[864:865, :] = flat_ref[864:865, :] + scales

        rows = []
        for h in range(HEADS):
            d = dpos_ref[h]
            d = jnp.where(first_half, d + pltpu.roll(d, PLACES, 1), 0.0)
            tile = jnp.zeros((WINDOW, LANES), f32)
            for j in range(WINDOW):
                tile = tile + pltpu.roll(d[8 * j : 8 * j + 8], 56 - 8 * j, 1)
            rows.append(jnp.concatenate([tile[r : r + 1] for r in range(WINDOW)], 1))
        rows.append(jnp.zeros((8 - HEADS, WINDOW * LANES), f32))
        d_table = exact(jnp.concatenate(rows, 0), one_hot(target_ref[...]), ((1,), (1,)))
        net, coords = net_ref[...], coords_ref[...]
        column, hidden, slope = bias_net(net, coords)
        gate = 1.0 / (1.0 + jnp.exp(-exact(head_rows(net), hidden, ((1,), (0,)))))
        d_logit = d_table * (16.0 * gate * (1.0 - gate))
        g_w2 = exact(d_logit, hidden, ((1,), (1,)))
        d_hidden = column(3) * d_logit[0:1] + column(4) * d_logit[1:2] + column(5) * d_logit[2:3]
        g_first = exact(coords, d_hidden * slope, ((1,), (1,)))
        for i, row in enumerate(
            [g_first[0:1], g_first[1:2], g_first[2:3], g_w2[0:1], g_w2[1:2], g_w2[2:3]]
        ):
            for k in range(4):
                at = 879 + 4 * i + k
                flat_ref[at : at + 1, :] = row[:, k * LANES : (k + 1) * LANES]

        slots, slot_rows, _ = grads_ref.shape
        share = slot_rows - 2
        for j in range(slots):
            grads_ref[j, 0:share, :] = flat_ref[share * j : share * (j + 1), :]
        for i in range(2):
            grads_ref[:, share + i : share + i + 1, :WIDTH] = jnp.broadcast_to(
                totals[9 + i][None], (slots, 1, WIDTH)
            )
            grads_ref[:, share + i : share + i + 1, WIDTH:] = jnp.zeros(
                (slots, 1, LANES - WIDTH), f32
            )


def run_block(flags, lead, x, ct, halo, stats, running, prepared, net, coords, target, token_count):
    items, tile_rows, flat = x.shape
    half = flat // 2
    step_items = block_of(items)

    def own(i):
        return (i, 0, 1)

    def rows(n):
        return pl.BlockSpec((step_items, n, half), lambda i: (i, 0, 0))

    smem = pl.BlockSpec(memory_space=pltpu.SMEM)
    field = pl.BlockSpec((step_items, tile_rows, half), own)
    out_rows = (12, 12, 24, 8, 8)
    slots = stats.shape[0]
    slot_rows = -(-PAYLOAD // slots)
    slot_rows = -(-(slot_rows + 2) // 8) * 8
    tail = [
        jax.ShapeDtypeStruct((slots, slot_rows, LANES), f32),
        jax.ShapeDtypeStruct((8, LANES), f32),
    ]
    return pl.pallas_call(
        partial(block_kernel, step_items, float(token_count)),
        grid=(items // step_items,),
        in_specs=[smem, smem, field, rows(24), rows(8), rows(8), field]
        + [whole(a) for a in (stats, running, *prepared, net, coords, target)],
        out_specs=[rows(n) for n in out_rows] + [whole(a) for a in tail],
        out_shape=[jax.ShapeDtypeStruct((items, n, half), f32) for n in out_rows] + tail,
        scratch_shapes=[
            pltpu.VMEM((2, WIDTH, LANES), f32),
            pltpu.VMEM((3 * WIDTH, LANES), f32),
            pltpu.VMEM((WIDTH, LANES), f32),
            pltpu.VMEM((HIDDEN, LANES), f32),
            pltpu.VMEM((HIDDEN, LANES), f32),
            pltpu.VMEM((11, WIDTH, LANES), f32),
            pltpu.VMEM((HEADS, PLACES, LANES), f32),
            pltpu.VMEM((HEADS, 8, LANES), f32),
            pltpu.VMEM((slots * (slot_rows - 2), LANES), f32),
        ],
        compiler_params=in_order,
    )(flags, lead, x, *halo, ct, stats, running, *prepared, net, coords, target)


def place(ref_out, m, keep, right, down, corner, part, fn):
    half = keep.shape[2]
    at, low = 12 * part, 4 * part
    for rows, left, own in (
        (slice(0, SHIFT), corner[m, low : low + SHIFT, :], down[m, low : low + SHIFT, :]),
        (slice(SHIFT, 16), right[m, at : at + 12, :], keep[m]),
    ):
        for lanes, value in ((slice(0, half), left), (slice(half, 2 * half), own)):
            ref_out[m, rows, lanes] = fn(value, rows, lanes)


def outputs_kernel(keep_ref, right_ref, down_ref, corner_ref, out_ref):
    for m in range(out_ref.shape[0]):
        place(out_ref, m, keep_ref, right_ref, down_ref, corner_ref, 0, lambda v, r, l: v)


def input_grad_kernel(
    token_count, x_ref, keep_ref, right_ref, down_ref, corner_ref, norm_ref, sums_ref, out_ref
):
    cols = x_ref.shape[2] // WIDTH

    def wide(row):
        return jnp.concatenate([row[:, :WIDTH]] * cols, 1)

    mean, inv_std = norm_ref[0:1], norm_ref[1:2]
    at = sums_ref.shape[0] - 2
    mean_grad = sums_ref[at : at + 1] * (1.0 / token_count)
    mean_cross = sums_ref[at + 1 : at + 2] * (1.0 / token_count)
    factor, centre = wide(inv_std), wide(mean)
    offset, slope = wide(inv_std * mean_grad), wide(inv_std * inv_std * mean_cross)
    for m in range(x_ref.shape[0]):

        def grad(v, rows, lanes):
            x = x_ref[m, rows, lanes] - centre[:, lanes]
            return factor[:, lanes] * v - offset[:, lanes] - x * slope[:, lanes]

        place(out_ref, m, keep_ref, right_ref, down_ref, corner_ref, 1, grad)


def final_specs(x_shape):
    items, rows, flat = x_shape
    step_items = block_of(items)

    def spec(n):
        return pl.BlockSpec((step_items, n, flat // 2), lambda i: (i, 0, 0))

    field = pl.BlockSpec((step_items, rows, flat), lambda i: (i, 0, 0))
    return (items // step_items,), field, [spec(12), spec(24), spec(8), spec(8)]


def place_outputs(x_shape, parts):
    grid, field, specs = final_specs(x_shape)
    return pl.pallas_call(
        outputs_kernel,
        grid=grid,
        in_specs=specs,
        out_specs=field,
        out_shape=jax.ShapeDtypeStruct(x_shape, f32),
        compiler_params=in_order,
    )(*parts)


def input_grad(x, parts, norm, sums, token_count):
    grid, field, specs = final_specs(x.shape)
    return pl.pallas_call(
        partial(input_grad_kernel, float(token_count)),
        grid=grid,
        in_specs=[field]
        + specs
        + [pl.BlockSpec(a.shape, lambda i: (0, 0)) for a in (norm, sums)],
        out_specs=field,
        out_shape=jax.ShapeDtypeStruct(x.shape, f32),
        compiler_params=in_order,
    )(x, *parts, norm, sums)


def unpack_kernel(
    all_ref,
    qkv_ref,
    qv_ref,
    scale_ref,
    w1_ref,
    b1_ref,
    w2_ref,
    out_ref,
    b_out_ref,
    up_ref,
    b_up_ref,
    down_ref,
    b_down_ref,
    norm_ref,
    flat_ref,
):
    slots, slot_rows, _ = all_ref.shape
    share = slot_rows - 2
    for j in range(slots):
        flat_ref[share * j : share * (j + 1), :] = all_ref[j, 0:share, :]
    qkv_ref[:, 0:LANES] = flat_ref[0:96, :]
    qkv_ref[:, LANES : 2 * LANES] = flat_ref[96:192, :]
    qkv_ref[:, 2 * LANES :] = flat_ref[192:288, WIDTH:]
    out_ref[...] = flat_ref[192:288, :WIDTH]
    for k in range(3):
        lanes = slice(k * LANES, (k + 1) * LANES)
        up_ref[:, lanes] = flat_ref[288 + 96 * k : 384 + 96 * k, :]
        down_ref[:, lanes] = flat_ref[576 + 96 * k : 672 + 96 * k, :]
        b_up_ref[:, lanes] = flat_ref[876 + k : 877 + k, :]
    norm_ref[...] = flat_ref[864:872, :WIDTH]
    scale_ref[...] = flat_ref[864:865, WIDTH : WIDTH + HEADS]
    b_down_ref[...] = flat_ref[872:873, :WIDTH]
    b_out_ref[...] = flat_ref[873:874, :WIDTH]
    qv_ref[...] = flat_ref[874:876, :WIDTH]
    for k in range(4):
        lanes = slice(k * LANES, (k + 1) * LANES)
        for i in range(2):
            w1_ref[i : i + 1, lanes] = flat_ref[879 + 4 * i + k : 880 + 4 * i + k, :]
        b1_ref[:, lanes] = flat_ref[887 + k : 888 + k, :]
        for i in range(3):
            w2_ref[i : i + 1, lanes] = flat_ref[891 + 4 * i + k : 892 + 4 * i + k, :]


def unpack(everything):
    slots, slot_rows, _ = everything.shape
    shapes = [
        (WIDTH, 3 * WIDTH),
        (2, WIDTH),
        (1, HEADS),
        (2, 512),
        (1, 512),
        (HEADS, 512),
        (WIDTH, WIDTH),
        (1, WIDTH),
        (WIDTH, HIDDEN),
        (1, HIDDEN),
        (WIDTH, HIDDEN),
        (1, WIDTH),
        (8, WIDTH),
    ]
    shapes = [jax.ShapeDtypeStruct(s, f32) for s in shapes]
    return pl.pallas_call(
        unpack_kernel,
        grid=(1,),
        in_specs=[whole(everything)],
        out_specs=[whole(a) for a in shapes],
        out_shape=shapes,
        compiler_params=in_order,
        scratch_shapes=[pltpu.VMEM((slots * (slot_rows - 2), LANES), f32)],
    )(everything)


def take_from(block, dy, dx):
    rows, cols = lax.axis_size("ty"), lax.axis_size("tx")
    route = []
    for i in range(rows * cols):
        y, x = divmod(i, cols)
        route.append((((y + dy) % rows) * cols + (x + dx) % cols, i))
    return lax.ppermute(block, ("ty", "tx"), route)


def exchange(slots):
    return lax.all_to_all(slots, axes_all, 0, 0, tiled=True)


def shards(
    inputs,
    regions,
    lead_step_index,
    running_channel_mean,
    running_channel_variance,
    query_key_value_weight,
    query_value_bias,
    log_cosine_scale,
    bias_net_weight1,
    bias_net_bias1,
    bias_net_weight2,
    output_weight,
    projection_bias,
    up_weight,
    up_bias,
    down_weight,
    down_bias,
    conditioned_norm_values,
    cotangent,
):
    items, tile_rows, flat = inputs.shape
    devices = lax.axis_size(axes_all)
    token_count = items * tile_rows * (flat // WIDTH) * devices

    stats, right, down, corner = pack(inputs, cotangent, devices)
    halo = (take_from(right, 0, 1), take_from(down, 1, 0), take_from(corner, 1, 1))
    stats = exchange(stats)

    row_cut = regions[:, ::WINDOW, 0] != regions[:, WINDOW - 1 :: WINDOW, 0]
    col_cut = regions[:, ::WINDOW, 0] != regions[:, ::WINDOW, WINDOW - 1]
    flags = (2 * row_cut.astype(jnp.int32) + col_cut.astype(jnp.int32)).reshape(-1)
    rows = jnp.concatenate(
        [
            query_value_bias,
            projection_bias[None],
            down_bias[None],
            conditioned_norm_values.reshape(8, WIDTH),
        ],
        0,
    )
    net = jnp.concatenate(
        [
            bias_net_weight1,
            bias_net_bias1[None],
            bias_net_weight2.T,
            jnp.zeros((2, bias_net_bias1.shape[0]), f32),
        ],
        0,
    )
    coords, target = offset_constants()
    weights = (query_key_value_weight, output_weight, up_weight, down_weight)
    prepared = prepare(weights, rows, up_bias[None], log_cosine_scale, net, coords, target)
    running = jnp.stack([running_channel_mean, running_channel_variance])
    out_keep, dn_keep, right, down, corner, grads, norm = run_block(
        flags,
        lead_step_index,
        inputs,
        cotangent,
        halo,
        stats,
        running,
        prepared,
        net,
        coords,
        target,
        token_count,
    )
    halo = (take_from(right, 0, -1), take_from(down, -1, 0), take_from(corner, -1, -1))
    share = jnp.sum(exchange(grads), 0)
    share, halo = lax.optimization_barrier((share, halo))
    outputs = place_outputs(inputs.shape, (out_keep,) + halo)
    grad_inputs = input_grad(inputs, (dn_keep,) + halo, norm, share, token_count)
    everything = exchange(jnp.broadcast_to(share[None], grads.shape))
    (
        g_qkv,
        g_qv,
        g_scale,
        g_w1,
        g_b1,
        g_w2,
        g_out,
        g_b_out,
        g_up,
        g_b_up,
        g_down,
        g_b_down,
        g_norm,
    ) = unpack(everything)
    return (
        outputs,
        grad_inputs,
        g_qkv,
        g_qv,
        g_scale.reshape(-1),
        g_w1,
        g_b1.reshape(-1),
        g_w2.T,
        g_out,
        g_b_out.reshape(-1),
        g_up,
        g_b_up.reshape(-1),
        g_down,
        g_b_down.reshape(-1),
        g_norm.reshape(2, 4, WIDTH),
        norm[2, :WIDTH],
        norm[3, :WIDTH],
    )


def solution(mesh):
    tiled = P("items", "ty", "tx")
    placed = (tiled, tiled, P("items")) + (P(),) * 15 + (tiled,)
    return jax.shard_map(
        shards,
        mesh=mesh,
        in_specs=placed,
        out_specs=(tiled, tiled) + (P(),) * 15,
        check_vma=False,
    )
```

time: 241 us -> 130 us (0.54)
  waiting for transfers between devices: 82.9 us -> 37 us
  Pallas kernels: 91.7 us -> 58.9 us
  local copies, waits for them, and re-layouts: 25.6 us -> 5.58 us
  matrix products: 7.77 us -> 0 us
  other arithmetic: 8.61 us -> 3.94 us
    ppermute x5 -> x0, waiting for transfers between devices: 58.4 us -> none  [reduce_all(): v = v + lax.ppermute(v, axes_all, [(i, i ^ step) for i in range(n)])]
    pallas_call x3 -> x6, Pallas kernels: 91.7 us -> 58.9 us  [the longest x1 39.7 us: run_block(): pl.pallas_call(partial(block_kernel, step_items, float(token_count)), gri...]
    all_to_all x1 -> x3, waiting for transfers between devices: 0.01 us -> 18.2 us  [exchange(): return lax.all_to_all(slots, axes_all, 0, 0, tiled=True)]
    dot_general x7 -> x0, matrix products: 7.77 us -> none  [the longest x2 3.61 us: position_bias(): lax.dot_general(table, one_hot, (((0,), (1,)), ((), ())), precision=precise)]
    all_to_all x1 -> x3, starting transfers between devices: 7.43 us -> 13.3 us  [exchange(): return lax.all_to_all(slots, axes_all, 0, 0, tiled=True)]
    slice x13 -> x0, local copies, waits for them, and re-layouts: 5.83 us -> none  [the longest x2 1.95 us: halo(): field[:, :SHIFT, :half]]
    ppermute x12 -> x6, waiting for transfers between devices: 24.5 us -> 18.8 us  [take_from(): return lax.ppermute(block, ('ty', 'tx'), route)]
    ppermute x5 -> x0, starting transfers between devices: 5.58 us -> none  [reduce_all(): v = v + lax.ppermute(v, axes_all, [(i, i ^ step) for i in range(n)])]
  transfers between devices with their start and end apart: 18 -> 9, of which waited for: 9 -> 6; matrix products, arithmetic and copies ran while one was open for 12% -> 4% of each run, Pallas kernels for 0% -> 10%
where the time goes in v2:
time: 130 us; the launch traced here: 128 us
  Pallas kernels  58.9 us (45%)
  waiting for transfers between devices  37 us (28%)
  starting transfers between devices  21.9 us (17%)
  local copies, waits for them, and re-layouts  5.58 us (4%)
  other arithmetic  3.94 us (3%)
    pallas_call x1, Pallas kernels, run_block(): pl.pallas_call(partial(block_kernel, step_items, float(token_count)), gri...  39.7 us
    ppermute x6, waiting for transfers between devices, take_from(): return lax.ppermute(block, ('ty', 'tx'), route)  18.8 us
    all_to_all x3, waiting for transfers between devices, exchange(): return lax.all_to_all(slots, axes_all, 0, 0, tiled=True)  18.2 us
    all_to_all x3, starting transfers between devices, exchange(): return lax.all_to_all(slots, axes_all, 0, 0, tiled=True)  13.3 us
    ppermute x6, starting transfers between devices, take_from(): return lax.ppermute(block, ('ty', 'tx'), route)  8.6 us
    pallas_call x1, Pallas kernels, prepare(): pl.pallas_call(prepare_kernel, grid=(1,), in_specs=[whole(a) for a in (*w...  4.52 us
    pallas_call x1, Pallas kernels, input_grad(): pl.pallas_call(partial(input_grad_kernel, float(token_count)), grid=grid,...  4.45 us
    pallas_call x1, Pallas kernels, pack(): pl.pallas_call(partial(pack_kernel, items), grid=(items // step_items,),...  4.43 us
  transfers between devices with their start and end apart: 9, of which 6 were waited for; matrix products, arithmetic and copies ran while one was open for 4% of the time, Pallas kernels for 10%

profile of v2, /device:TPU:0, one launch (start us, length us, event | category | flops | bytes accessed | tf_op | source)
XLA Modules:
  0.0 128.1 jit_solution(4509363267703666718)
XLA Ops:
  0.8 4.4 %shard_map.332 = (f32[32,1,256]{2,1,0:T(1,128)}, f32[32,24,384]{2,1,0:T(8,128)}, f32[32,8,384]{2,1,0:T(8,128)}, f32[32,8,384]{2,1,0:T(8,128)}) custom-call(f32[32,16,768]{2,1,0:T(8,128)} %x_ref.3, f32[32,16,768]{2,1,0:T(8,128)} %ct_own.1), custom_call_target="tpu_custom_call" | custom-call | tf_op jit(solution)/shard_map/pallas_call | solution.py:134
  5.2 2.4 %collective-permute-start = (f32[32,24,384]{2,1,0:T(8,128)}, f32[32,24,384]{2,1,0:T(8,128)S(1)}, u32[]{:S(2)}, u32[]{:S(2)}) collective-permute-start(f32[32,24,384]{2,1,0:T(8,128)} %get-tuple-element.57), channel_id=1, source_target_pairs={{4,0},{8,4},{12,8},{0,12},{20,16},{24,20},{28,24},{16,28},{5,1},{9... | collective-permute-start | bytes 3538952 | tf_op jit(solution)/shard_map/ppermute | solution.py:917
  7.6 5.0 %all-to-all-start = ((f32[32,1,256]{2,1,0:T(1,128)}), f32[32,1,256]{2,1,0:T(1,128)S(1)}, u32[]{:S(2)}, u32[]{:S(2)}) async-start(f32[32,1,256]{2,1,0:T(1,128)} %get-tuple-element.60), calls=%async_computation | async-start | bytes 65536 | tf_op jit(solution)/shard_map/all_to_all | solution.py:921
  12.6 1.8 %collective-permute-start.1 = (f32[32,8,384]{2,1,0:T(8,128)}, f32[32,8,384]{2,1,0:T(8,128)S(1)}, u32[]{:S(2)}, u32[]{:S(2)}) collective-permute-start(f32[32,8,384]{2,1,0:T(8,128)} %get-tuple-element.58), channel_id=1, source_target_pairs={{16,0},{20,4},{24,8},{28,12},{0,16},{4,20},{8,24},{12,28},{17,1},{... | collective-permute-start | bytes 1179656 | tf_op jit(solution)/shard_map/ppermute | solution.py:917
  14.4 0.9 collective-permute-start.2
  18.8 4.5 %shard_map.333 = (bf16[576,192]{1,0:T(8,128)(2,1)}, bf16[192,192]{1,0:T(8,128)(2,1)}, bf16[768,192]{1,0:T(8,128)(2,1)}, bf16[192,384]{1,0:T(8,128)(2,1)}, bf16[7...) custom-call(f32[96,288]{1,0:T(8,128)} %w_qkv_ref.1, ...), custom_call_target="tpu_custom_call" | custom-call | tf_op jit(solution)/shard_map/pallas_call | solution.py:286
  23.9 1.1 collective-permute-done.1.x_down
  25.1 7.2 %collective-permute-done.2.x_corner = f32[32,8,384]{2,1,0:T(8,128)S(1)} collective-permute-done((f32[32,8,384]{2,1,0:T(8,128)}, f32[32,8,384]{2,1,0:T(8,128)S(1)}, u32[]{:S(2)}, u32[]{:S(2)}) %collective-permute-start.2) | collective-permute-done | bytes 393248 | tf_op jit(solution)/shard_map/ppermute | solution.py:917
  33.4 39.7 %shard_map.334 = (f32[32,12,384]{2,1,0:T(8,128)}, f32[32,12,384]{2,1,0:T(8,128)}, f32[32,24,384]{2,1,0:T(8,128)}, f32[32,8,384]{2,1,0:T(8,128)}, f32[32,8,384]{2...) custom-call(s32[64]{0:T(128)} %add.8.flags_ref, s32[32]{0:T(128)} %lead_ref.1, f32[32,16,768]{2,1,0:T(8,128)} %x_ref.3, ...), custom_call_target="tpu_custom_call" | custom-call | tf_op jit(solution)/shard_map/pallas_call | solution.py:740
  73.2 1.6 %collective-permute-start.3 = (f32[32,24,384]{2,1,0:T(8,128)}, f32[32,24,384]{2,1,0:T(8,128)S(1)}, u32[]{:S(2)}, u32[]{:S(2)}) collective-permute-start(f32[32,24,384]{2,1,0:T(8,128)} %get-tuple-element.75), channel_id=1, source_target_pairs={{12,0},{0,4},{4,8},{8,12},{28,16},{16,20},{20,24},{24,28},{13,1},{... | collective-permute-start | bytes 3538952 | tf_op jit(solution)/shard_map/ppermute | solution.py:917
  74.8 4.3 %all-to-all-start.1 = ((f32[32,32,128]{2,1,0:T(8,128)}), f32[32,32,128]{2,1,0:T(8,128)S(1)}, u32[]{:S(2)}, u32[]{:S(2)}) async-start(f32[32,32,128]{2,1,0:T(8,128)} %get-tuple-element.74), calls=%async_computation.1 | async-start | bytes 1048576 | tf_op jit(solution)/shard_map/all_to_all | solution.py:921
  79.1 1.8 %collective-permute-start.4 = (f32[32,8,384]{2,1,0:T(8,128)}, f32[32,8,384]{2,1,0:T(8,128)S(1)}, u32[]{:S(2)}, u32[]{:S(2)}) collective-permute-start(f32[32,8,384]{2,1,0:T(8,128)} %get-tuple-element.76), channel_id=1, source_target_pairs={{16,0},{20,4},{24,8},{28,12},{0,16},{4,20},{8,24},{12,28},{17,1},{... | collective-permute-start | bytes 1179656 | tf_op jit(solution)/shard_map/ppermute | solution.py:917
  80.9 13.4 %all-to-all-done.1 = f32[32,32,128]{2,1,0:T(8,128)S(1)} async-done(((f32[32,32,128]{2,1,0:T(8,128)}), f32[32,32,128]{2,1,0:T(8,128)S(1)}, u32[]{:S(2)}, u32[]{:S(2)}) %all-to-all-start.1) | async-done | bytes 524320 | tf_op jit(solution)/shard_map/all_to_all | solution.py:921
  94.4 2.1 %collective-permute-done.4.down_ref = f32[32,8,384]{2,1,0:T(8,128)S(1)} collective-permute-done((f32[32,8,384]{2,1,0:T(8,128)}, f32[32,8,384]{2,1,0:T(8,128)S(1)}, u32[]{:S(2)}, u32[]{:S(2)}) %collective-permute-start.4) | collective-permute-done | bytes 393248 | tf_op jit(solution)/shard_map/ppermute | solution.py:917
  96.5 8.4 %collective-permute-done.5.corner_ref = f32[32,8,384]{2,1,0:T(8,128)S(1)} collective-permute-done((f32[32,8,384]{2,1,0:T(8,128)}, f32[32,8,384]{2,1,0:T(8,128)S(1)}, u32[]{:S(2)}, u32[]{:S(2)}) %collective-permute-start.5) | collective-permute-done | bytes 393248 | tf_op jit(solution)/shard_map/ppermute | solution.py:917
  104.9 0.9 broadcast_in_dim.26
  105.8 4.0 %all-to-all-start.2 = ((f32[32,32,128]{2,1,0:T(8,128)}), f32[32,32,128]{2,1,0:T(8,128)S(1)}, u32[]{:S(2)}, u32[]{:S(2)}) async-start(f32[32,32,128]{2,1,0:T(8,128)} %broadcast_in_dim.26), calls=%async_computation.2 | async-start | bytes 1048576 | tf_op jit(solution)/shard_map/all_to_all | solution.py:921
  109.8 1.3 slice_bitcast_fusion
  111.1 4.4 %shard_map.336 = f32[32,16,768]{2,1,0:T(8,128)} custom-call(f32[32,16,768]{2,1,0:T(8,128)} %x_ref.3, f32[32,12,384]{2,1,0:T(8,128)} %get-tuple-element.81.keep_ref, f32[32,24,384]{2,1,0:T(8,128)} %copy-done, f32[32,8,384]{2,1,0:T(8,128)} %copy-done.2, f32[32,8,384]{2,1,0:T(8,128)} %copy-done.3, f32[8,128]{1,0:T(8,128)} %get-tuple-element.82.norm_ref, ...), custom_call_target="tpu_custom_call" | custom-call | tf_op jit(solution)/shard_map/pallas_call | solution.py:826
  115.5 3.8 %shard_map.335 = f32[32,16,768]{2,1,0:T(8,128)} custom-call(f32[32,12,384]{2,1,0:T(8,128)} %get-tuple-element.73.keep_ref, f32[32,24,384]{2,1,0:T(8,128)} %copy-done, f32[32,8,384]{2,1,0:T(8,128)} %copy-done.2, f32[32,8,384]{2,1,0:T(8,128)} %copy-done.3), custom_call_target="tpu_custom_call" | custom-call | tf_op jit(solution)/shard_map/pallas_call | solution.py:814
  119.4 4.8 %all-to-all-done.2.all_ref = f32[32,32,128]{2,1,0:T(8,128)S(1)} async-done(((f32[32,32,128]{2,1,0:T(8,128)}), f32[32,32,128]{2,1,0:T(8,128)S(1)}, u32[]{:S(2)}, u32[]{:S(2)}) %all-to-all-start.2) | async-done | bytes 524320 | tf_op jit(solution)/shard_map/all_to_all | solution.py:921
  124.1 0.8 copy-done.1
  125.0 1.9 %shard_map.337 = (f32[96,288]{1,0:T(8,128)}, f32[2,96]{1,0:T(2,128)}, f32[1,3]{1,0:T(1,128)}, f32[2,512]{1,0:T(2,128)}, f32[1,512]{1,0:T(1,128)}, /*index=5*/f32...) custom-call(f32[32,32,128]{2,1,0:T(8,128)} %copy-done.1), custom_call_target="tpu_custom_call" | custom-call | tf_op jit(solution)/shard_map/pallas_call | solution.py:900
  126.9 1.3 reduce
  (51 shorter events, 5.2 us)
Async XLA Ops:
  0.7 15.5 %copy-start.10 = (f32[2,4,96]{2,1,0:T(4,128)S(1)}, f32[2,4,96]{2,1,0:T(4,128)}, u32[]{:S(2)}) copy-start(f32[2,4,96]{2,1,0:T(4,128)} %param.38) | copy-start | bytes 9220
  0.7 15.5 %copy-start.15 = (f32[96]{0:T(128)S(1)}, f32[96]{0:T(128)}, u32[]{:S(2)}) copy-start(f32[96]{0:T(128)} %param.37) | copy-start | bytes 1156
  0.7 15.5 %copy-start.16 = (f32[96]{0:T(128)S(1)}, f32[96]{0:T(128)}, u32[]{:S(2)}) copy-start(f32[96]{0:T(128)} %param.33) | copy-start | bytes 1156
  0.7 15.5 %copy-start.14 = (f32[2,96]{1,0:T(2,128)S(1)}, f32[2,96]{1,0:T(2,128)}, u32[]{:S(2)}) copy-start(f32[2,96]{1,0:T(2,128)} %param.27) | copy-start | bytes 2308
  0.7 16.1 %copy-start.12 = (f32[384]{0:T(512)S(1)}, f32[384]{0:T(512)}, u32[]{:S(2)}) copy-start(f32[384]{0:T(512)} %param.35) | copy-start | bytes 4612
  0.7 17.5 %copy-start.9 = (f32[512,3]{0,1:T(4,128)S(1)}, f32[512,3]{0,1:T(4,128)}, u32[]{:S(2)}) copy-start(f32[512,3]{0,1:T(4,128)} %param.31) | copy-start | bytes 18436
  0.7 17.4 %copy-start.13 = (f32[512]{0:T(512)S(1)}, f32[512]{0:T(512)}, u32[]{:S(2)}) copy-start(f32[512]{0:T(512)} %param.30) | copy-start | bytes 6148
  0.7 17.4 %copy-start.11 = (f32[2,512]{1,0:T(2,128)S(1)}, f32[2,512]{1,0:T(2,128)}, u32[]{:S(2)}) copy-start(f32[2,512]{1,0:T(2,128)} %param.29) | copy-start | bytes 12292
  0.7 22.6 %copy-start.17 = (f32[96]{0:T(128)S(1)}, f32[96]{0:T(128)}, u32[]{:S(2)}) copy-start(f32[96]{0:T(128)} %param.25) | copy-start | bytes 1156
  0.7 22.6 %copy-start.18 = (f32[96]{0:T(128)S(1)}, f32[96]{0:T(128)}, u32[]{:S(2)}) copy-start(f32[96]{0:T(128)} %param.24) | copy-start | bytes 1156
  5.2 27.1 %collective-permute-start = (f32[32,24,384]{2,1,0:T(8,128)}, f32[32,24,384]{2,1,0:T(8,128)S(1)}, u32[]{:S(2)}, u32[]{:S(2)}) collective-permute-start(f32[32,24,384]{2,1,0:T(8,128)} %get-tuple-element.57), channel_id=1, source_target_pairs={{4,0},{8,4},{12,8},{0,12},{20,16},{24,20},{28,24},{16,28},{5,1},{9... | collective-permute-start | bytes 3538952 | tf_op jit(solution)/shard_map/ppermute | solution.py:917
  7.6 16.3 %all-to-all-start = ((f32[32,1,256]{2,1,0:T(1,128)}), f32[32,1,256]{2,1,0:T(1,128)S(1)}, u32[]{:S(2)}, u32[]{:S(2)}) async-start(f32[32,1,256]{2,1,0:T(1,128)} %get-tuple-element.60), calls=%async_computation | async-start | bytes 65536 | tf_op jit(solution)/shard_map/all_to_all | solution.py:921
  12.6 12.5 %collective-permute-start.1 = (f32[32,8,384]{2,1,0:T(8,128)}, f32[32,8,384]{2,1,0:T(8,128)S(1)}, u32[]{:S(2)}, u32[]{:S(2)}) collective-permute-start(f32[32,8,384]{2,1,0:T(8,128)} %get-tuple-element.58), channel_id=1, source_target_pairs={{16,0},{20,4},{24,8},{28,12},{0,16},{4,20},{8,24},{12,28},{17,1},{... | collective-permute-start | bytes 1179656 | tf_op jit(solution)/shard_map/ppermute | solution.py:917
  14.4 17.8 %collective-permute-start.2 = (f32[32,8,384]{2,1,0:T(8,128)}, f32[32,8,384]{2,1,0:T(8,128)S(1)}, u32[]{:S(2)}, u32[]{:S(2)}) collective-permute-start(f32[32,8,384]{2,1,0:T(8,128)} %get-tuple-element.59), channel_id=1, source_target_pairs={{20,0},{24,4},{28,8},{16,12},{4,16},{8,20},{12,24},{0,28},{21,1},{... | collective-permute-start | bytes 1179656 | tf_op jit(solution)/shard_map/ppermute | solution.py:917
  23.9 8.3 %copy-start.8 = (f32[32,1,256]{2,1,0:T(1,128)}, f32[32,1,256]{2,1,0:T(1,128)S(1)}, u32[]{:S(2)}) copy-start(f32[32,1,256]{2,1,0:T(1,128)S(1)} %all-to-all-done.stats_ref) | copy-start | bytes 98308
  25.1 7.2 %copy-start.5 = (f32[32,8,384]{2,1,0:T(8,128)}, f32[32,8,384]{2,1,0:T(8,128)S(1)}, u32[]{:S(2)}) copy-start(f32[32,8,384]{2,1,0:T(8,128)S(1)} %collective-permute-done.1.x_down) | copy-start | bytes 1179652
  73.2 31.7 %collective-permute-start.3 = (f32[32,24,384]{2,1,0:T(8,128)}, f32[32,24,384]{2,1,0:T(8,128)S(1)}, u32[]{:S(2)}, u32[]{:S(2)}) collective-permute-start(f32[32,24,384]{2,1,0:T(8,128)} %get-tuple-element.75), channel_id=1, source_target_pairs={{12,0},{0,4},{4,8},{8,12},{28,16},{16,20},{20,24},{24,28},{13,1},{... | collective-permute-start | bytes 3538952 | tf_op jit(solution)/shard_map/ppermute | solution.py:917
  74.8 19.6 %all-to-all-start.1 = ((f32[32,32,128]{2,1,0:T(8,128)}), f32[32,32,128]{2,1,0:T(8,128)S(1)}, u32[]{:S(2)}, u32[]{:S(2)}) async-start(f32[32,32,128]{2,1,0:T(8,128)} %get-tuple-element.74), calls=%async_computation.1 | async-start | bytes 1048576 | tf_op jit(solution)/shard_map/all_to_all | solution.py:921
  79.1 17.4 %collective-permute-start.4 = (f32[32,8,384]{2,1,0:T(8,128)}, f32[32,8,384]{2,1,0:T(8,128)S(1)}, u32[]{:S(2)}, u32[]{:S(2)}) collective-permute-start(f32[32,8,384]{2,1,0:T(8,128)} %get-tuple-element.76), channel_id=1, source_target_pairs={{16,0},{20,4},{24,8},{28,12},{0,16},{4,20},{8,24},{12,28},{17,1},{... | collective-permute-start | bytes 1179656 | tf_op jit(solution)/shard_map/ppermute | solution.py:917
  80.9 23.9 %collective-permute-start.5 = (f32[32,8,384]{2,1,0:T(8,128)}, f32[32,8,384]{2,1,0:T(8,128)S(1)}, u32[]{:S(2)}, u32[]{:S(2)}) collective-permute-start(f32[32,8,384]{2,1,0:T(8,128)} %get-tuple-element.77), channel_id=1, source_target_pairs={{28,0},{16,4},{20,8},{24,12},{12,16},{0,20},{4,24},{8,28},{29,1},{... | collective-permute-start | bytes 1179656 | tf_op jit(solution)/shard_map/ppermute | solution.py:917
  94.4 16.7 %copy-start.7 = (f32[32,128]{1,0:T(8,128)}, f32[32,128]{1,0:T(8,128)S(1)}, u32[]{:S(2)}) copy-start(f32[32,128]{1,0:T(8,128)S(1)} %reduce_sum.9.sums_ref) | copy-start | bytes 49156
  96.5 14.6 %copy-start.2 = (f32[32,8,384]{2,1,0:T(8,128)}, f32[32,8,384]{2,1,0:T(8,128)S(1)}, u32[]{:S(2)}) copy-start(f32[32,8,384]{2,1,0:T(8,128)S(1)} %collective-permute-done.4.down_ref) | copy-start | bytes 1179652
  104.9 6.2 %copy-start.3 = (f32[32,8,384]{2,1,0:T(8,128)}, f32[32,8,384]{2,1,0:T(8,128)S(1)}, u32[]{:S(2)}) copy-start(f32[32,8,384]{2,1,0:T(8,128)S(1)} %collective-permute-done.5.corner_ref) | copy-start | bytes 1179652
  105.8 18.3 %all-to-all-start.2 = ((f32[32,32,128]{2,1,0:T(8,128)}), f32[32,32,128]{2,1,0:T(8,128)S(1)}, u32[]{:S(2)}, u32[]{:S(2)}) async-start(f32[32,32,128]{2,1,0:T(8,128)} %broadcast_in_dim.26), calls=%async_computation.2 | async-start | bytes 1048576 | tf_op jit(solution)/shard_map/all_to_all | solution.py:921
  (4 other events, 8.9 us)

commit v3 on v2

v3 whole, which is shorter than its diff:
```python
from functools import partial

import jax
import jax.numpy as jnp
import numpy as np
from jax import lax
from jax.experimental import pallas as pl
from jax.experimental.pallas import tpu as pltpu
from jax.sharding import PartitionSpec as P

HEADS = 3
HEAD_DIM = 32
WIDTH = 96
HIDDEN = 384
WINDOW = 8
SHIFT = 4
LEAD_STEPS = 14
PLACES = WINDOW * WINDOW
SPAN = 2 * WINDOW - 1
PAIR = 2 * PLACES
LANES = 128
OFFSETS = 256
PAYLOAD = 903
PARTS = 2

masked_score = -1000000000.0
norm_eps = 1e-05
unit_eps = 1e-06
momentum = 0.1
axes_all = ("ty", "tx", "items")

f32 = jnp.float32
bf16 = jnp.bfloat16

in_order = pltpu.CompilerParams(
    dimension_semantics=("arbitrary",), vmem_limit_bytes=60 * 1024 * 1024
)


def about(microseconds):
    return pl.CostEstimate(flops=microseconds * 10**9, bytes_accessed=10**6, transcendentals=0)


def block_of(items, most=8):
    return max(n for n in range(1, most + 1) if items % n == 0)


def whole(a):
    return pl.BlockSpec(a.shape, lambda i: (0,) * len(a.shape))


def dot(a, b):
    return lax.dot_general(a, b, (((1,), (0,)), ((), ())), preferred_element_type=f32)


def dot_rows(a, b):
    return lax.dot_general(a, b, (((1,), (1,)), ((), ())), preferred_element_type=f32)


def split(x):
    hi = x.astype(bf16)
    return hi, (x - hi.astype(f32)).astype(bf16)


def normal_parts(u):
    phi = 0.5 + 0.5 * lax.erf(u * 0.7071067811865476)
    return phi, (u * 0.3989422804014327) * jnp.exp(-0.5 * (u * u))


def pack_kernel(items, part_steps, x_ref, ct_ref, ct_top_ref, stats_ref, *refs):
    step = pl.program_id(0)
    step_items, rows, flat = x_ref.shape
    cols = flat // WIDTH
    half = flat // 2

    sums_ref = refs[-1]

    def send(right_ref, down_ref, corner_ref):
        for part, ref in enumerate((x_ref, ct_ref)):
            right_ref[:, 12 * part : 12 * part + 12, :] = ref[:, SHIFT:, :half]
            corner_ref[:, 4 * part : 4 * part + 4, :] = ref[:, :SHIFT, :half]
        down_ref[:, 0:4, :] = x_ref[:, :SHIFT, half:]
        down_ref[:, 4:8, :] = ct_top_ref[:, :SHIFT, :]

    for n in range(PARTS):
        pl.when(step // part_steps == n)(partial(send, *refs[3 * n : 3 * n + 3]))

    def fold(v):
        total = v[:, :WIDTH]
        for j in range(1, cols):
            total = total + v[:, j * WIDTH : (j + 1) * WIDTH]
        return jnp.sum(total, 0, keepdims=True)

    def total(fn):
        acc = jnp.zeros((8, flat), f32)
        for i in range(step_items):
            acc = acc + fn(x_ref[i, 0:8, :]) + fn(x_ref[i, 8:16, :])
        return acc

    @pl.when(step == 0)
    def _():
        pivot = fold(total(lambda v: v)) * (1.0 / (step_items * rows * cols))
        sums_ref[0] = jnp.broadcast_to(jnp.concatenate([pivot] * cols, 1), (8, flat))
        sums_ref[1] = jnp.zeros((8, flat), f32)
        sums_ref[2] = jnp.zeros((8, flat), f32)

    pivot = sums_ref[0]
    sums_ref[1] += total(lambda v: v - pivot)
    sums_ref[2] += total(lambda v: (v - pivot) * (v - pivot))

    @pl.when(step == pl.num_programs(0) - 1)
    def _():
        count = items * rows * cols
        offset = fold(sums_ref[1]) * (1.0 / count)
        square = fold(sums_ref[2]) - count * offset * offset
        pad = jnp.zeros((1, LANES - WIDTH), f32)
        row = jnp.concatenate([sums_ref[0, 0:1, :WIDTH] + offset, pad, square, pad], 1)
        stats_ref[...] = jnp.broadcast_to(row[None], stats_ref.shape)


def spread_kernel(row_ref, out_ref):
    out_ref[...] = jnp.broadcast_to(row_ref[0:1][None], out_ref.shape)


def pack(x, ct, devices):
    items, rows, flat = x.shape
    half = flat // 2
    part_items = items // PARTS
    step_items = block_of(part_items, 16)
    part_steps = part_items // step_items

    def spec(n, width):
        return pl.BlockSpec((step_items, n, width), lambda i: (i, 0, 0))

    def of_part(n, count):
        return pl.BlockSpec(
            (step_items, count, half),
            lambda i: (jnp.clip(i - n * part_steps, 0, part_steps - 1), 0, 0),
        )

    stats = jax.ShapeDtypeStruct((devices, 1, 2 * LANES), f32)
    counts = (24, 8, 8)
    outs = pl.pallas_call(
        partial(pack_kernel, items, part_steps),
        grid=(items // step_items,),
        in_specs=[
            spec(rows, flat),
            spec(rows, half),
            pl.BlockSpec((step_items, 8, half), lambda i: (i, 0, 1)),
        ],
        out_specs=[whole(stats)] + [of_part(n, c) for n in range(PARTS) for c in counts],
        out_shape=[stats]
        + [jax.ShapeDtypeStruct((part_items, c, half), f32) for _ in range(PARTS) for c in counts],
        scratch_shapes=[pltpu.VMEM((3, 8, flat), f32)],
        cost_estimate=about(4),
        compiler_params=in_order,
    )(x, ct, ct)
    stats = outs[0]
    return stats, [outs[1 + 3 * n : 4 + 3 * n] for n in range(PARTS)]


def offset_constants():
    coords = np.zeros((8, OFFSETS), np.float32)
    o = np.arange(SPAN * SPAN)
    for k, along in enumerate((o // SPAN - (WINDOW - 1), o % SPAN - (WINDOW - 1))):
        u = along.astype(np.float32) * np.float32(8.0 / (WINDOW - 1))
        coords[k, : SPAN * SPAN] = np.sign(u) * np.log2(np.abs(u) + np.float32(1.0)) / np.float32(3.0)
    coords[2, : SPAN * SPAN] = 1.0
    key_row, lane = np.divmod(np.arange(WINDOW * LANES), LANES)
    across, row = np.divmod(lane, WINDOW)
    target = (row - key_row + WINDOW - 1) * SPAN + across
    target = np.where(across < SPAN, target, -1).astype(np.int32)
    return jnp.asarray(coords), jnp.asarray(np.broadcast_to(target, (8, target.size)).copy())


def exact(a, b):
    return jnp.dot(a, b, preferred_element_type=f32, precision=lax.Precision.HIGHEST)


def net_columns(net):
    columns = jnp.concatenate([net, jnp.zeros((LANES - 8, net.shape[1]), f32)], 0).T

    def column(i):
        return jnp.broadcast_to(columns[:, i : i + 1], (net.shape[1], OFFSETS))

    return column


def bias_net(net, coords):
    column = net_columns(net)
    u = column(0) * coords[0:1] + column(1) * coords[1:2] + column(2)
    phi, bell = normal_parts(u)
    return u * phi, phi + bell


def head_rows(net):
    return jnp.concatenate([net[3:6], jnp.zeros((5, net.shape[1]), f32)], 0)


def one_hot(target):
    rows = lax.broadcasted_iota(jnp.int32, (OFFSETS, WINDOW * LANES), 0)
    return jnp.where(rows == target[0:1], 1.0, 0.0).astype(bf16)


def three_parts(v):
    hi, lo = split(v)
    rest = v - hi.astype(f32) - lo.astype(f32)
    return jnp.concatenate([hi.astype(f32), lo.astype(f32), rest], 0).astype(bf16)


def add_parts(v):
    return v[:8] + v[8:16] + v[16:]


def prepare_kernel(
    log_scale_ref,
    qv_ref,
    proj_ref,
    down_ref,
    norms_ref,
    up_ref,
    mean_ref,
    var_ref,
    w1_ref,
    b1_ref,
    w2_ref,
    coords_ref,
    target_ref,
    scale_ref,
    bias_ref,
    vec_ref,
    net_ref,
    gate_ref,
):
    def row(ref):
        return ref[...].reshape(1, ref.shape[0])

    vec_ref[...] = jnp.zeros_like(vec_ref)
    vec_ref[0:2, :WIDTH] = qv_ref[...]
    vec_ref[2:3, :WIDTH] = row(proj_ref)
    vec_ref[3:4, :WIDTH] = row(down_ref)
    vec_ref[4:8, :WIDTH] = norms_ref[0]
    vec_ref[8:12, :WIDTH] = norms_ref[1]
    vec_ref[12:13, :HIDDEN] = row(up_ref)
    vec_ref[13:14, :WIDTH] = row(mean_ref)
    vec_ref[14:15, :WIDTH] = row(var_ref)
    units = w1_ref.shape[1]
    net = jnp.concatenate([w1_ref[...], row(b1_ref), w2_ref[...], jnp.zeros((2, units), f32)], 0)
    vec_ref[16:24, :] = net
    lanes = lax.broadcasted_iota(jnp.int32, (1, LANES), 1)
    hidden, slope = bias_net(net, coords_ref[...])
    gate = 1.0 / (1.0 + jnp.exp(-exact(head_rows(net), hidden)))
    net_ref[0] = hidden
    net_ref[1] = slope
    gate_ref[...] = 16.0 * gate * (1.0 - gate)
    spots = one_hot(target_ref[...])
    tiles = add_parts(dot(three_parts(16.0 * gate), spots))
    scale_ref[...] = jnp.zeros_like(scale_ref)
    for h in range(HEADS):
        scale = jnp.exp(jnp.full((1, LANES), log_scale_ref[h], f32))
        scale_ref[h : h + 1, :] = scale
        tile = jnp.concatenate(
            [tiles[h : h + 1, r * LANES : (r + 1) * LANES] for r in range(WINDOW)], 0
        )
        columns = []
        for j in range(WINDOW):
            turned = pltpu.roll(tile, (72 + 8 * j) % LANES, 1)
            columns.append(jnp.where(lanes < PLACES, turned, pltpu.roll(turned, PLACES, 1)))
        bias_ref[h] = jnp.concatenate(columns, 0) - (scale + 16.0)


def prepare(log_scale, vectors, coords, target):
    units = vectors[-1].shape[1]
    shapes = [
        (8, LANES),
        (HEADS, PLACES, LANES),
        (24, units),
        (2, units, OFFSETS),
        (8, OFFSETS),
    ]
    shapes = [jax.ShapeDtypeStruct(a, f32) for a in shapes]
    inputs = (*vectors, coords, target)
    return pl.pallas_call(
        prepare_kernel,
        grid=(1,),
        in_specs=[pl.BlockSpec(memory_space=pltpu.SMEM)] + [whole(a) for a in inputs],
        out_specs=[whole(a) for a in shapes],
        out_shape=shapes,
        cost_estimate=about(0),
        compiler_params=in_order,
    )(log_scale, *inputs)


def packed(w):
    hi, lo = split(w)
    return jnp.concatenate([hi, lo, hi], 1)


def stack_rows(hi, lo):
    return jnp.concatenate([hi, lo], 0)


def block_kernel(
    step_items,
    first_item,
    token_count,
    is_first,
    is_last,
    flags_ref,
    lead_ref,
    x_own,
    x_right,
    x_down,
    x_corner,
    ct_own,
    stats_ref,
    w_qkv_ref,
    w_out_ref,
    w_up_ref,
    w_down_ref,
    scale_ref,
    base_ref,
    vec_ref,
    *refs,
):
    step = pl.program_id(0)
    if is_last:
        (net_ref, gate_ref, coords_ref, target_ref), refs = refs[:4], refs[4:]
    refs, scratch = refs[:-11], refs[-11:]
    qkv_f, out_f, up_f, down_f, down_b, up_b, out_b, qkv_b, cols_ref, up_cols_ref, bias_ref = scratch
    count = len(totals_shapes)
    so_far, refs = (refs[:0], refs) if is_first else (refs[:count], refs[count:])
    out_keep, dn_keep, send_right, send_down, send_corner = refs[:5]
    refs = refs[5:]
    if is_last:
        grads_ref, norm_ref, affine_ref, flat_ref = refs[:4]
        refs = refs[4:]
    else:
        affine_ref, refs = refs[-1], refs[:-1]
    g_qkv_ref, g_out_ref, g_up_ref, g_down_ref, sums_ref, dpos_ref, dcos_ref = refs

    @pl.when(step == 0)
    def _():
        every = stats_ref[...]
        devices = every.shape[0]
        means, squares = every[:, 0, :LANES], every[:, 0, LANES:]
        mean = jnp.sum(means, 0, keepdims=True) * (1.0 / devices)
        apart = means - mean
        var = (
            jnp.sum(squares, 0, keepdims=True) * (1.0 / token_count)
            + jnp.sum(apart * apart, 0, keepdims=True) * (1.0 / devices)
        )
        inv_std = lax.rsqrt(var + norm_eps)
        affine_ref[0] = jnp.broadcast_to(mean, (LANES, LANES)).T[:WIDTH]
        affine_ref[1] = jnp.broadcast_to(inv_std, (LANES, LANES)).T[:WIDTH]
        if is_last:
            pad = jnp.zeros((2, LANES - WIDTH), f32)
            running = jnp.concatenate([vec_ref[13:15, :WIDTH], pad], 1)
            norm_ref[0:1] = mean
            norm_ref[1:2] = inv_std
            norm_ref[2:3] = (1.0 - momentum) * running[0:1] + momentum * mean
            norm_ref[3:4] = (1.0 - momentum) * running[1:2] + momentum * var * (
                token_count / (token_count - 1.0)
            )
            norm_ref[4:8] = jnp.zeros((4, LANES), f32)
        for n, ref in enumerate(refs):
            ref[...] = jnp.zeros_like(ref) if is_first else so_far[n][...]
        qkv_f[...] = packed(w_qkv_ref[...].T)
        qkv_b[...] = packed(w_qkv_ref[...])
        out_f[...] = packed(w_out_ref[...].T)
        out_b[...] = packed(w_out_ref[...])
        up_f[...] = packed(w_up_ref[...].T)
        up_b[...] = packed(w_up_ref[...])
        down_b[...] = packed(w_down_ref[...].T)
        down_f[...] = packed(w_down_ref[...])
        for i in range(cols_ref.shape[0]):
            cols_ref[i] = jnp.broadcast_to(vec_ref[i : i + 1, :WIDTH], (LANES, WIDTH)).T
        up_cols_ref[...] = jnp.broadcast_to(vec_ref[12:13, :HIDDEN], (LANES, HIDDEN)).T
        place = lax.broadcasted_iota(jnp.int32, (PLACES, LANES), 0)
        other = lax.broadcasted_iota(jnp.int32, (PLACES, LANES), 1) % PLACES
        apart_r = (place % WINDOW < SHIFT) != (other % WINDOW < SHIFT)
        apart_c = (place // WINDOW < SHIFT) != (other // WINDOW < SHIFT)
        for h in range(HEADS):
            bias = base_ref[h]
            bias_ref[0, h] = bias
            bias_ref[1, h] = jnp.where(apart_c, masked_score, bias)
            bias_ref[2, h] = jnp.where(apart_r, masked_score, bias)
            bias_ref[3, h] = jnp.where(apart_r | apart_c, masked_score, bias)

    first_half = lax.broadcasted_iota(jnp.int32, (1, PAIR), 1) < PLACES

    def product(weight, x_hi, x_lo):
        return dot(weight[...], jnp.concatenate([x_hi, x_hi, x_lo], 0))

    def halves(v):
        m = v.shape[0] // 2
        return jnp.where(first_half, v[:m], v[m:])

    def col(i):
        return cols_ref[i]

    def per_item(fn):
        return jnp.concatenate([fn(m) for m in range(step_items)], 1)

    def spread_cols(i):
        c = col(i)
        return jnp.concatenate([c] * step_items, 1)

    def gather(own, part, m):
        right, down = 12 * part, 4 * part
        top_l = own[m, SHIFT : SHIFT + WINDOW, :]
        top_r = x_right[m, right : right + WINDOW, :]
        low_l = jnp.concatenate([own[m, SHIFT + WINDOW :, :], x_down[m, down : down + SHIFT, :]], 0)
        low_r = jnp.concatenate(
            [x_right[m, right + WINDOW : right + 12, :], x_corner[m, down : down + SHIFT, :]], 0
        )
        tiles = [
            side[:, j * WIDTH : (j + 1) * WIDTH]
            for side in (top_l, top_r, low_l, low_r)
            for j in range(4)
        ]
        return jnp.concatenate(tiles, 0).T

    def scatter(value, keep, part, m):
        rows = value.T
        sides = [
            jnp.concatenate([rows[(4 * s + j) * 8 : (4 * s + j + 1) * 8] for j in range(4)], 1)
            for s in range(4)
        ]
        right, down = 12 * part, 4 * part
        keep[m, 0:WINDOW, :] = sides[0]
        keep[m, WINDOW:, :] = sides[2][:SHIFT]
        send_right[m, right : right + WINDOW, :] = sides[1]
        send_right[m, right + WINDOW : right + 12, :] = sides[3][:SHIFT]
        send_down[m, down : down + SHIFT, :] = sides[2][SHIFT:]
        send_corner[m, down : down + SHIFT, :] = sides[3][SHIFT:]

    def mean_rows(v):
        return jnp.sum(v, 0, keepdims=True) * (1.0 / WIDTH)

    def layer_norm(v):
        centred = v - mean_rows(v)
        rstd = lax.rsqrt(mean_rows(centred * centred) + norm_eps)
        return centred * rstd, rstd

    items = [first_item + step * step_items + m for m in range(step_items)]
    leads = [(lead_ref[i] + 1).astype(f32) * (1.0 / LEAD_STEPS) for i in items]
    raw = per_item(lambda m: gather(x_own, 0, m))
    mean = jnp.concatenate([affine_ref[0]] * step_items, 1)
    inv_std = jnp.concatenate([affine_ref[1]] * step_items, 1)
    normed = (raw - mean) * inv_std
    n_hi, n_lo = split(normed)

    joined = product(qkv_f, n_hi, n_lo)
    query = joined[:WIDTH] + spread_cols(0)
    key = joined[WIDTH : 2 * WIDTH]
    value = joined[2 * WIDTH :] + spread_cols(1)

    def unit(v):
        rows, inverses = [], []
        for h in range(HEADS):
            part = v[h * HEAD_DIM : (h + 1) * HEAD_DIM]
            inverse = lax.rsqrt(jnp.sum(part * part, 0, keepdims=True) + unit_eps)
            rows.append(part * inverse)
            inverses.append(inverse)
        return rows, inverses

    q_rows, q_inv = unit(query)
    k_rows, k_inv = unit(key)
    v_rows = [value[h * HEAD_DIM : (h + 1) * HEAD_DIM] for h in range(HEADS)]

    def of_item(v, m):
        return v[:, m * PAIR : (m + 1) * PAIR]

    def three(a_hi, a_lo, b_hi, b_lo):
        left = jnp.concatenate([a_hi, a_lo, a_hi], 0)
        right = jnp.concatenate([b_hi, b_hi, b_lo], 0)
        return halves(dot(left.T, right))

    def apart(x):
        zero = jnp.zeros_like(x)
        return jnp.concatenate(
            [jnp.where(first_half, x, zero), jnp.where(first_half, zero, x)], 0
        )

    def two_rows(v_hi, v_lo):
        return jnp.concatenate(
            [
                jnp.concatenate([v_hi, v_hi], 1),
                jnp.concatenate([v_lo, jnp.zeros_like(v_lo)], 1),
            ],
            0,
        )

    def over_keys(v_hi, v_lo, e_hi, e_lo):
        r = dot(two_rows(v_hi, v_lo), stack_rows(apart(e_hi), apart(e_lo)))
        return r[:HEAD_DIM] + r[HEAD_DIM:]

    def over_queries(v_hi, v_lo, e_hi, e_lo):
        weights = jnp.concatenate([e_hi, e_lo], 1)
        r = dot_rows(two_rows(apart(v_hi), apart(v_lo)), stack_rows(weights, weights))
        return halves(r[:PLACES] + r[PLACES:])

    pairs = [(m, h) for m in range(step_items) for h in range(HEADS)]
    q_parts = [split(of_item(q_rows[h], m)) for m, h in pairs]
    k_parts = [split(of_item(k_rows[h], m)) for m, h in pairs]
    v_parts = [split(of_item(v_rows[h], m)) for m, h in pairs]
    cosines = [three(*k, *q) for k, q in zip(k_parts, q_parts)]
    expos, inverses = [], []
    for (m, h), cosine in zip(pairs, cosines):
        flag0, flag1 = flags_ref[0, items[m]], flags_ref[1, items[m]]
        offset = jnp.where(first_half, bias_ref[flag0, h], bias_ref[flag1, h])
        expo = jnp.exp(cosine * scale_ref[h : h + 1, :] + offset)
        expos.append(expo)
        inverses.append(1.0 / jnp.sum(expo, 0, keepdims=True))
    e_parts = [split(e) for e in expos]
    mixes = [
        over_keys(*v, *e) * inverse for v, e, inverse in zip(v_parts, e_parts, inverses)
    ]
    mixed = jnp.concatenate(
        [jnp.concatenate(mixes[HEADS * m : HEADS * (m + 1)], 0) for m in range(step_items)], 1
    )

    o_hi, o_lo = split(mixed)
    attn_hat, attn_rstd = layer_norm(product(out_f, o_hi, o_lo) + spread_cols(2))

    def gain(base):
        return per_item(lambda m: 1.0 + col(base) + leads[m] * col(base + 1))

    def shift(base):
        return per_item(lambda m: col(base + 2) + leads[m] * col(base + 3))

    gain0 = gain(4)
    first = normed + attn_hat * gain0 + shift(4)
    f_hi, f_lo = split(first)

    up_bias = jnp.concatenate([up_cols_ref[...]] * step_items, 1)
    u = product(up_f, f_hi, f_lo) + up_bias
    phi, bell = normal_parts(u)
    hidden = u * phi
    slope = phi + bell
    h_hi, h_lo = split(hidden)
    branch = product(down_f, h_hi, h_lo) + spread_cols(3)
    hat, rstd = layer_norm(branch)
    gain1 = gain(8)
    out = first + hat * gain1 + shift(8)
    for m in range(step_items):
        scatter(of_item(out, m), out_keep, 0, m)

    def norm_back(g, hat, rstd, gain, base):
        weighted = g * hat
        for m in range(step_items):
            a, b = of_item(weighted, m), of_item(g, m)
            sums_ref[base] += a
            sums_ref[base + 1] += leads[m] * a
            sums_ref[base + 2] += b
            sums_ref[base + 3] += leads[m] * b
        e = g * gain
        return (e - mean_rows(e) - hat * mean_rows(e * hat)) * rstd

    def add_items(v):
        total = of_item(v, 0)
        for m in range(1, step_items):
            total = total + of_item(v, m)
        return total

    ones_rows = jnp.where(
        lax.broadcasted_iota(jnp.int32, (LANES - WIDTH, step_items * PAIR), 0) == 0, 1.0, 0.0
    ).astype(bf16)
    zero_rows = jnp.zeros((LANES - WIDTH, step_items * PAIR), bf16)

    def outer(a_hi, a_lo, b_hi, b_lo):
        right = jnp.concatenate([b_hi, ones_rows, b_lo, zero_rows], 0)
        r = dot_rows(stack_rows(a_hi, a_lo), right)
        m = a_hi.shape[0]
        return (r[:m, :LANES] + r[m:, :LANES]) + r[:m, LANES:]

    cot = per_item(lambda m: gather(ct_own, 1, m))
    d_branch = norm_back(cot, hat, rstd, gain1, 4)
    sums_ref[8] += add_items(d_branch)
    z_hi, z_lo = split(d_branch)
    g_down_ref[...] += outer(h_hi, h_lo, z_hi, z_lo)
    d_pre = product(down_b, z_hi, z_lo) * slope
    p_hi, p_lo = split(d_pre)
    g_up_ref[...] += outer(p_hi, p_lo, f_hi, f_lo)
    d_first = cot + product(up_b, p_hi, p_lo)
    d_attn = norm_back(d_first, attn_hat, attn_rstd, gain0, 0)
    a_hi, a_lo = split(d_attn)
    g_out_ref[...] += outer(a_hi, a_lo, o_hi, o_lo)
    d_mixed = product(out_b, a_hi, a_lo)

    d_outs = [
        of_item(d_mixed, m)[h * HEAD_DIM : (h + 1) * HEAD_DIM] * inverse
        for (m, h), inverse in zip(pairs, inverses)
    ]
    d_parts = [split(d) for d in d_outs]
    d_probs = [three(*v, *d) for v, d in zip(v_parts, d_parts)]
    s_parts = []
    for n, (m, h) in enumerate(pairs):
        delta = jnp.sum(d_outs[n] * mixes[n], 0, keepdims=True)
        d_scores = expos[n] * (d_probs[n] - delta)
        dpos_ref[h] += d_scores
        folded = d_scores * cosines[n]
        total = folded[0:8]
        for i in range(1, PLACES // 8):
            total = total + folded[8 * i : 8 * i + 8]
        dcos_ref[h] += total
        s_parts.append(split(d_scores))
    dv_rows = [over_queries(*d, *e) for d, e in zip(d_parts, e_parts)]
    dk_rows = [over_queries(*q, *d) for q, d in zip(q_parts, s_parts)]
    dq_rows = [over_keys(*k, *d) for k, d in zip(k_parts, s_parts)]

    def unit_back(grads, rows, inverse):
        out = []
        for n, (m, h) in enumerate(pairs):
            d = grads[n] * scale_ref[h : h + 1, :]
            row = of_item(rows[h], m)
            d = d - row * jnp.sum(row * d, 0, keepdims=True)
            out.append(d * of_item(inverse[h], m))
        return out

    dq_rows = unit_back(dq_rows, q_rows, q_inv)
    dk_rows = unit_back(dk_rows, k_rows, k_inv)
    d_joined = jnp.concatenate(
        [
            jnp.concatenate(
                [d for rows in (dq_rows, dk_rows, dv_rows) for d in rows[HEADS * m : HEADS * (m + 1)]], 0
            )
            for m in range(step_items)
        ],
        1,
    )
    j_hi, j_lo = split(d_joined)
    g_qkv_ref[...] += outer(j_hi, j_lo, n_hi, n_lo)
    d_normed = d_first + product(qkv_b, j_hi, j_lo)
    sums_ref[9] += add_items(d_normed)
    sums_ref[10] += add_items(d_normed * normed)
    for m in range(step_items):
        scatter(of_item(d_normed, m), dn_keep, 1, m)

    def finish():
        def lane_sums(v):
            return jnp.sum(v.T, 0, keepdims=True)

        flat_ref[...] = jnp.zeros_like(flat_ref)
        g = g_qkv_ref[...].T
        flat_ref[0:96, :] = g[:WIDTH, :LANES]
        flat_ref[96:192, :] = g[:WIDTH, LANES : 2 * LANES]
        qv = g[WIDTH : WIDTH + 1]
        g_out = g_out_ref[...].T
        flat_ref[192:288, :] = jnp.concatenate([g_out[:WIDTH], g[:WIDTH, 2 * LANES :]], 1)
        g_up = g_up_ref[...].T
        g_down = g_down_ref[...].T
        for k in range(3):
            lanes = slice(k * LANES, (k + 1) * LANES)
            flat_ref[288 + 96 * k : 384 + 96 * k, :] = g_up[:WIDTH, lanes]
            flat_ref[576 + 96 * k : 672 + 96 * k, :] = g_down[:WIDTH, lanes]
            flat_ref[876 + k : 877 + k, :] = g_up[WIDTH : WIDTH + 1, lanes]
        totals = [lane_sums(sums_ref[i]) for i in range(11)]
        for i in range(8):
            flat_ref[864 + i : 865 + i, :WIDTH] = totals[i]
        flat_ref[872:873, :WIDTH] = totals[8]
        flat_ref[873:874, :WIDTH] = g_out[WIDTH : WIDTH + 1]
        flat_ref[874:875, :WIDTH] = qv[:, :WIDTH]
        flat_ref[875:876, :WIDTH] = qv[:, 2 * WIDTH :]
        lane = lax.broadcasted_iota(jnp.int32, (1, LANES), 1)
        scales = jnp.zeros((1, LANES), f32)
        for h in range(HEADS):
            total = jnp.sum(jnp.sum(dcos_ref[h], 0, keepdims=True), 1, keepdims=True)
            scales = jnp.where(lane == WIDTH + h, total * scale_ref[h : h + 1, :], scales)
        flat_ref[864:865, :] = flat_ref[864:865, :] + scales

        rows = []
        for h in range(HEADS):
            d = dpos_ref[h]
            d = jnp.where(first_half, d + pltpu.roll(d, PLACES, 1), 0.0)
            tile = jnp.zeros((WINDOW, LANES), f32)
            for j in range(WINDOW):
                tile = tile + pltpu.roll(d[8 * j : 8 * j + 8], 56 - 8 * j, 1)
            rows.append(jnp.concatenate([tile[r : r + 1] for r in range(WINDOW)], 1))
        rows.append(jnp.zeros((8 - HEADS, WINDOW * LANES), f32))
        found = dot_rows(three_parts(jnp.concatenate(rows, 0)), one_hot(target_ref[...]))
        d_table = add_parts(found)
        d_logit = d_table * gate_ref[...]

        def against(v, units):
            v_hi, v_lo = split(v)
            u_hi, u_lo = split(units)
            both = jnp.concatenate([v_hi.astype(f32), v_lo.astype(f32)], 0).astype(bf16)
            r = dot_rows(both, u_hi)
            return r[:8] + r[8:] + dot_rows(v_hi, u_lo)

        g_w2 = against(d_logit, net_ref[0])
        column = net_columns(vec_ref[16:24, :])
        d_hidden = sum(column(3 + h) * d_logit[h : h + 1] for h in range(HEADS))
        g_first = against(coords_ref[...], d_hidden * net_ref[1])
        for i, row in enumerate(
            [g_first[0:1], g_first[1:2], g_first[2:3], g_w2[0:1], g_w2[1:2], g_w2[2:3]]
        ):
            for k in range(4):
                at = 879 + 4 * i + k
                flat_ref[at : at + 1, :] = row[:, k * LANES : (k + 1) * LANES]

        slots, slot_rows, _ = grads_ref.shape
        share = slot_rows - 2
        for j in range(slots):
            grads_ref[j, 0:share, :] = flat_ref[share * j : share * (j + 1), :]
        for i in range(2):
            grads_ref[:, share + i : share + i + 1, :WIDTH] = jnp.broadcast_to(
                totals[9 + i][None], (slots, 1, WIDTH)
            )
            grads_ref[:, share + i : share + i + 1, WIDTH:] = jnp.zeros(
                (slots, 1, LANES - WIDTH), f32
            )

    if is_last:
        finish()


totals_shapes = [
    (3 * WIDTH, LANES),
    (WIDTH, LANES),
    (HIDDEN, LANES),
    (HIDDEN, LANES),
    (11, WIDTH, LANES),
    (HEADS, PLACES, LANES),
    (HEADS, 8, LANES),
]


def run_block(
    part,
    flags,
    lead,
    x,
    ct,
    halo,
    stats,
    weights,
    prepared,
    bias_net_parts,
    so_far,
    token_count,
):
    items, tile_rows, flat = x.shape
    half = flat // 2
    items = items // PARTS
    step_items = block_of(items, 16)
    steps = items // step_items
    is_first, is_last = part == 0, part == PARTS - 1

    def rows(n):
        return pl.BlockSpec((step_items, n, half), lambda i: (i, 0, 0))

    smem = pl.BlockSpec(memory_space=pltpu.SMEM)
    field = pl.BlockSpec((step_items, tile_rows, half), lambda i: (part * steps + i, 0, 1))
    out_rows = (12, 12, 24, 8, 8)
    slots = stats.shape[0]
    slot_rows = -(-PAYLOAD // slots)
    slot_rows = -(-(slot_rows + 2) // 8) * 8
    totals = [jax.ShapeDtypeStruct(s, f32) for s in totals_shapes]
    scratch = [pltpu.VMEM((2, WIDTH, LANES), f32)]
    if is_last:
        tail = [
            jax.ShapeDtypeStruct((slots, slot_rows, LANES), f32),
            jax.ShapeDtypeStruct((8, LANES), f32),
        ]
        scratch.append(pltpu.VMEM((slots * (slot_rows - 2), LANES), f32))
        scratch += [pltpu.VMEM(s, f32) for s in totals_shapes]
    else:
        tail = totals
    scratch += [
        pltpu.VMEM((3 * WIDTH, 3 * WIDTH), bf16),
        pltpu.VMEM((WIDTH, 3 * WIDTH), bf16),
        pltpu.VMEM((HIDDEN, 3 * WIDTH), bf16),
        pltpu.VMEM((WIDTH, 3 * HIDDEN), bf16),
        pltpu.VMEM((HIDDEN, 3 * WIDTH), bf16),
        pltpu.VMEM((WIDTH, 3 * HIDDEN), bf16),
        pltpu.VMEM((WIDTH, 3 * WIDTH), bf16),
        pltpu.VMEM((WIDTH, 9 * WIDTH), bf16),
        pltpu.VMEM((12, WIDTH, LANES), f32),
        pltpu.VMEM((HIDDEN, LANES), f32),
        pltpu.VMEM((4, HEADS, PLACES, LANES), f32),
    ]
    constants = (stats, *weights, *prepared, *(bias_net_parts if is_last else ()), *so_far)
    return pl.pallas_call(
        partial(block_kernel, step_items, part * items, float(token_count), is_first, is_last),
        grid=(steps,),
        in_specs=[smem, smem, field, rows(24), rows(8), rows(8), field]
        + [whole(a) for a in constants],
        out_specs=[rows(n) for n in out_rows] + [whole(a) for a in tail],
        out_shape=[jax.ShapeDtypeStruct((items, n, half), f32) for n in out_rows] + tail,
        scratch_shapes=scratch,
        cost_estimate=about(40),
        compiler_params=in_order,
    )(flags, lead, x, *halo, ct, *constants)


def place(ref_out, m, keep, right, down, corner, part, fn):
    half = keep.shape[2]
    at, low = 12 * part, 4 * part
    for rows, left, own in (
        (slice(0, SHIFT), corner[m, low : low + SHIFT, :], down[m, low : low + SHIFT, :]),
        (slice(SHIFT, 16), right[m, at : at + 12, :], keep[m]),
    ):
        for lanes, value in ((slice(0, half), left), (slice(half, 2 * half), own)):
            ref_out[m, rows, lanes] = fn(value, rows, lanes)


def final_kernel(token_count, part_steps, x_ref, norm_ref, sums_ref, *refs):
    cols = x_ref.shape[2] // WIDTH
    out_ref, grad_ref = refs[-2:]

    def wide(row):
        return jnp.concatenate([row[:, :WIDTH]] * cols, 1)

    mean, inv_std = norm_ref[0:1], norm_ref[1:2]
    at = sums_ref.shape[1] - 2
    mean_grad = sums_ref[0, at : at + 1] * (1.0 / token_count)
    mean_cross = sums_ref[0, at + 1 : at + 2] * (1.0 / token_count)
    factor, centre = wide(inv_std), wide(mean)
    offset, slope = wide(inv_std * mean_grad), wide(inv_std * inv_std * mean_cross)

    def work(out_keep, dn_keep, *halo):
        for m in range(x_ref.shape[0]):

            def grad(v, rows, lanes):
                x = x_ref[m, rows, lanes] - centre[:, lanes]
                return factor[:, lanes] * v - offset[:, lanes] - x * slope[:, lanes]

            place(out_ref, m, out_keep, *halo, 0, lambda v, rows, lanes: v)
            place(grad_ref, m, dn_keep, *halo, 1, grad)

    for n in range(PARTS):
        pl.when(pl.program_id(0) // part_steps == n)(partial(work, *refs[5 * n : 5 * n + 5]))


def finish_fields(x, parts, norm, sums, token_count):
    items, rows, flat = x.shape
    step_items = block_of(items // PARTS, 16)
    part_steps = items // PARTS // step_items

    def spec(part, n):
        return pl.BlockSpec(
            (step_items, n, flat // 2),
            lambda i: (jnp.clip(i - part * part_steps, 0, part_steps - 1), 0, 0),
        )

    field = pl.BlockSpec((step_items, rows, flat), lambda i: (i, 0, 0))
    return pl.pallas_call(
        partial(final_kernel, float(token_count), part_steps),
        grid=(items // step_items,),
        in_specs=[
            field,
            whole(norm),
            pl.BlockSpec((1,) + sums.shape[1:], lambda i: (0, 0, 0)),
        ]
        + [spec(part, n) for part in range(PARTS) for n in (12, 12, 24, 8, 8)],
        out_specs=[field] * 2,
        out_shape=[jax.ShapeDtypeStruct(x.shape, f32)] * 2,
        cost_estimate=about(60),
        compiler_params=in_order,
    )(x, norm, sums, *[a for part in parts for a in part])


def sum_slots_kernel(slots_ref, all_ref):
    total = slots_ref[0]
    for j in range(1, slots_ref.shape[0]):
        total = total + slots_ref[j]
    all_ref[...] = jnp.broadcast_to(total[None], all_ref.shape)


def sum_slots(slots):
    return pl.pallas_call(
        sum_slots_kernel,
        grid=(1,),
        in_specs=[whole(slots)],
        out_specs=whole(slots),
        out_shape=jax.ShapeDtypeStruct(slots.shape, f32),
        compiler_params=pltpu.CompilerParams(vmem_limit_bytes=16 * 1024 * 1024),
    )(slots)


def unpack_kernel(
    all_ref,
    qkv_ref,
    qv_ref,
    scale_ref,
    w1_ref,
    b1_ref,
    w2_ref,
    out_ref,
    b_out_ref,
    up_ref,
    b_up_ref,
    down_ref,
    b_down_ref,
    norm_ref,
    flat_ref,
):
    slots, slot_rows, _ = all_ref.shape
    share = slot_rows - 2
    for j in range(slots):
        flat_ref[share * j : share * (j + 1), :] = all_ref[j, 0:share, :]
    qkv_ref[:, 0:LANES] = flat_ref[0:96, :]
    qkv_ref[:, LANES : 2 * LANES] = flat_ref[96:192, :]
    qkv_ref[:, 2 * LANES :] = flat_ref[192:288, WIDTH:]
    out_ref[...] = flat_ref[192:288, :WIDTH]
    for k in range(3):
        lanes = slice(k * LANES, (k + 1) * LANES)
        up_ref[:, lanes] = flat_ref[288 + 96 * k : 384 + 96 * k, :]
        down_ref[:, lanes] = flat_ref[576 + 96 * k : 672 + 96 * k, :]
        b_up_ref[k : k + 1, :] = flat_ref[876 + k : 877 + k, :]
    norm_ref[...] = flat_ref[864:872, :WIDTH]
    scale_ref[...] = flat_ref[864:865, WIDTH : WIDTH + HEADS]
    b_down_ref[...] = flat_ref[872:873, :WIDTH]
    b_out_ref[...] = flat_ref[873:874, :WIDTH]
    qv_ref[...] = flat_ref[874:876, :WIDTH]
    for k in range(4):
        lanes = slice(k * LANES, (k + 1) * LANES)
        for i in range(2):
            w1_ref[i : i + 1, lanes] = flat_ref[879 + 4 * i + k : 880 + 4 * i + k, :]
        b1_ref[:, lanes] = flat_ref[887 + k : 888 + k, :]
        for i in range(3):
            w2_ref[i : i + 1, lanes] = flat_ref[891 + 4 * i + k : 892 + 4 * i + k, :]


def unpack(everything):
    slots, slot_rows, _ = everything.shape
    shapes = [
        (WIDTH, 3 * WIDTH),
        (2, WIDTH),
        (1, HEADS),
        (2, 512),
        (1, 512),
        (HEADS, 512),
        (WIDTH, WIDTH),
        (1, WIDTH),
        (WIDTH, HIDDEN),
        (3, LANES),
        (WIDTH, HIDDEN),
        (1, WIDTH),
        (8, WIDTH),
    ]
    shapes = [jax.ShapeDtypeStruct(s, f32) for s in shapes]
    return pl.pallas_call(
        unpack_kernel,
        grid=(1,),
        in_specs=[whole(everything)],
        out_specs=[whole(a) for a in shapes],
        out_shape=shapes,
        compiler_params=pltpu.CompilerParams(vmem_limit_bytes=16 * 1024 * 1024),
        scratch_shapes=[pltpu.VMEM((slots * (slot_rows - 2), LANES), f32)],
    )(everything)


def take_from(block, dy, dx):
    rows, cols = lax.axis_size("ty"), lax.axis_size("tx")
    route = []
    for i in range(rows * cols):
        y, x = divmod(i, cols)
        route.append((((y + dy) % rows) * cols + (x + dx) % cols, i))
    return lax.ppermute(block, ("ty", "tx"), route)


def exchange(slots):
    return lax.all_to_all(slots, axes_all, 0, 0, tiled=True)


def shards(
    inputs,
    regions,
    lead_step_index,
    running_channel_mean,
    running_channel_variance,
    query_key_value_weight,
    query_value_bias,
    log_cosine_scale,
    bias_net_weight1,
    bias_net_bias1,
    bias_net_weight2,
    output_weight,
    projection_bias,
    up_weight,
    up_bias,
    down_weight,
    down_bias,
    conditioned_norm_values,
    cotangent,
):
    items, tile_rows, flat = inputs.shape
    devices = lax.axis_size(axes_all)
    token_count = items * tile_rows * (flat // WIDTH) * devices

    stats, sent = pack(inputs, cotangent, devices)
    halos = []
    for part, (right, down, corner) in enumerate(sent):
        if part:
            (right, down, corner), halos[-1] = lax.optimization_barrier(
                ((right, down, corner), halos[-1])
            )
        halos.append((take_from(right, 0, 1), take_from(down, 1, 0), take_from(corner, 1, 1)))
    stats = exchange(stats)

    corners = regions.transpose(1, 2, 0)
    row_cut = corners[::WINDOW, 0] != corners[WINDOW - 1 :: WINDOW, 0]
    col_cut = corners[::WINDOW, 0] != corners[::WINDOW, WINDOW - 1]
    flags = 2 * row_cut.astype(jnp.int32) + col_cut.astype(jnp.int32)
    vectors = (
        query_value_bias,
        projection_bias,
        down_bias,
        conditioned_norm_values,
        up_bias,
        running_channel_mean,
        running_channel_variance,
        bias_net_weight1,
        bias_net_bias1,
        bias_net_weight2.T,
    )
    coords, target = offset_constants()
    weights = (query_key_value_weight, output_weight, up_weight, down_weight)
    *prepared, net, gate = prepare(log_cosine_scale, vectors, coords, target)
    bias_net_parts = (net, gate, coords, target)
    totals, out_parts, dn_parts, home = [], [], [], []
    for part in range(PARTS):
        out_keep, dn_keep, right, down, corner, *totals = run_block(
            part,
            flags,
            lead_step_index,
            inputs,
            cotangent,
            halos[part],
            stats,
            weights,
            prepared,
            bias_net_parts,
            totals,
            token_count,
        )
        home.append((take_from(right, 0, -1), take_from(down, -1, 0), take_from(corner, -1, -1)))
        out_parts.append(out_keep)
        dn_parts.append(dn_keep)
    grads, norm = totals
    shares = sum_slots(exchange(grads))
    outputs, grad_inputs = finish_fields(
        inputs,
        [(o, d, *h) for o, d, h in zip(out_parts, dn_parts, home)],
        norm,
        shares,
        token_count,
    )
    everything = exchange(shares)
    (
        g_qkv,
        g_qv,
        g_scale,
        g_w1,
        g_b1,
        g_w2,
        g_out,
        g_b_out,
        g_up,
        g_b_up,
        g_down,
        g_b_down,
        g_norm,
    ) = unpack(everything)
    return (
        outputs,
        grad_inputs,
        g_qkv,
        g_qv,
        g_scale.reshape(-1),
        g_w1,
        g_b1.reshape(-1),
        g_w2.T,
        g_out,
        g_b_out.reshape(-1),
        g_up,
        g_b_up.reshape(-1),
        g_down,
        g_b_down.reshape(-1),
        g_norm.reshape(2, 4, WIDTH),
        norm[2, :WIDTH],
        norm[3, :WIDTH],
    )


def solution(mesh):
    tiled = P("items", "ty", "tx")
    placed = (tiled, tiled, P("items")) + (P(),) * 15 + (tiled,)
    return jax.shard_map(
        shards,
        mesh=mesh,
        in_specs=placed,
        out_specs=(tiled, tiled) + (P(),) * 15,
        check_vma=False,
    )
```

time: 130 us -> 99.9 us (0.77)
  waiting for transfers between devices: 37 us -> 17.4 us
  Pallas kernels: 58.9 us -> 47.2 us
  starting transfers between devices: 21.9 us -> 27.9 us
  other arithmetic: 3.94 us -> 1.34 us
  local copies, waits for them, and re-layouts: 5.58 us -> 3.7 us
    all_to_all x3, waiting for transfers between devices: 18.2 us -> 5.66 us  [exchange(): return lax.all_to_all(slots, axes_all, 0, 0, tiled=True)]
    pallas_call x5 -> x6, Pallas kernels: 57 us -> 46.4 us  [the longest x2 34.6 us: run_block(): pl.pallas_call(partial(block_kernel, step_items, part * items, float(toke...]
    ppermute x6 -> x12, waiting for transfers between devices: 18.8 us -> 11.7 us  [take_from(): return lax.ppermute(block, ('ty', 'tx'), route)]
    ppermute x6 -> x12, starting transfers between devices: 8.6 us -> 12.3 us  [take_from(): return lax.ppermute(block, ('ty', 'tx'), route)]
    all_to_all x3, starting transfers between devices: 13.3 us -> 15.6 us  [exchange(): return lax.all_to_all(slots, axes_all, 0, 0, tiled=True)]
    broadcast_in_dim x3 -> x0, local copies, waits for them, and re-layouts: 1.51 us -> none  [the longest x1 0.94 us: shards(): everything = exchange(jnp.broadcast_to(share[None], grads.shape))]
  transfers between devices with their start and end apart: 9 -> 15, of which waited for: 6 -> 5; matrix products, arithmetic and copies ran while one was open for 4% -> 3% of each run, Pallas kernels for 10% -> 26%
where the time goes in v3:
time: 99.9 us; the launch traced here: 98.6 us
  Pallas kernels  47.2 us (47%)
  starting transfers between devices  27.9 us (28%)
  waiting for transfers between devices  17.4 us (17%)
  local copies, waits for them, and re-layouts  3.7 us (4%)
  other arithmetic  1.34 us (1%)
  between operations  1.08 us (1%)
    pallas_call x2, Pallas kernels, run_block(): pl.pallas_call(partial(block_kernel, step_items, part * items, float(toke...  34.6 us
    all_to_all x3, starting transfers between devices, exchange(): return lax.all_to_all(slots, axes_all, 0, 0, tiled=True)  15.6 us
    ppermute x12, starting transfers between devices, take_from(): return lax.ppermute(block, ('ty', 'tx'), route)  12.3 us
    ppermute x12, waiting for transfers between devices, take_from(): return lax.ppermute(block, ('ty', 'tx'), route)  11.7 us
    all_to_all x3, waiting for transfers between devices, exchange(): return lax.all_to_all(slots, axes_all, 0, 0, tiled=True)  5.66 us
    pallas_call x1, Pallas kernels, finish_fields(): pl.pallas_call(partial(final_kernel, float(token_count), part_steps), gri...  4.23 us
    pallas_call x1, Pallas kernels, pack(): pl.pallas_call(partial(pack_kernel, items, part_steps), grid=(items // st...  3.5 us
    pallas_call x1, Pallas kernels, prepare(): pl.pallas_call(prepare_kernel, grid=(1,), in_specs=[pl.BlockSpec(memory_s...  3.12 us
  transfers between devices with their start and end apart: 15, of which 5 were waited for; matrix products, arithmetic and copies ran while one was open for 3% of the time, Pallas kernels for 26%

profile of v3, /device:TPU:0, one launch (start us, length us, event | category | flops | bytes accessed | tf_op | source)
XLA Modules:
  0.0 98.6 jit_solution(15316739771335538657)
XLA Ops:
  0.7 3.5 %shard_map.332 = (f32[32,1,256]{2,1,0:T(1,128)}, f32[16,24,384]{2,1,0:T(8,128)}, f32[16,8,384]{2,1,0:T(8,128)}, f32[16,8,384]{2,1,0:T(8,128)}, f32[16,24,384]{2,...) custom-call(f32[32,16,768]{2,1,0:T(8,128)} %x_ref.3, f32[32,16,768]{2,1,0:T(8,128)} %ct_own.3, ...), custom_call_target="tpu_custom_call" | custom-call | flops 4000000000 | bytes 1000000 | tf_op jit(solution)/shard_map/pallas_call | solution.py:143
  4.2 2.4 %collective-permute-start = (f32[16,24,384]{2,1,0:T(8,128)}, f32[16,24,384]{2,1,0:T(8,128)S(1)}, u32[]{:S(2)}, u32[]{:S(2)}) collective-permute-start(f32[16,24,384]{2,1,0:T(8,128)} %get-tuple-element.72), channel_id=1, source_target_pairs={{4,0},{8,4},{12,8},{0,12},{20,16},{24,20},{28,24},{16,28},{5,1},{9... | collective-permute-start | bytes 1769480 | tf_op jit(solution)/shard_map/ppermute | solution.py:963
  6.6 1.5 %collective-permute-start.1 = (f32[16,8,384]{2,1,0:T(8,128)}, f32[16,8,384]{2,1,0:T(8,128)S(1)}, u32[]{:S(2)}, u32[]{:S(2)}) collective-permute-start(f32[16,8,384]{2,1,0:T(8,128)} %get-tuple-element.73), channel_id=1, source_target_pairs={{16,0},{20,4},{24,8},{28,12},{0,16},{4,20},{8,24},{12,28},{17,1},{... | collective-permute-start | bytes 589832 | tf_op jit(solution)/shard_map/ppermute | solution.py:963
  8.4 4.9 %all-to-all-start = ((f32[32,1,256]{2,1,0:T(1,128)}), f32[32,1,256]{2,1,0:T(1,128)S(1)}, u32[]{:S(2)}, u32[]{:S(2)}) async-start(f32[32,1,256]{2,1,0:T(1,128)} %get-tuple-element.78), calls=%async_computation | async-start | bytes 65536 | tf_op jit(solution)/shard_map/all_to_all | solution.py:967
  13.3 1.3 %fusion = s32[2,1,32]{2,1,0:T(1,128)} fusion(s32[16,8,32]{2,1,0:T(8,128)} %bitcast.17), kind=kLoop, calls=%fused_computation.2 | loop fusion | flops 320 | bytes 1024 | tf_op jit(solution)/shard_map/add | solution.py:1008
  14.7 3.1 %shard_map.333 = (f32[8,128]{1,0:T(8,128)}, f32[3,64,128]{2,1,0:T(8,128)}, f32[24,512]{1,0:T(8,128)}, f32[2,512,256]{2,1,0:T(8,128)}, f32[8,256]{1,0:T(8,128)}) custom-call(f32[3]{0:T(128)} %log_scale_ref.1, f32[2,96]{1,0:T(2,128)} %qv_ref.1, f32[96]{0:T(128)} %proj_ref.1, f32[96]{0:T(128)} %down_ref.1, f32[2,4,96]{2,1,0:T(4,128)} %norms_ref.1, f32[384]{0:T(512)} %up_ref.1, ...), custom_call_target="tpu_custom_call" | custom-call | bytes 1000000 | tf_op jit(solution)/shard_map/pallas_call | solution.py:283
  17.8 1.6 %collective-permute-start.3 = (f32[16,24,384]{2,1,0:T(8,128)}, f32[16,24,384]{2,1,0:T(8,128)S(1)}, u32[]{:S(2)}, u32[]{:S(2)}) collective-permute-start(f32[16,24,384]{2,1,0:T(8,128)} %get-tuple-element.75), channel_id=1, source_target_pairs={{4,0},{8,4},{12,8},{0,12},{20,16},{24,20},{28,24},{16,28},{5,1},{9... | collective-permute-start | bytes 1769480 | tf_op jit(solution)/shard_map/ppermute | solution.py:963
  19.4 1.5 %collective-permute-start.4 = (f32[16,8,384]{2,1,0:T(8,128)}, f32[16,8,384]{2,1,0:T(8,128)S(1)}, u32[]{:S(2)}, u32[]{:S(2)}) collective-permute-start(f32[16,8,384]{2,1,0:T(8,128)} %get-tuple-element.76), channel_id=1, source_target_pairs={{16,0},{20,4},{24,8},{28,12},{0,16},{4,20},{8,24},{12,28},{17,1},{... | collective-permute-start | bytes 589832 | tf_op jit(solution)/shard_map/ppermute | solution.py:963
  21.6 17.0 %shard_map.334 = (f32[16,12,384]{2,1,0:T(8,128)}, f32[16,12,384]{2,1,0:T(8,128)}, f32[16,24,384]{2,1,0:T(8,128)}, f32[16,8,384]{2,1,0:T(8,128)}, f32[16,8,384]{2...) custom-call(s32[2,32]{1,0:T(2,128)} %bitcast.15, ...), custom_call_target="tpu_custom_call" | custom-call | flops 40000000000 | bytes 1000000 | tf_op jit(solution)/shard_map/pallas_call | solution.py:786
  39.6 17.6 %shard_map.335 = (f32[16,12,384]{2,1,0:T(8,128)}, f32[16,12,384]{2,1,0:T(8,128)}, f32[16,24,384]{2,1,0:T(8,128)}, f32[16,8,384]{2,1,0:T(8,128)}, f32[16,8,384]{2...) custom-call(s32[2,32]{1,0:T(2,128)} %bitcast.16, s32[32]{0:T(128)} %lead_ref.3, f32[32,16,768]{2,1,0:T(8,128)} %x_ref.3, ...), custom_call_target="tpu_custom_call" | custom-call | flops 40000000000 | bytes 1000000 | tf_op jit(solution)/shard_map/pallas_call | solution.py:786
  57.2 5.2 %all-to-all-start.1 = ((f32[32,32,128]{2,1,0:T(8,128)}), f32[32,32,128]{2,1,0:T(8,128)S(1)}, u32[]{:S(2)}, u32[]{:S(2)}) async-start(f32[32,32,128]{2,1,0:T(8,128)} %get-tuple-element.95), calls=%async_computation.1 | async-start | bytes 1048576 | tf_op jit(solution)/shard_map/all_to_all | solution.py:967
  62.7 1.6 %collective-permute-start.9 = (f32[16,24,384]{2,1,0:T(8,128)}, f32[16,24,384]{2,1,0:T(8,128)S(1)}, u32[]{:S(2)}, u32[]{:S(2)}) collective-permute-start(f32[16,24,384]{2,1,0:T(8,128)} %get-tuple-element.103), channel_id=1, source_target_pairs={{12,0},{0,4},{4,8},{8,12},{28,16},{16,20},{20,24},{24,28},{13,1},{... | collective-permute-start | bytes 1769480 | tf_op jit(solution)/shard_map/ppermute | solution.py:963
  64.4 1.5 %collective-permute-start.7 = (f32[16,8,384]{2,1,0:T(8,128)S(1)}, f32[16,8,384]{2,1,0:T(8,128)S(1)}, u32[]{:S(2)}, u32[]{:S(2)}) collective-permute-start(f32[16,8,384]{2,1,0:T(8,128)S(1)} %copy-done.7), channel_id=1, source_target_pairs={{16,0},{20,4},{24,8},{28,12},{0,16},{4,20},{8,24},{12,28},{17,1},{... | collective-permute-start | bytes 589832 | tf_op jit(solution)/shard_map/ppermute | solution.py:963
  65.9 1.4 %collective-permute-start.10 = (f32[16,8,384]{2,1,0:T(8,128)}, f32[16,8,384]{2,1,0:T(8,128)S(1)}, u32[]{:S(2)}, u32[]{:S(2)}) collective-permute-start(f32[16,8,384]{2,1,0:T(8,128)} %get-tuple-element.104), channel_id=1, source_target_pairs={{16,0},{20,4},{24,8},{28,12},{0,16},{4,20},{8,24},{12,28},{17,1},{... | collective-permute-start | bytes 589832 | tf_op jit(solution)/shard_map/ppermute | solution.py:963
  67.3 6.6 %collective-permute-done.7.refs_3_ = f32[16,8,384]{2,1,0:T(8,128)S(1)} collective-permute-done((f32[16,8,384]{2,1,0:T(8,128)S(1)}, f32[16,8,384]{2,1,0:T(8,128)S(1)}, u32[]{:S(2)}, u32[]{:S(2)}) %collective-permute-start.7) | collective-permute-done | bytes 196640 | tf_op jit(solution)/shard_map/ppermute | solution.py:963
  73.9 1.3 %slice_bitcast_fusion = (f32[96]{0:T(128)}, f32[96]{0:T(128)}) fusion(f32[8,128]{1,0:T(8,128)} %get-tuple-element.94.norm_ref), kind=kLoop, calls=%fused_computation.3 | loop fusion | bytes 1536 | tf_op jit(solution)/shard_map/squeeze | solution.py:1086
  75.2 1.6 %all-to-all-done.1.slots_ref = f32[32,32,128]{2,1,0:T(8,128)S(1)} async-done(((f32[32,32,128]{2,1,0:T(8,128)}), f32[32,32,128]{2,1,0:T(8,128)S(1)}, u32[]{:S(2)}, u32[]{:S(2)}) %all-to-all-start.1) | async-done | bytes 524320 | tf_op jit(solution)/shard_map/all_to_all | solution.py:967
  76.8 0.9 shard_map.336.sums_ref
  77.7 5.5 %all-to-all-start.2 = ((f32[32,32,128]{2,1,0:T(8,128)}), f32[32,32,128]{2,1,0:T(8,128)S(1)}, u32[]{:S(2)}, u32[]{:S(2)}) async-start(f32[32,32,128]{2,1,0:T(8,128)} %shard_map.336.sums_ref), calls=%async_computation.2 | async-start | bytes 1048576 | tf_op jit(solution)/shard_map/all_to_all | solution.py:967
  83.8 4.6 %collective-permute-done.11.refs_9_ = f32[16,8,384]{2,1,0:T(8,128)S(1)} collective-permute-done((f32[16,8,384]{2,1,0:T(8,128)}, f32[16,8,384]{2,1,0:T(8,128)S(1)}, u32[]{:S(2)}, u32[]{:S(2)}) %collective-permute-start.11) | collective-permute-done | bytes 196640 | tf_op jit(solution)/shard_map/ppermute | solution.py:963
  88.4 0.6 copy-done.15
  89.3 4.2 %shard_map.337 = (f32[32,16,768]{2,1,0:T(8,128)}, f32[32,16,768]{2,1,0:T(8,128)}) custom-call(f32[32,16,768]{2,1,0:T(8,128)} %x_ref.3, f32[8,128]{1,0:T(8,128)} %get-tuple-element.94.norm_ref, f32[32,32,128]{2,1,0:T(8,128)} %shard_map.336.sums_ref, f32[16,12,384]{2,1,0:T(8,128)} %get-tuple-element.96.refs_0_, f32[16,12,384]{2,1,0:T(8,128)} %get-tuple-element.97.refs_1_, ...), custom_call_target="tpu_custom_call" | custom-call | flops 60000002048 | bytes 1000000 | tf_op jit(solution)/shard_map/pallas_call | solution.py:850
  93.5 4.1 %all-to-all-done.2.all_ref = f32[32,32,128]{2,1,0:T(8,128)S(1)} async-done(((f32[32,32,128]{2,1,0:T(8,128)}), f32[32,32,128]{2,1,0:T(8,128)S(1)}, u32[]{:S(2)}, u32[]{:S(2)}) %all-to-all-start.2) | async-done | bytes 524320 | tf_op jit(solution)/shard_map/all_to_all | solution.py:967
  97.6 0.8 shard_map.338
  (47 shorter events, 3.1 us)
Async XLA Ops:
  4.2 13.7 %collective-permute-start = (f32[16,24,384]{2,1,0:T(8,128)}, f32[16,24,384]{2,1,0:T(8,128)S(1)}, u32[]{:S(2)}, u32[]{:S(2)}) collective-permute-start(f32[16,24,384]{2,1,0:T(8,128)} %get-tuple-element.72), channel_id=1, source_target_pairs={{4,0},{8,4},{12,8},{0,12},{20,16},{24,20},{28,24},{16,28},{5,1},{9... | collective-permute-start | bytes 1769480 | tf_op jit(solution)/shard_map/ppermute | solution.py:963
  6.6 11.2 %collective-permute-start.1 = (f32[16,8,384]{2,1,0:T(8,128)}, f32[16,8,384]{2,1,0:T(8,128)S(1)}, u32[]{:S(2)}, u32[]{:S(2)}) collective-permute-start(f32[16,8,384]{2,1,0:T(8,128)} %get-tuple-element.73), channel_id=1, source_target_pairs={{16,0},{20,4},{24,8},{28,12},{0,16},{4,20},{8,24},{12,28},{17,1},{... | collective-permute-start | bytes 589832 | tf_op jit(solution)/shard_map/ppermute | solution.py:963
  8.1 9.8 %collective-permute-start.2 = (f32[16,8,384]{2,1,0:T(8,128)}, f32[16,8,384]{2,1,0:T(8,128)S(1)}, u32[]{:S(2)}, u32[]{:S(2)}) collective-permute-start(f32[16,8,384]{2,1,0:T(8,128)} %get-tuple-element.74), channel_id=1, source_target_pairs={{20,0},{24,4},{28,8},{16,12},{4,16},{8,20},{12,24},{0,28},{21,1},{... | collective-permute-start | bytes 589832 | tf_op jit(solution)/shard_map/ppermute | solution.py:963
  8.4 12.5 %all-to-all-start = ((f32[32,1,256]{2,1,0:T(1,128)}), f32[32,1,256]{2,1,0:T(1,128)S(1)}, u32[]{:S(2)}, u32[]{:S(2)}) async-start(f32[32,1,256]{2,1,0:T(1,128)} %get-tuple-element.78), calls=%async_computation | async-start | bytes 65536 | tf_op jit(solution)/shard_map/all_to_all | solution.py:967
  17.8 3.2 %copy-start.9 = (f32[16,8,384]{2,1,0:T(8,128)}, f32[16,8,384]{2,1,0:T(8,128)S(1)}, u32[]{:S(2)}) copy-start(f32[16,8,384]{2,1,0:T(8,128)S(1)} %collective-permute-done.1.x_down) | copy-start | bytes 589828
  17.8 3.2 %copy-start.11 = (f32[16,8,384]{2,1,0:T(8,128)}, f32[16,8,384]{2,1,0:T(8,128)S(1)}, u32[]{:S(2)}) copy-start(f32[16,8,384]{2,1,0:T(8,128)S(1)} %collective-permute-done.2.x_corner) | copy-start | bytes 589828
  17.8 20.8 %collective-permute-start.3 = (f32[16,24,384]{2,1,0:T(8,128)}, f32[16,24,384]{2,1,0:T(8,128)S(1)}, u32[]{:S(2)}, u32[]{:S(2)}) collective-permute-start(f32[16,24,384]{2,1,0:T(8,128)} %get-tuple-element.75), channel_id=1, source_target_pairs={{4,0},{8,4},{12,8},{0,12},{20,16},{24,20},{28,24},{16,28},{5,1},{9... | collective-permute-start | bytes 1769480 | tf_op jit(solution)/shard_map/ppermute | solution.py:963
  19.4 19.2 %collective-permute-start.4 = (f32[16,8,384]{2,1,0:T(8,128)}, f32[16,8,384]{2,1,0:T(8,128)S(1)}, u32[]{:S(2)}, u32[]{:S(2)}) collective-permute-start(f32[16,8,384]{2,1,0:T(8,128)} %get-tuple-element.76), channel_id=1, source_target_pairs={{16,0},{20,4},{24,8},{28,12},{0,16},{4,20},{8,24},{12,28},{17,1},{... | collective-permute-start | bytes 589832 | tf_op jit(solution)/shard_map/ppermute | solution.py:963
  20.9 17.7 %collective-permute-start.5 = (f32[16,8,384]{2,1,0:T(8,128)}, f32[16,8,384]{2,1,0:T(8,128)S(1)}, u32[]{:S(2)}, u32[]{:S(2)}) collective-permute-start(f32[16,8,384]{2,1,0:T(8,128)} %get-tuple-element.77), channel_id=1, source_target_pairs={{20,0},{24,4},{28,8},{16,12},{4,16},{8,20},{12,24},{0,28},{21,1},{... | collective-permute-start | bytes 589832 | tf_op jit(solution)/shard_map/ppermute | solution.py:963
  39.5 22.9 %copy-start.1 = (f32[16,24,384]{2,1,0:T(8,128)S(1)}, f32[16,24,384]{2,1,0:T(8,128)}, u32[]{:S(2)}) copy-start(f32[16,24,384]{2,1,0:T(8,128)} %get-tuple-element.98) | copy-start | bytes 1769476
  39.5 24.8 %copy-start.7 = (f32[16,8,384]{2,1,0:T(8,128)S(1)}, f32[16,8,384]{2,1,0:T(8,128)}, u32[]{:S(2)}) copy-start(f32[16,8,384]{2,1,0:T(8,128)} %get-tuple-element.99) | copy-start | bytes 589828
  39.6 26.3 %copy-start.6 = (f32[16,8,384]{2,1,0:T(8,128)S(1)}, f32[16,8,384]{2,1,0:T(8,128)}, u32[]{:S(2)}) copy-start(f32[16,8,384]{2,1,0:T(8,128)} %get-tuple-element.100) | copy-start | bytes 589828
  57.2 19.6 %all-to-all-start.1 = ((f32[32,32,128]{2,1,0:T(8,128)}), f32[32,32,128]{2,1,0:T(8,128)S(1)}, u32[]{:S(2)}, u32[]{:S(2)}) async-start(f32[32,32,128]{2,1,0:T(8,128)} %get-tuple-element.95), calls=%async_computation.1 | async-start | bytes 1048576 | tf_op jit(solution)/shard_map/all_to_all | solution.py:967
  62.4 20.8 %collective-permute-start.6 = (f32[16,24,384]{2,1,0:T(8,128)S(1)}, f32[16,24,384]{2,1,0:T(8,128)S(1)}, u32[]{:S(2)}, u32[]{:S(2)}) collective-permute-start(f32[16,24,384]{2,1,0:T(8,128)S(1)} %copy-done.1), channel_id=1, source_target_pairs={{12,0},{0,4},{4,8},{8,12},{28,16},{16,20},{20,24},{24,28},{13,1},{... | collective-permute-start | bytes 1769480 | tf_op jit(solution)/shard_map/ppermute | solution.py:963
  62.7 25.6 %collective-permute-start.9 = (f32[16,24,384]{2,1,0:T(8,128)}, f32[16,24,384]{2,1,0:T(8,128)S(1)}, u32[]{:S(2)}, u32[]{:S(2)}) collective-permute-start(f32[16,24,384]{2,1,0:T(8,128)} %get-tuple-element.103), channel_id=1, source_target_pairs={{12,0},{0,4},{4,8},{8,12},{28,16},{16,20},{20,24},{24,28},{13,1},{... | collective-permute-start | bytes 1769480 | tf_op jit(solution)/shard_map/ppermute | solution.py:963
  64.4 9.6 %collective-permute-start.7 = (f32[16,8,384]{2,1,0:T(8,128)S(1)}, f32[16,8,384]{2,1,0:T(8,128)S(1)}, u32[]{:S(2)}, u32[]{:S(2)}) collective-permute-start(f32[16,8,384]{2,1,0:T(8,128)S(1)} %copy-done.7), channel_id=1, source_target_pairs={{16,0},{20,4},{24,8},{28,12},{0,16},{4,20},{8,24},{12,28},{17,1},{... | collective-permute-start | bytes 589832 | tf_op jit(solution)/shard_map/ppermute | solution.py:963
  65.8 17.4 %collective-permute-start.8 = (f32[16,8,384]{2,1,0:T(8,128)S(1)}, f32[16,8,384]{2,1,0:T(8,128)S(1)}, u32[]{:S(2)}, u32[]{:S(2)}) collective-permute-start(f32[16,8,384]{2,1,0:T(8,128)S(1)} %copy-done.6), channel_id=1, source_target_pairs={{28,0},{16,4},{20,8},{24,12},{12,16},{0,20},{4,24},{8,28},{29,1},{... | collective-permute-start | bytes 589832 | tf_op jit(solution)/shard_map/ppermute | solution.py:963
  65.9 17.9 %collective-permute-start.10 = (f32[16,8,384]{2,1,0:T(8,128)}, f32[16,8,384]{2,1,0:T(8,128)S(1)}, u32[]{:S(2)}, u32[]{:S(2)}) collective-permute-start(f32[16,8,384]{2,1,0:T(8,128)} %get-tuple-element.104), channel_id=1, source_target_pairs={{16,0},{20,4},{24,8},{28,12},{0,16},{4,20},{8,24},{12,28},{17,1},{... | collective-permute-start | bytes 589832 | tf_op jit(solution)/shard_map/ppermute | solution.py:963
  73.9 14.4 %copy-start.8 = (f32[16,8,384]{2,1,0:T(8,128)}, f32[16,8,384]{2,1,0:T(8,128)S(1)}, u32[]{:S(2)}) copy-start(f32[16,8,384]{2,1,0:T(8,128)S(1)} %collective-permute-done.7.refs_3_) | copy-start | bytes 589828
  73.9 14.4 %collective-permute-start.11 = (f32[16,8,384]{2,1,0:T(8,128)}, f32[16,8,384]{2,1,0:T(8,128)S(1)}, u32[]{:S(2)}, u32[]{:S(2)}) collective-permute-start(f32[16,8,384]{2,1,0:T(8,128)} %get-tuple-element.105), channel_id=1, source_target_pairs={{28,0},{16,4},{20,8},{24,12},{12,16},{0,20},{4,24},{8,28},{29,1},{... | collective-permute-start | bytes 589832 | tf_op jit(solution)/shard_map/ppermute | solution.py:963
  77.7 19.9 %all-to-all-start.2 = ((f32[32,32,128]{2,1,0:T(8,128)}), f32[32,32,128]{2,1,0:T(8,128)S(1)}, u32[]{:S(2)}, u32[]{:S(2)}) async-start(f32[32,32,128]{2,1,0:T(8,128)} %shard_map.336.sums_ref), calls=%async_computation.2 | async-start | bytes 1048576 | tf_op jit(solution)/shard_map/all_to_all | solution.py:967
  83.2 5.2 %copy-start.10 = (f32[16,8,384]{2,1,0:T(8,128)}, f32[16,8,384]{2,1,0:T(8,128)S(1)}, u32[]{:S(2)}) copy-start(f32[16,8,384]{2,1,0:T(8,128)S(1)} %collective-permute-done.8.refs_4_) | copy-start | bytes 589828
  83.2 5.1 %copy-start.2 = (f32[16,24,384]{2,1,0:T(8,128)}, f32[16,24,384]{2,1,0:T(8,128)S(1)}, u32[]{:S(2)}) copy-start(f32[16,24,384]{2,1,0:T(8,128)S(1)} %collective-permute-done.6.refs_2_) | copy-start | bytes 1769476
  83.8 4.6 %copy-start.12 = (f32[16,8,384]{2,1,0:T(8,128)}, f32[16,8,384]{2,1,0:T(8,128)S(1)}, u32[]{:S(2)}) copy-start(f32[16,8,384]{2,1,0:T(8,128)S(1)} %collective-permute-done.10.refs_8_) | copy-start | bytes 589828
  (7 other events, 7.7 us)

commit v4 on v3

--- a/solution.py
+++ b/solution.py
@@ -67,23 +67,25 @@
     return phi, (u * 0.3989422804014327) * jnp.exp(-0.5 * (u * u))
 
 
-def pack_kernel(items, part_steps, x_ref, ct_ref, ct_top_ref, stats_ref, *refs):
+def pack_halo(fields, tops, right_ref, down_ref, corner_ref):
+    for part, (ref, top) in enumerate(zip(fields, tops)):
+        right_ref[:, 12 * part : 12 * part + 12, :] = ref[:, SHIFT:, :]
+        corner_ref[:, 4 * part : 4 * part + 4, :] = ref[:, :SHIFT, :]
+        down_ref[:, 4 * part : 4 * part + 4, :] = top[:, :SHIFT, :]
+
+
+def pack_kernel(
+    items, part_steps, x_ref, ct_ref, ct_top_ref, stats_ref, right_ref, down_ref, corner_ref, sums_ref
+):
     step = pl.program_id(0)
     step_items, rows, flat = x_ref.shape
     cols = flat // WIDTH
     half = flat // 2
 
-    sums_ref = refs[-1]
-
-    def send(right_ref, down_ref, corner_ref):
-        for part, ref in enumerate((x_ref, ct_ref)):
-            right_ref[:, 12 * part : 12 * part + 12, :] = ref[:, SHIFT:, :half]
-            corner_ref[:, 4 * part : 4 * part + 4, :] = ref[:, :SHIFT, :half]
-        down_ref[:, 0:4, :] = x_ref[:, :SHIFT, half:]
-        down_ref[:, 4:8, :] = ct_top_ref[:, :SHIFT, :]
-
-    for n in range(PARTS):
-        pl.when(step // part_steps == n)(partial(send, *refs[3 * n : 3 * n + 3]))
+    @pl.when(step >= pl.num_programs(0) - part_steps)
+    def _():
+        fields = (x_ref.at[:, :, :half], ct_ref)
+        pack_halo(fields, (x_ref.at[:, :, half:], ct_top_ref), right_ref, down_ref, corner_ref)
 
     def fold(v):
         total = v[:, :WIDTH]
@@ -118,45 +120,37 @@
         stats_ref[...] = jnp.broadcast_to(row[None], stats_ref.shape)
 
 
-def spread_kernel(row_ref, out_ref):
-    out_ref[...] = jnp.broadcast_to(row_ref[0:1][None], out_ref.shape)
-
-
 def pack(x, ct, devices):
     items, rows, flat = x.shape
     half = flat // 2
     part_items = items // PARTS
     step_items = block_of(part_items, 16)
     part_steps = part_items // step_items
-
-    def spec(n, width):
-        return pl.BlockSpec((step_items, n, width), lambda i: (i, 0, 0))
-
-    def of_part(n, count):
+    steps = items // step_items
+
+    def of_part(count, lanes):
         return pl.BlockSpec(
             (step_items, count, half),
-            lambda i: (jnp.clip(i - n * part_steps, 0, part_steps - 1), 0, 0),
+            lambda i: (jnp.minimum(steps - 1 - i, part_steps - 1), 0, lanes),
         )
 
     stats = jax.ShapeDtypeStruct((devices, 1, 2 * LANES), f32)
     counts = (24, 8, 8)
-    outs = pl.pallas_call(
+    stats, *sent = pl.pallas_call(
         partial(pack_kernel, items, part_steps),
-        grid=(items // step_items,),
+        grid=(steps,),
         in_specs=[
-            spec(rows, flat),
-            spec(rows, half),
-            pl.BlockSpec((step_items, 8, half), lambda i: (i, 0, 1)),
+            pl.BlockSpec((step_items, rows, flat), lambda i: (steps - 1 - i, 0, 0)),
+            of_part(rows, 0),
+            of_part(8, 1),
         ],
-        out_specs=[whole(stats)] + [of_part(n, c) for n in range(PARTS) for c in counts],
-        out_shape=[stats]
-        + [jax.ShapeDtypeStruct((part_items, c, half), f32) for _ in range(PARTS) for c in counts],
+        out_specs=[whole(stats)] + [of_part(c, 0) for c in counts],
+        out_shape=[stats] + [jax.ShapeDtypeStruct((part_items, c, half), f32) for c in counts],
         scratch_shapes=[pltpu.VMEM((3, 8, flat), f32)],
         cost_estimate=about(4),
         compiler_params=in_order,
     )(x, ct, ct)
-    stats = outs[0]
-    return stats, [outs[1 + 3 * n : 4 + 3 * n] for n in range(PARTS)]
+    return stats, sent
 
 
 def offset_constants():
@@ -213,7 +207,9 @@
 
 
 def prepare_kernel(
+    part_refs,
     log_scale_ref,
+    regions_ref,
     qv_ref,
     proj_ref,
     down_ref,
@@ -226,12 +222,23 @@
     w2_ref,
     coords_ref,
     target_ref,
-    scale_ref,
-    bias_ref,
-    vec_ref,
-    net_ref,
-    gate_ref,
+    *refs,
 ):
+    given, (flags_ref, scale_ref, bias_ref, vec_ref, net_ref, gate_ref), sent = (
+        refs[: 4 * part_refs],
+        refs[4 * part_refs : 4 * part_refs + 6],
+        refs[4 * part_refs + 6 :],
+    )
+    for n in range(part_refs):
+        x_ref, ct_ref, x_top_ref, ct_top_ref = given[4 * n : 4 * n + 4]
+        pack_halo((x_ref, ct_ref), (x_top_ref, ct_top_ref), *sent[3 * n : 3 * n + 3])
+    for w in range(flags_ref.shape[0]):
+        first, last = WINDOW * w, WINDOW * w + WINDOW - 1
+        corner = regions_ref[first, 0:1, :]
+        row_cut = jnp.where(corner != regions_ref[last, 0:1, :], 2, 0)
+        col_cut = jnp.where(corner != regions_ref[first, WINDOW - 1 : WINDOW, :], 1, 0)
+        flags_ref[w : w + 1, :] = row_cut + col_cut
+
     def row(ref):
         return ref[...].reshape(1, ref.shape[0])
 
@@ -269,8 +276,11 @@
         bias_ref[h] = jnp.concatenate(columns, 0) - (scale + 16.0)
 
 
-def prepare(log_scale, vectors, coords, target):
+def prepare(x, ct, log_scale, regions, vectors, coords, target):
     units = vectors[-1].shape[1]
+    items, rows, flat = x.shape
+    half = flat // 2
+    part_items = items // PARTS
     shapes = [
         (8, LANES),
         (HEADS, PLACES, LANES),
@@ -279,16 +289,28 @@
         (8, OFFSETS),
     ]
     shapes = [jax.ShapeDtypeStruct(a, f32) for a in shapes]
-    inputs = (*vectors, coords, target)
-    return pl.pallas_call(
-        prepare_kernel,
+    flags = jax.ShapeDtypeStruct((regions.shape[0] // WINDOW, regions.shape[2]), jnp.int32)
+    shapes = [flags, *shapes]
+    shapes += [
+        jax.ShapeDtypeStruct((part_items, c, half), f32)
+        for _ in range(1, PARTS)
+        for c in (24, 8, 8)
+    ]
+    inputs = (regions, *vectors, coords, target)
+    parts = []
+    for n in range(1, PARTS):
+        parts += [pl.BlockSpec((part_items, rows, half), lambda i, n=n: (n, 0, 0))] * 2
+        parts += [pl.BlockSpec((part_items, 8, half), lambda i, n=n: (n, 0, 1))] * 2
+    *made, = pl.pallas_call(
+        partial(prepare_kernel, PARTS - 1),
         grid=(1,),
-        in_specs=[pl.BlockSpec(memory_space=pltpu.SMEM)] + [whole(a) for a in inputs],
+        in_specs=[pl.BlockSpec(memory_space=pltpu.SMEM)] + [whole(a) for a in inputs] + parts,
         out_specs=[whole(a) for a in shapes],
         out_shape=shapes,
         cost_estimate=about(0),
         compiler_params=in_order,
-    )(log_scale, *inputs)
+    )(log_scale, *inputs, *([x, ct, x, ct] * (PARTS - 1)))
+    return made[:6], [made[6 + 3 * n : 9 + 3 * n] for n in range(PARTS - 1)]
 
 
 def packed(w):
@@ -792,7 +814,9 @@
         out_shape=[jax.ShapeDtypeStruct((items, n, half), f32) for n in out_rows] + tail,
         scratch_shapes=scratch,
         cost_estimate=about(40),
-        compiler_params=in_order,
+        compiler_params=pltpu.CompilerParams(
+            dimension_semantics=("arbitrary",), vmem_limit_bytes=65024 * 1024
+        ),
     )(flags, lead, x, *halo, ct, *constants)
 
 
@@ -993,19 +1017,8 @@
     token_count = items * tile_rows * (flat // WIDTH) * devices
 
     stats, sent = pack(inputs, cotangent, devices)
-    halos = []
-    for part, (right, down, corner) in enumerate(sent):
-        if part:
-            (right, down, corner), halos[-1] = lax.optimization_barrier(
-                ((right, down, corner), halos[-1])
-            )
-        halos.append((take_from(right, 0, 1), take_from(down, 1, 0), take_from(corner, 1, 1)))
     stats = exchange(stats)
 
-    corners = regions.transpose(1, 2, 0)
-    row_cut = corners[::WINDOW, 0] != corners[WINDOW - 1 :: WINDOW, 0]
-    col_cut = corners[::WINDOW, 0] != corners[::WINDOW, WINDOW - 1]
-    flags = 2 * row_cut.astype(jnp.int32) + col_cut.astype(jnp.int32)
     vectors = (
         query_value_bias,
         projection_bias,
@@ -1020,7 +1033,17 @@
     )
     coords, target = offset_constants()
     weights = (query_key_value_weight, output_weight, up_weight, down_weight)
-    *prepared, net, gate = prepare(log_cosine_scale, vectors, coords, target)
+    corners = regions.transpose(1, 2, 0)
+    (flags, *prepared, net, gate), sent_later = prepare(
+        inputs, cotangent, log_cosine_scale, corners, vectors, coords, target
+    )
+    halos = []
+    for right, down, corner in (sent, *sent_later):
+        if halos:
+            (right, down, corner), halos[-1] = lax.optimization_barrier(
+                ((right, down, corner), halos[-1])
+            )
+        halos.append((take_from(right, 0, 1), take_from(down, 1, 0), take_from(corner, 1, 1)))
     bias_net_parts = (net, gate, coords, target)
     totals, out_parts, dn_parts, home = [], [], [], []
     for part in range(PARTS):

time: 99.9 us -> 98.5 us (0.986)
  other arithmetic: 1.34 us -> 0 us
    add x1 -> x0, other arithmetic: 1.34 us -> none  [shards(): flags = 2 * row_cut.astype(jnp.int32) + col_cut.astype(jnp.int32)]
    unnamed x32 -> x24, local copies, waits for them, and re-layouts: 2.43 us -> 1.49 us
  transfers between devices with their start and end apart: 15 -> 15, of which waited for: 5 -> 6; matrix products, arithmetic and copies ran while one was open for 3% -> 1% of each run, Pallas kernels for 26% -> 27%
where the time goes in v4:
time: 98.5 us; the launch traced here: 97.3 us
  Pallas kernels  47.7 us (48%)
  starting transfers between devices  28.2 us (29%)
  waiting for transfers between devices  17.6 us (18%)
  local copies, waits for them, and re-layouts  2.77 us (3%)
  between operations  1.05 us (1%)
    pallas_call x2, Pallas kernels, run_block(): pl.pallas_call(partial(block_kernel, step_items, part * items, float(toke...  34.7 us
    all_to_all x3, starting transfers between devices, exchange(): return lax.all_to_all(slots, axes_all, 0, 0, tiled=True)  15.9 us
    ppermute x12, starting transfers between devices, take_from(): return lax.ppermute(block, ('ty', 'tx'), route)  12.3 us
    ppermute x12, waiting for transfers between devices, take_from(): return lax.ppermute(block, ('ty', 'tx'), route)  11.8 us
    all_to_all x3, waiting for transfers between devices, exchange(): return lax.all_to_all(slots, axes_all, 0, 0, tiled=True)  5.79 us
    pallas_call x1, Pallas kernels, finish_fields(): pl.pallas_call(partial(final_kernel, float(token_count), part_steps), gri...  4.23 us
    pallas_call x1, Pallas kernels, prepare(): pl.pallas_call(partial(prepare_kernel, PARTS - 1), grid=(1,), in_specs=[p...  4 us
    pallas_call x1, Pallas kernels, pack(): pl.pallas_call(partial(pack_kernel, items, part_steps), grid=(steps,), in...  3.05 us
  transfers between devices with their start and end apart: 15, of which 6 were waited for; matrix products, arithmetic and copies ran while one was open for 1% of the time, Pallas kernels for 27%

profile of v4, /device:TPU:0, one launch (start us, length us, event | category | flops | bytes accessed | tf_op | source)
XLA Modules:
  0.0 97.3 jit_solution(13914430806089715469)
XLA Ops:
  0.7 3.0 %shard_map.333 = (f32[32,1,256]{2,1,0:T(1,128)}, f32[16,24,384]{2,1,0:T(8,128)}, f32[16,8,384]{2,1,0:T(8,128)}, f32[16,8,384]{2,1,0:T(8,128)}) custom-call(f32[32,16,768]{2,1,0:T(8,128)} %x_ref.3, f32[32,16,768]{2,1,0:T(8,128)} %ct_own.3, f32[32,16,768]{2,1,0:T(8,128)} %ct_own.3), custom_call_target="tpu_custom_call" | custom-call | flops 4000000000 | bytes 1000000 | tf_op jit(solution)/shard_map/pallas_call | solution.py:139
  3.7 2.4 %collective-permute-start = (f32[16,24,384]{2,1,0:T(8,128)}, f32[16,24,384]{2,1,0:T(8,128)S(1)}, u32[]{:S(2)}, u32[]{:S(2)}) collective-permute-start(f32[16,24,384]{2,1,0:T(8,128)} %get-tuple-element.74), channel_id=1, source_target_pairs={{4,0},{8,4},{12,8},{0,12},{20,16},{24,20},{28,24},{16,28},{5,1},{9... | collective-permute-start | bytes 1769480 | tf_op jit(solution)/shard_map/ppermute | solution.py:987
  6.1 1.5 %collective-permute-start.1 = (f32[16,8,384]{2,1,0:T(8,128)}, f32[16,8,384]{2,1,0:T(8,128)S(1)}, u32[]{:S(2)}, u32[]{:S(2)}) collective-permute-start(f32[16,8,384]{2,1,0:T(8,128)} %get-tuple-element.75), channel_id=1, source_target_pairs={{16,0},{20,4},{24,8},{28,12},{0,16},{4,20},{8,24},{12,28},{17,1},{... | collective-permute-start | bytes 589832 | tf_op jit(solution)/shard_map/ppermute | solution.py:987
  8.0 4.9 %all-to-all-start = ((f32[32,1,256]{2,1,0:T(1,128)}), f32[32,1,256]{2,1,0:T(1,128)S(1)}, u32[]{:S(2)}, u32[]{:S(2)}) async-start(f32[32,1,256]{2,1,0:T(1,128)} %get-tuple-element.80), calls=%async_computation | async-start | bytes 65536 | tf_op jit(solution)/shard_map/all_to_all | solution.py:991
  12.9 4.0 %shard_map.332 = (s32[2,32]{1,0:T(2,128)}, f32[8,128]{1,0:T(8,128)}, f32[3,64,128]{2,1,0:T(8,128)}, f32[24,512]{1,0:T(8,128)}, f32[2,512,256]{2,1,0:T(8,128)}, /...) custom-call(f32[3]{0:T(128)} %log_scale_ref.1, ...), custom_call_target="tpu_custom_call" | custom-call | bytes 1000000 | tf_op jit(solution)/shard_map/pallas_call | solution.py:304
  16.9 1.6 %collective-permute-start.3 = (f32[16,24,384]{2,1,0:T(8,128)}, f32[16,24,384]{2,1,0:T(8,128)}, u32[]{:S(2)}, u32[]{:S(2)}) collective-permute-start(f32[16,24,384]{2,1,0:T(8,128)} %get-tuple-element.77), channel_id=1, source_target_pairs={{4,0},{8,4},{12,8},{0,12},{20,16},{24,20},{28,24},{16,28},{5,1},{9... | collective-permute-start | bytes 1769480 | tf_op jit(solution)/shard_map/ppermute | solution.py:987
  18.5 1.5 %collective-permute-start.4 = (f32[16,8,384]{2,1,0:T(8,128)}, f32[16,8,384]{2,1,0:T(8,128)}, u32[]{:S(2)}, u32[]{:S(2)}) collective-permute-start(f32[16,8,384]{2,1,0:T(8,128)} %get-tuple-element.78), channel_id=1, source_target_pairs={{16,0},{20,4},{24,8},{28,12},{0,16},{4,20},{8,24},{12,28},{17,1},{... | collective-permute-start | bytes 589832 | tf_op jit(solution)/shard_map/ppermute | solution.py:987
  20.2 0.6 copy-done
  20.8 17.0 %shard_map.334 = (f32[16,12,384]{2,1,0:T(8,128)}, f32[16,12,384]{2,1,0:T(8,128)}, f32[16,24,384]{2,1,0:T(8,128)}, f32[16,8,384]{2,1,0:T(8,128)}, f32[16,8,384]{2...) custom-call(s32[2,32]{1,0:T(2,128)} %get-tuple-element.70.flags_ref,, ...), custom_call_target="tpu_custom_call" | custom-call | flops 40000000000 | bytes 1000000 | tf_op jit(solution)/shard_map/pallas_call | solution.py:808
  37.8 17.7 %shard_map.335 = (f32[16,12,384]{2,1,0:T(8,128)}, f32[16,12,384]{2,1,0:T(8,128)}, f32[16,24,384]{2,1,0:T(8,128)}, f32[16,8,384]{2,1,0:T(8,128)}, f32[16,8,384]{2...) custom-call(s32[2,32]{1,0:T(2,128)} %get-tuple-element.70.flags_ref, s32[32]{0:T(128)} %lead_ref.3, ...), custom_call_target="tpu_custom_call" | custom-call | flops 40000000000 | bytes 1000000 | tf_op jit(solution)/shard_map/pallas_call | solution.py:808
  55.6 5.6 %all-to-all-start.1 = ((f32[32,32,128]{2,1,0:T(8,128)}), f32[32,32,128]{2,1,0:T(8,128)S(1)}, u32[]{:S(2)}, u32[]{:S(2)}) async-start(f32[32,32,128]{2,1,0:T(8,128)} %get-tuple-element.97), calls=%async_computation.1 | async-start | bytes 1048576 | tf_op jit(solution)/shard_map/all_to_all | solution.py:991
  61.5 1.6 %collective-permute-start.9 = (f32[16,24,384]{2,1,0:T(8,128)}, f32[16,24,384]{2,1,0:T(8,128)S(1)}, u32[]{:S(2)}, u32[]{:S(2)}) collective-permute-start(f32[16,24,384]{2,1,0:T(8,128)} %get-tuple-element.105), channel_id=1, source_target_pairs={{12,0},{0,4},{4,8},{8,12},{28,16},{16,20},{20,24},{24,28},{13,1},{... | collective-permute-start | bytes 1769480 | tf_op jit(solution)/shard_map/ppermute | solution.py:987
  63.1 1.5 %collective-permute-start.7 = (f32[16,8,384]{2,1,0:T(8,128)S(1)}, f32[16,8,384]{2,1,0:T(8,128)S(1)}, u32[]{:S(2)}, u32[]{:S(2)}) collective-permute-start(f32[16,8,384]{2,1,0:T(8,128)S(1)} %copy-done.5), channel_id=1, source_target_pairs={{16,0},{20,4},{24,8},{28,12},{0,16},{4,20},{8,24},{12,28},{17,1},{... | collective-permute-start | bytes 589832 | tf_op jit(solution)/shard_map/ppermute | solution.py:987
  64.6 1.4 %collective-permute-start.10 = (f32[16,8,384]{2,1,0:T(8,128)}, f32[16,8,384]{2,1,0:T(8,128)S(1)}, u32[]{:S(2)}, u32[]{:S(2)}) collective-permute-start(f32[16,8,384]{2,1,0:T(8,128)} %get-tuple-element.106), channel_id=1, source_target_pairs={{16,0},{20,4},{24,8},{28,12},{0,16},{4,20},{8,24},{12,28},{17,1},{... | collective-permute-start | bytes 589832 | tf_op jit(solution)/shard_map/ppermute | solution.py:987
  66.1 6.6 %collective-permute-done.7.refs_3_ = f32[16,8,384]{2,1,0:T(8,128)S(1)} collective-permute-done((f32[16,8,384]{2,1,0:T(8,128)S(1)}, f32[16,8,384]{2,1,0:T(8,128)S(1)}, u32[]{:S(2)}, u32[]{:S(2)}) %collective-permute-start.7) | collective-permute-done | bytes 196640 | tf_op jit(solution)/shard_map/ppermute | solution.py:987
  72.7 1.3 %slice_bitcast_fusion = (f32[96]{0:T(128)}, f32[96]{0:T(128)}) fusion(f32[8,128]{1,0:T(8,128)} %get-tuple-element.96.norm_ref), kind=kLoop, calls=%fused_computation | loop fusion | bytes 1536 | tf_op jit(solution)/shard_map/squeeze | solution.py:1109
  74.0 1.6 %all-to-all-done.1.slots_ref = f32[32,32,128]{2,1,0:T(8,128)S(1)} async-done(((f32[32,32,128]{2,1,0:T(8,128)}), f32[32,32,128]{2,1,0:T(8,128)S(1)}, u32[]{:S(2)}, u32[]{:S(2)}) %all-to-all-start.1) | async-done | bytes 524320 | tf_op jit(solution)/shard_map/all_to_all | solution.py:991
  75.5 0.9 shard_map.336.sums_ref
  76.4 5.5 %all-to-all-start.2 = ((f32[32,32,128]{2,1,0:T(8,128)}), f32[32,32,128]{2,1,0:T(8,128)S(1)}, u32[]{:S(2)}, u32[]{:S(2)}) async-start(f32[32,32,128]{2,1,0:T(8,128)} %shard_map.336.sums_ref), calls=%async_computation.2 | async-start | bytes 1048576 | tf_op jit(solution)/shard_map/all_to_all | solution.py:991
  82.5 4.6 %collective-permute-done.11.refs_9_ = f32[16,8,384]{2,1,0:T(8,128)S(1)} collective-permute-done((f32[16,8,384]{2,1,0:T(8,128)}, f32[16,8,384]{2,1,0:T(8,128)S(1)}, u32[]{:S(2)}, u32[]{:S(2)}) %collective-permute-start.11) | collective-permute-done | bytes 196640 | tf_op jit(solution)/shard_map/ppermute | solution.py:987
  87.1 0.6 copy-done.11
  88.0 4.2 %shard_map.337 = (f32[32,16,768]{2,1,0:T(8,128)}, f32[32,16,768]{2,1,0:T(8,128)}) custom-call(f32[32,16,768]{2,1,0:T(8,128)} %x_ref.3, f32[8,128]{1,0:T(8,128)} %get-tuple-element.96.norm_ref, f32[32,32,128]{2,1,0:T(8,128)} %shard_map.336.sums_ref, f32[16,12,384]{2,1,0:T(8,128)} %get-tuple-element.98.refs_0_, f32[16,12,384]{2,1,0:T(8,128)} %get-tuple-element.99.refs_1_, ...), custom_call_target="tpu_custom_call" | custom-call | flops 60000002048 | bytes 1000000 | tf_op jit(solution)/shard_map/pallas_call | solution.py:874
  92.2 4.1 %all-to-all-done.2.all_ref = f32[32,32,128]{2,1,0:T(8,128)S(1)} async-done(((f32[32,32,128]{2,1,0:T(8,128)}), f32[32,32,128]{2,1,0:T(8,128)S(1)}, u32[]{:S(2)}, u32[]{:S(2)}) %all-to-all-start.2) | async-done | bytes 524320 | tf_op jit(solution)/shard_map/all_to_all | solution.py:991
  96.3 0.8 shard_map.338
  (38 shorter events, 1.7 us)
Async XLA Ops:
  3.7 13.2 %collective-permute-start = (f32[16,24,384]{2,1,0:T(8,128)}, f32[16,24,384]{2,1,0:T(8,128)S(1)}, u32[]{:S(2)}, u32[]{:S(2)}) collective-permute-start(f32[16,24,384]{2,1,0:T(8,128)} %get-tuple-element.74), channel_id=1, source_target_pairs={{4,0},{8,4},{12,8},{0,12},{20,16},{24,20},{28,24},{16,28},{5,1},{9... | collective-permute-start | bytes 1769480 | tf_op jit(solution)/shard_map/ppermute | solution.py:987
  6.1 10.8 %collective-permute-start.1 = (f32[16,8,384]{2,1,0:T(8,128)}, f32[16,8,384]{2,1,0:T(8,128)S(1)}, u32[]{:S(2)}, u32[]{:S(2)}) collective-permute-start(f32[16,8,384]{2,1,0:T(8,128)} %get-tuple-element.75), channel_id=1, source_target_pairs={{16,0},{20,4},{24,8},{28,12},{0,16},{4,20},{8,24},{12,28},{17,1},{... | collective-permute-start | bytes 589832 | tf_op jit(solution)/shard_map/ppermute | solution.py:987
  7.6 9.3 %collective-permute-start.2 = (f32[16,8,384]{2,1,0:T(8,128)}, f32[16,8,384]{2,1,0:T(8,128)S(1)}, u32[]{:S(2)}, u32[]{:S(2)}) collective-permute-start(f32[16,8,384]{2,1,0:T(8,128)} %get-tuple-element.76), channel_id=1, source_target_pairs={{20,0},{24,4},{28,8},{16,12},{4,16},{8,20},{12,24},{0,28},{21,1},{... | collective-permute-start | bytes 589832 | tf_op jit(solution)/shard_map/ppermute | solution.py:987
  8.0 12.2 %all-to-all-start = ((f32[32,1,256]{2,1,0:T(1,128)}), f32[32,1,256]{2,1,0:T(1,128)S(1)}, u32[]{:S(2)}, u32[]{:S(2)}) async-start(f32[32,1,256]{2,1,0:T(1,128)} %get-tuple-element.80), calls=%async_computation | async-start | bytes 65536 | tf_op jit(solution)/shard_map/all_to_all | solution.py:991
  16.9 3.3 %copy-start.6 = (f32[16,8,384]{2,1,0:T(8,128)}, f32[16,8,384]{2,1,0:T(8,128)S(1)}, u32[]{:S(2)}) copy-start(f32[16,8,384]{2,1,0:T(8,128)S(1)} %collective-permute-done.1.x_down) | copy-start | bytes 589828
  16.9 3.3 %copy-start.8 = (f32[16,8,384]{2,1,0:T(8,128)}, f32[16,8,384]{2,1,0:T(8,128)S(1)}, u32[]{:S(2)}) copy-start(f32[16,8,384]{2,1,0:T(8,128)S(1)} %collective-permute-done.2.x_corner) | copy-start | bytes 589828
  16.9 3.2 %copy-start.2 = (f32[16,24,384]{2,1,0:T(8,128)}, f32[16,24,384]{2,1,0:T(8,128)S(1)}, u32[]{:S(2)}) copy-start(f32[16,24,384]{2,1,0:T(8,128)S(1)} %collective-permute-done.x_right) | copy-start | bytes 1769476
  16.9 20.9 %collective-permute-start.3 = (f32[16,24,384]{2,1,0:T(8,128)}, f32[16,24,384]{2,1,0:T(8,128)}, u32[]{:S(2)}, u32[]{:S(2)}) collective-permute-start(f32[16,24,384]{2,1,0:T(8,128)} %get-tuple-element.77), channel_id=1, source_target_pairs={{4,0},{8,4},{12,8},{0,12},{20,16},{24,20},{28,24},{16,28},{5,1},{9... | collective-permute-start | bytes 1769480 | tf_op jit(solution)/shard_map/ppermute | solution.py:987
  18.5 19.3 %collective-permute-start.4 = (f32[16,8,384]{2,1,0:T(8,128)}, f32[16,8,384]{2,1,0:T(8,128)}, u32[]{:S(2)}, u32[]{:S(2)}) collective-permute-start(f32[16,8,384]{2,1,0:T(8,128)} %get-tuple-element.78), channel_id=1, source_target_pairs={{16,0},{20,4},{24,8},{28,12},{0,16},{4,20},{8,24},{12,28},{17,1},{... | collective-permute-start | bytes 589832 | tf_op jit(solution)/shard_map/ppermute | solution.py:987
  20.0 17.8 %collective-permute-start.5 = (f32[16,8,384]{2,1,0:T(8,128)}, f32[16,8,384]{2,1,0:T(8,128)}, u32[]{:S(2)}, u32[]{:S(2)}) collective-permute-start(f32[16,8,384]{2,1,0:T(8,128)} %get-tuple-element.79), channel_id=1, source_target_pairs={{20,0},{24,4},{28,8},{16,12},{4,16},{8,20},{12,24},{0,28},{21,1},{... | collective-permute-start | bytes 589832 | tf_op jit(solution)/shard_map/ppermute | solution.py:987
  37.8 25.3 %copy-start.5 = (f32[16,8,384]{2,1,0:T(8,128)S(1)}, f32[16,8,384]{2,1,0:T(8,128)}, u32[]{:S(2)}) copy-start(f32[16,8,384]{2,1,0:T(8,128)} %get-tuple-element.101) | copy-start | bytes 589828
  37.8 26.7 %copy-start.4 = (f32[16,8,384]{2,1,0:T(8,128)S(1)}, f32[16,8,384]{2,1,0:T(8,128)}, u32[]{:S(2)}) copy-start(f32[16,8,384]{2,1,0:T(8,128)} %get-tuple-element.102) | copy-start | bytes 589828
  55.6 20.0 %all-to-all-start.1 = ((f32[32,32,128]{2,1,0:T(8,128)}), f32[32,32,128]{2,1,0:T(8,128)S(1)}, u32[]{:S(2)}, u32[]{:S(2)}) async-start(f32[32,32,128]{2,1,0:T(8,128)} %get-tuple-element.97), calls=%async_computation.1 | async-start | bytes 1048576 | tf_op jit(solution)/shard_map/all_to_all | solution.py:991
  61.2 20.8 %collective-permute-start.6 = (f32[16,24,384]{2,1,0:T(8,128)}, f32[16,24,384]{2,1,0:T(8,128)S(1)}, u32[]{:S(2)}, u32[]{:S(2)}) collective-permute-start(f32[16,24,384]{2,1,0:T(8,128)} %get-tuple-element.100), channel_id=1, source_target_pairs={{12,0},{0,4},{4,8},{8,12},{28,16},{16,20},{20,24},{24,28},{13,1},{... | collective-permute-start | bytes 1769480 | tf_op jit(solution)/shard_map/ppermute | solution.py:987
  61.5 25.6 %collective-permute-start.9 = (f32[16,24,384]{2,1,0:T(8,128)}, f32[16,24,384]{2,1,0:T(8,128)S(1)}, u32[]{:S(2)}, u32[]{:S(2)}) collective-permute-start(f32[16,24,384]{2,1,0:T(8,128)} %get-tuple-element.105), channel_id=1, source_target_pairs={{12,0},{0,4},{4,8},{8,12},{28,16},{16,20},{20,24},{24,28},{13,1},{... | collective-permute-start | bytes 1769480 | tf_op jit(solution)/shard_map/ppermute | solution.py:987
  63.1 9.6 %collective-permute-start.7 = (f32[16,8,384]{2,1,0:T(8,128)S(1)}, f32[16,8,384]{2,1,0:T(8,128)S(1)}, u32[]{:S(2)}, u32[]{:S(2)}) collective-permute-start(f32[16,8,384]{2,1,0:T(8,128)S(1)} %copy-done.5), channel_id=1, source_target_pairs={{16,0},{20,4},{24,8},{28,12},{0,16},{4,20},{8,24},{12,28},{17,1},{... | collective-permute-start | bytes 589832 | tf_op jit(solution)/shard_map/ppermute | solution.py:987
  64.6 17.4 %collective-permute-start.8 = (f32[16,8,384]{2,1,0:T(8,128)S(1)}, f32[16,8,384]{2,1,0:T(8,128)S(1)}, u32[]{:S(2)}, u32[]{:S(2)}) collective-permute-start(f32[16,8,384]{2,1,0:T(8,128)S(1)} %copy-done.4), channel_id=1, source_target_pairs={{28,0},{16,4},{20,8},{24,12},{12,16},{0,20},{4,24},{8,28},{29,1},{... | collective-permute-start | bytes 589832 | tf_op jit(solution)/shard_map/ppermute | solution.py:987
  64.6 17.9 %collective-permute-start.10 = (f32[16,8,384]{2,1,0:T(8,128)}, f32[16,8,384]{2,1,0:T(8,128)S(1)}, u32[]{:S(2)}, u32[]{:S(2)}) collective-permute-start(f32[16,8,384]{2,1,0:T(8,128)} %get-tuple-element.106), channel_id=1, source_target_pairs={{16,0},{20,4},{24,8},{28,12},{0,16},{4,20},{8,24},{12,28},{17,1},{... | collective-permute-start | bytes 589832 | tf_op jit(solution)/shard_map/ppermute | solution.py:987
  72.7 14.4 %copy-start.7 = (f32[16,8,384]{2,1,0:T(8,128)}, f32[16,8,384]{2,1,0:T(8,128)S(1)}, u32[]{:S(2)}) copy-start(f32[16,8,384]{2,1,0:T(8,128)S(1)} %collective-permute-done.7.refs_3_) | copy-start | bytes 589828
  72.7 14.4 %collective-permute-start.11 = (f32[16,8,384]{2,1,0:T(8,128)}, f32[16,8,384]{2,1,0:T(8,128)S(1)}, u32[]{:S(2)}, u32[]{:S(2)}) collective-permute-start(f32[16,8,384]{2,1,0:T(8,128)} %get-tuple-element.107), channel_id=1, source_target_pairs={{28,0},{16,4},{20,8},{24,12},{12,16},{0,20},{4,24},{8,28},{29,1},{... | collective-permute-start | bytes 589832 | tf_op jit(solution)/shard_map/ppermute | solution.py:987
  76.4 19.9 %all-to-all-start.2 = ((f32[32,32,128]{2,1,0:T(8,128)}), f32[32,32,128]{2,1,0:T(8,128)S(1)}, u32[]{:S(2)}, u32[]{:S(2)}) async-start(f32[32,32,128]{2,1,0:T(8,128)} %shard_map.336.sums_ref), calls=%async_computation.2 | async-start | bytes 1048576 | tf_op jit(solution)/shard_map/all_to_all | solution.py:991
  81.9 5.2 %copy-start.9 = (f32[16,8,384]{2,1,0:T(8,128)}, f32[16,8,384]{2,1,0:T(8,128)S(1)}, u32[]{:S(2)}) copy-start(f32[16,8,384]{2,1,0:T(8,128)S(1)} %collective-permute-done.8.refs_4_) | copy-start | bytes 589828
  81.9 5.2 %copy-start.1 = (f32[16,24,384]{2,1,0:T(8,128)}, f32[16,24,384]{2,1,0:T(8,128)S(1)}, u32[]{:S(2)}) copy-start(f32[16,24,384]{2,1,0:T(8,128)S(1)} %collective-permute-done.6.refs_2_) | copy-start | bytes 1769476
  82.5 4.6 %copy-start.10 = (f32[16,8,384]{2,1,0:T(8,128)}, f32[16,8,384]{2,1,0:T(8,128)S(1)}, u32[]{:S(2)}) copy-start(f32[16,8,384]{2,1,0:T(8,128)S(1)} %collective-permute-done.10.refs_8_) | copy-start | bytes 589828
  (3 other events, 2.2 us)

commit v5 on v4

--- a/solution.py
+++ b/solution.py
@@ -27,7 +27,9 @@
 norm_eps = 1e-05
 unit_eps = 1e-06
 momentum = 0.1
-axes_all = ("ty", "tx", "items")
+axes_all = ("ty", "th", "tl", "items")
+axes_far = ("ty", "th", "items")
+axes_tiles = ("ty", "th", "tl")
 
 f32 = jnp.float32
 bf16 = jnp.bfloat16
@@ -330,6 +332,7 @@
     is_last,
     flags_ref,
     lead_ref,
+    side_ref,
     x_own,
     x_right,
     x_down,
@@ -355,8 +358,8 @@
     out_keep, dn_keep, send_right, send_down, send_corner = refs[:5]
     refs = refs[5:]
     if is_last:
-        grads_ref, norm_ref, affine_ref, flat_ref = refs[:4]
-        refs = refs[4:]
+        own_ref, give_ref, norm_ref, affine_ref, flat_ref = refs[:5]
+        refs = refs[5:]
     else:
         affine_ref, refs = refs[-1], refs[:-1]
     g_qkv_ref, g_out_ref, g_up_ref, g_down_ref, sums_ref, dpos_ref, dcos_ref = refs
@@ -723,17 +726,22 @@
                 at = 879 + 4 * i + k
                 flat_ref[at : at + 1, :] = row[:, k * LANES : (k + 1) * LANES]
 
-        slots, slot_rows, _ = grads_ref.shape
+        slots, slot_rows, _ = own_ref.shape
         share = slot_rows - 2
+        first_side = side_ref[0] == 0
         for j in range(slots):
-            grads_ref[j, 0:share, :] = flat_ref[share * j : share * (j + 1), :]
-        for i in range(2):
-            grads_ref[:, share + i : share + i + 1, :WIDTH] = jnp.broadcast_to(
-                totals[9 + i][None], (slots, 1, WIDTH)
-            )
-            grads_ref[:, share + i : share + i + 1, WIDTH:] = jnp.zeros(
-                (slots, 1, LANES - WIDTH), f32
-            )
+            near = flat_ref[share * j : share * (j + 1), :]
+            far = flat_ref[share * (slots + j) : share * (slots + j + 1), :]
+            own_ref[j, 0:share, :] = jnp.where(first_side, near, far)
+            give_ref[j, 0:share, :] = jnp.where(first_side, far, near)
+        for ref in (own_ref, give_ref):
+            for i in range(2):
+                ref[:, share + i : share + i + 1, :WIDTH] = jnp.broadcast_to(
+                    totals[9 + i][None], (slots, 1, WIDTH)
+                )
+                ref[:, share + i : share + i + 1, WIDTH:] = jnp.zeros(
+                    (slots, 1, LANES - WIDTH), f32
+                )
 
     if is_last:
         finish()
@@ -754,6 +762,7 @@
     part,
     flags,
     lead,
+    side,
     x,
     ct,
     halo,
@@ -784,7 +793,8 @@
     scratch = [pltpu.VMEM((2, WIDTH, LANES), f32)]
     if is_last:
         tail = [
-            jax.ShapeDtypeStruct((slots, slot_rows, LANES), f32),
+            jax.ShapeDtypeStruct((slots // 2, slot_rows, LANES), f32),
+            jax.ShapeDtypeStruct((slots // 2, slot_rows, LANES), f32),
             jax.ShapeDtypeStruct((8, LANES), f32),
         ]
         scratch.append(pltpu.VMEM((slots * (slot_rows - 2), LANES), f32))
@@ -808,7 +818,7 @@
     return pl.pallas_call(
         partial(block_kernel, step_items, part * items, float(token_count), is_first, is_last),
         grid=(steps,),
-        in_specs=[smem, smem, field, rows(24), rows(8), rows(8), field]
+        in_specs=[smem, smem, smem, field, rows(24), rows(8), rows(8), field]
         + [whole(a) for a in constants],
         out_specs=[rows(n) for n in out_rows] + [whole(a) for a in tail],
         out_shape=[jax.ShapeDtypeStruct((items, n, half), f32) for n in out_rows] + tail,
@@ -817,7 +827,7 @@
         compiler_params=pltpu.CompilerParams(
             dimension_semantics=("arbitrary",), vmem_limit_bytes=65024 * 1024
         ),
-    )(flags, lead, x, *halo, ct, *constants)
+    )(flags, lead, side, x, *halo, ct, *constants)
 
 
 def place(ref_out, m, keep, right, down, corner, part, fn):
@@ -906,7 +916,9 @@
 
 
 def unpack_kernel(
-    all_ref,
+    side_ref,
+    mine_ref,
+    other_ref,
     qkv_ref,
     qv_ref,
     scale_ref,
@@ -922,10 +934,15 @@
     norm_ref,
     flat_ref,
 ):
-    slots, slot_rows, _ = all_ref.shape
+    slots, slot_rows, _ = mine_ref.shape
     share = slot_rows - 2
+    first_side = side_ref[0] == 0
     for j in range(slots):
-        flat_ref[share * j : share * (j + 1), :] = all_ref[j, 0:share, :]
+        mine, other = mine_ref[j, 0:share, :], other_ref[j, 0:share, :]
+        flat_ref[share * j : share * (j + 1), :] = jnp.where(first_side, mine, other)
+        flat_ref[share * (slots + j) : share * (slots + j + 1), :] = jnp.where(
+            first_side, other, mine
+        )
     qkv_ref[:, 0:LANES] = flat_ref[0:96, :]
     qkv_ref[:, LANES : 2 * LANES] = flat_ref[96:192, :]
     qkv_ref[:, 2 * LANES :] = flat_ref[192:288, WIDTH:]
@@ -949,8 +966,8 @@
             w2_ref[i : i + 1, lanes] = flat_ref[891 + 4 * i + k : 892 + 4 * i + k, :]
 
 
-def unpack(everything):
-    slots, slot_rows, _ = everything.shape
+def unpack(side, mine, other):
+    slots, slot_rows, _ = mine.shape
     shapes = [
         (WIDTH, 3 * WIDTH),
         (2, WIDTH),
@@ -970,25 +987,29 @@
     return pl.pallas_call(
         unpack_kernel,
         grid=(1,),
-        in_specs=[whole(everything)],
+        in_specs=[pl.BlockSpec(memory_space=pltpu.SMEM), whole(mine), whole(other)],
         out_specs=[whole(a) for a in shapes],
         out_shape=shapes,
         compiler_params=pltpu.CompilerParams(vmem_limit_bytes=16 * 1024 * 1024),
-        scratch_shapes=[pltpu.VMEM((slots * (slot_rows - 2), LANES), f32)],
-    )(everything)
+        scratch_shapes=[pltpu.VMEM((2 * slots * (slot_rows - 2), LANES), f32)],
+    )(side, mine, other)
 
 
 def take_from(block, dy, dx):
-    rows, cols = lax.axis_size("ty"), lax.axis_size("tx")
+    rows, cols = lax.axis_size("ty"), lax.axis_size(("th", "tl"))
     route = []
     for i in range(rows * cols):
         y, x = divmod(i, cols)
         route.append((((y + dy) % rows) * cols + (x + dx) % cols, i))
-    return lax.ppermute(block, ("ty", "tx"), route)
-
-
-def exchange(slots):
-    return lax.all_to_all(slots, axes_all, 0, 0, tiled=True)
+    return lax.ppermute(block, axes_tiles, route)
+
+
+def exchange(slots, axes):
+    return lax.all_to_all(slots, axes, 0, 0, tiled=True)
+
+
+def swap(block):
+    return lax.ppermute(block, "tl", [(0, 1), (1, 0)])
 
 
 def shards(
@@ -1017,7 +1038,8 @@
     token_count = items * tile_rows * (flat // WIDTH) * devices
 
     stats, sent = pack(inputs, cotangent, devices)
-    stats = exchange(stats)
+    stats = exchange(stats, axes_all)
+    side = lax.axis_index("tl").astype(jnp.int32).reshape(1)
 
     vectors = (
         query_value_bias,
@@ -1051,6 +1073,7 @@
             part,
             flags,
             lead_step_index,
+            side,
             inputs,
             cotangent,
             halos[part],
@@ -1064,8 +1087,9 @@
         home.append((take_from(right, 0, -1), take_from(down, -1, 0), take_from(corner, -1, -1)))
         out_parts.append(out_keep)
         dn_parts.append(dn_keep)
-    grads, norm = totals
-    shares = sum_slots(exchange(grads))
+    own, give, norm = totals
+    give, home[:-1] = lax.optimization_barrier((give, home[:-1]))
+    shares = sum_slots(exchange(own + swap(give), axes_far))
     outputs, grad_inputs = finish_fields(
         inputs,
         [(o, d, *h) for o, d, h in zip(out_parts, dn_parts, home)],
@@ -1073,7 +1097,9 @@
         shares,
         token_count,
     )
-    everything = exchange(shares)
+    mine = exchange(shares, axes_far)
+    mine, outputs, grad_inputs = lax.optimization_barrier((mine, outputs, grad_inputs))
+    other = swap(mine)
     (
         g_qkv,
         g_qv,
@@ -1088,7 +1114,7 @@
         g_down,
         g_b_down,
         g_norm,
-    ) = unpack(everything)
+    ) = unpack(side, mine, other)
     return (
         outputs,
         grad_inputs,
@@ -1111,11 +1137,13 @@
 
 
 def solution(mesh):
-    tiled = P("items", "ty", "tx")
+    rows, cols, depth = (mesh.shape[a] for a in ("ty", "tx", "items"))
+    split_mesh = jax.sharding.Mesh(mesh.devices.reshape(rows, cols // 2, 2, depth), axes_all)
+    tiled = P("items", "ty", ("th", "tl"))
     placed = (tiled, tiled, P("items")) + (P(),) * 15 + (tiled,)
     return jax.shard_map(
         shards,
-        mesh=mesh,
+        mesh=split_mesh,
         in_specs=placed,
         out_specs=(tiled, tiled) + (P(),) * 15,
         check_vma=False,

time: 98.5 us -> 95.7 us (0.972)
  waiting for transfers between devices: 17.6 us -> 14.8 us
  other arithmetic: 0 us -> 1.7 us
    ppermute x12 -> x14, waiting for transfers between devices: 11.8 us -> 1.52 us  [the longest x2 1.49 us: swap(): return lax.ppermute(block, 'tl', [(0, 1), (1, 0)])]
    all_to_all x3, waiting for transfers between devices: 5.79 us -> 13.2 us  [exchange(): return lax.all_to_all(slots, axes, 0, 0, tiled=True)]
    add x0 -> x1, other arithmetic: none -> 1.7 us  [shards(): shares = sum_slots(exchange(own + swap(give), axes_far))]
    all_to_all x3, starting transfers between devices: 15.9 us -> 14.9 us  [exchange(): return lax.all_to_all(slots, axes, 0, 0, tiled=True)]
    ppermute x12 -> x14, starting transfers between devices: 12.3 us -> 12.6 us  [the longest x12 12.3 us: take_from(): return lax.ppermute(block, axes_tiles, route)]
  transfers between devices with their start and end apart: 15 -> 17, of which waited for: 6 -> 4; matrix products, arithmetic and copies ran while one was open for 1% -> 3% of each run, Pallas kernels for 27% -> 46%
where the time goes in v5:
time: 95.7 us; the launch traced here: 95.2 us
  Pallas kernels  47.4 us (50%)
  starting transfers between devices  27.5 us (29%)
  waiting for transfers between devices  14.8 us (15%)
  local copies, waits for them, and re-layouts  2.8 us (3%)
  other arithmetic  1.7 us (2%)
  between operations  1.06 us (1%)
    pallas_call x2, Pallas kernels, run_block(): pl.pallas_call(partial(block_kernel, step_items, part * items, float(toke...  34.5 us
    all_to_all x3, starting transfers between devices, exchange(): return lax.all_to_all(slots, axes, 0, 0, tiled=True)  14.9 us
    all_to_all x3, waiting for transfers between devices, exchange(): return lax.all_to_all(slots, axes, 0, 0, tiled=True)  13.2 us
    ppermute x12, starting transfers between devices, take_from(): return lax.ppermute(block, axes_tiles, route)  12.3 us
    pallas_call x1, Pallas kernels, finish_fields(): pl.pallas_call(partial(final_kernel, float(token_count), part_steps), gri...  4.23 us
    pallas_call x1, Pallas kernels, prepare(): pl.pallas_call(partial(prepare_kernel, PARTS - 1), grid=(1,), in_specs=[p...  3.99 us
    pallas_call x1, Pallas kernels, pack(): pl.pallas_call(partial(pack_kernel, items, part_steps), grid=(steps,), in...  3.05 us
  transfers between devices with their start and end apart: 17, of which 4 were waited for; matrix products, arithmetic and copies ran while one was open for 3% of the time, Pallas kernels for 46%

profile of v5, /device:TPU:0, one launch (start us, length us, event | category | flops | bytes accessed | tf_op | source)
XLA Modules:
  0.0 95.2 jit_solution(3238445940994442991)
XLA Ops:
  0.7 3.0 %shard_map.333 = (f32[32,1,256]{2,1,0:T(1,128)}, f32[16,24,384]{2,1,0:T(8,128)}, f32[16,8,384]{2,1,0:T(8,128)}, f32[16,8,384]{2,1,0:T(8,128)}) custom-call(f32[32,16,768]{2,1,0:T(8,128)} %x_ref.3, f32[32,16,768]{2,1,0:T(8,128)} %ct_own.3, f32[32,16,768]{2,1,0:T(8,128)} %ct_own.3), custom_call_target="tpu_custom_call" | custom-call | flops 4000000000 | bytes 1000000 | tf_op jit(solution)/shard_map/pallas_call | solution.py:141
  3.7 2.4 %collective-permute-start = (f32[16,24,384]{2,1,0:T(8,128)}, f32[16,24,384]{2,1,0:T(8,128)S(1)}, u32[]{:S(2)}, u32[]{:S(2)}) collective-permute-start(f32[16,24,384]{2,1,0:T(8,128)} %get-tuple-element.82), channel_id=1, source_target_pairs={{4,0},{8,4},{12,8},{0,12},{20,16},{24,20},{28,24},{16,28},{5,1},{9... | collective-permute-start | bytes 1769480 | tf_op jit(solution)/shard_map/ppermute | solution.py:1004
  6.1 1.5 %collective-permute-start.1 = (f32[16,8,384]{2,1,0:T(8,128)}, f32[16,8,384]{2,1,0:T(8,128)S(1)}, u32[]{:S(2)}, u32[]{:S(2)}) collective-permute-start(f32[16,8,384]{2,1,0:T(8,128)} %get-tuple-element.83), channel_id=1, source_target_pairs={{16,0},{20,4},{24,8},{28,12},{0,16},{4,20},{8,24},{12,28},{17,1},{... | collective-permute-start | bytes 589832 | tf_op jit(solution)/shard_map/ppermute | solution.py:1004
  8.0 4.9 %all-to-all-start = ((f32[32,1,256]{2,1,0:T(1,128)}), f32[32,1,256]{2,1,0:T(1,128)S(1)}, u32[]{:S(2)}, u32[]{:S(2)}) async-start(f32[32,1,256]{2,1,0:T(1,128)} %get-tuple-element.88), calls=%async_computation | async-start | bytes 65536 | tf_op jit(solution)/shard_map/all_to_all | solution.py:1008
  12.9 4.0 %shard_map.332 = (s32[2,32]{1,0:T(2,128)}, f32[8,128]{1,0:T(8,128)}, f32[3,64,128]{2,1,0:T(8,128)}, f32[24,512]{1,0:T(8,128)}, f32[2,512,256]{2,1,0:T(8,128)}, /...) custom-call(f32[3]{0:T(128)} %log_scale_ref.1, ...), custom_call_target="tpu_custom_call" | custom-call | bytes 1000000 | tf_op jit(solution)/shard_map/pallas_call | solution.py:306
  16.9 1.8 %collective-permute-start.4 = (f32[16,8,384]{2,1,0:T(8,128)}, f32[16,8,384]{2,1,0:T(8,128)}, u32[]{:S(2)}, u32[]{:S(2)}) collective-permute-start(f32[16,8,384]{2,1,0:T(8,128)} %get-tuple-element.86), channel_id=1, source_target_pairs={{16,0},{20,4},{24,8},{28,12},{0,16},{4,20},{8,24},{12,28},{17,1},{... | collective-permute-start | bytes 589832 | tf_op jit(solution)/shard_map/ppermute | solution.py:1004
  18.7 0.9 collective-permute-start.5
  19.7 0.8 collective-permute-start.3
  21.1 17.0 %shard_map.334 = (f32[16,12,384]{2,1,0:T(8,128)}, f32[16,12,384]{2,1,0:T(8,128)}, f32[16,24,384]{2,1,0:T(8,128)}, f32[16,8,384]{2,1,0:T(8,128)}, f32[16,8,384]{2...) custom-call(s32[2,32]{1,0:T(2,128)} %get-tuple-element.78.flags_ref,, ...), custom_call_target="tpu_custom_call" | custom-call | flops 40000000000 | bytes 1000000 | tf_op jit(solution)/shard_map/pallas_call | solution.py:818
  38.1 1.5 %collective-permute-start.7 = (f32[16,8,384]{2,1,0:T(8,128)}, f32[16,8,384]{2,1,0:T(8,128)S(1)}, u32[]{:S(2)}, u32[]{:S(2)}) collective-permute-start(f32[16,8,384]{2,1,0:T(8,128)} %get-tuple-element.107), channel_id=1, source_target_pairs={{16,0},{20,4},{24,8},{28,12},{0,16},{4,20},{8,24},{12,28},{17,1},{... | collective-permute-start | bytes 589832 | tf_op jit(solution)/shard_map/ppermute | solution.py:1004
  39.7 0.7 collective-permute-start.6
  40.4 17.5 %shard_map.335 = (f32[16,12,384]{2,1,0:T(8,128)}, f32[16,12,384]{2,1,0:T(8,128)}, f32[16,24,384]{2,1,0:T(8,128)}, f32[16,8,384]{2,1,0:T(8,128)}, f32[16,8,384]{2...) custom-call(s32[2,32]{1,0:T(2,128)} %get-tuple-element.78.flags_ref, s32[32]{0:T(128)} %lead_ref.3, ...), custom_call_target="tpu_custom_call" | custom-call | flops 40000000000 | bytes 1000000 | tf_op jit(solution)/shard_map/pallas_call | solution.py:818
  58.5 1.2 %collective-permute-done.9 = f32[16,32,128]{2,1,0:T(8,128)S(1)} collective-permute-done((f32[16,32,128]{2,1,0:T(8,128)}, f32[16,32,128]{2,1,0:T(8,128)S(1)}, u32[]{:S(2)}, u32[]{:S(2)}) %collective-permute-start.9) | collective-permute-done | bytes 262176 | tf_op jit(solution)/shard_map/ppermute | solution.py:1012
  59.7 1.7 %add.3 = f32[16,32,128]{2,1,0:T(8,128)} add(f32[16,32,128]{2,1,0:T(8,128)} %get-tuple-element.104, f32[16,32,128]{2,1,0:T(8,128)S(1)} %collective-permute-done.9) | non-fusion elementwise | flops 65536 | bytes 786432 | tf_op jit(solution)/shard_map/add | solution.py:1092
  61.4 6.5 %all-to-all-start.1 = ((f32[16,32,128]{2,1,0:T(8,128)}), f32[16,32,128]{2,1,0:T(8,128)S(1)}, u32[]{:S(2)}, u32[]{:S(2)}) async-start(f32[16,32,128]{2,1,0:T(8,128)} %add.3), calls=%async_computation.1 | async-start | bytes 524288 | tf_op jit(solution)/shard_map/all_to_all | solution.py:1008
  68.0 1.9 %collective-permute-start.11 = (f32[16,8,384]{2,1,0:T(8,128)}, f32[16,8,384]{2,1,0:T(8,128)S(1)}, u32[]{:S(2)}, u32[]{:S(2)}) collective-permute-start(f32[16,8,384]{2,1,0:T(8,128)} %get-tuple-element.119), channel_id=1, source_target_pairs={{16,0},{20,4},{24,8},{28,12},{0,16},{4,20},{8,24},{12,28},{17,1},{... | collective-permute-start | bytes 589832 | tf_op jit(solution)/shard_map/ppermute | solution.py:1004
  69.9 9.0 %all-to-all-done.1.slots_ref = f32[16,32,128]{2,1,0:T(8,128)S(1)} async-done(((f32[16,32,128]{2,1,0:T(8,128)}), f32[16,32,128]{2,1,0:T(8,128)S(1)}, u32[]{:S(2)}, u32[]{:S(2)}) %all-to-all-start.1) | async-done | bytes 262176 | tf_op jit(solution)/shard_map/all_to_all | solution.py:1008
  78.9 0.7 shard_map.336.sums_ref
  79.7 3.5 %all-to-all-start.2 = ((f32[16,32,128]{2,1,0:T(8,128)}), f32[16,32,128]{2,1,0:T(8,128)S(1)}, u32[]{:S(2)}, u32[]{:S(2)}) async-start(f32[16,32,128]{2,1,0:T(8,128)} %shard_map.336.sums_ref), calls=%async_computation.2 | async-start | bytes 524288 | tf_op jit(solution)/shard_map/all_to_all | solution.py:1008
  83.3 0.6 copy-done.7
  84.2 4.2 %shard_map.337 = (f32[32,16,768]{2,1,0:T(8,128)}, f32[32,16,768]{2,1,0:T(8,128)}) custom-call(f32[32,16,768]{2,1,0:T(8,128)} %x_ref.3, f32[8,128]{1,0:T(8,128)} %get-tuple-element.110.norm_ref, f32[16,32,128]{2,1,0:T(8,128)} %shard_map.336.sums_ref, f32[16,12,384]{2,1,0:T(8,128)} %get-tuple-element.111.refs_0_, f32[16,12,384]{2,1,0:T(8,128)} %get-tuple-element.112.refs_1_, ...), custom_call_target="tpu_custom_call" | custom-call | flops 60000002048 | bytes 1000000 | tf_op jit(solution)/shard_map/pallas_call | solution.py:884
  88.4 4.2 %all-to-all-done.2.mine_ref = f32[16,32,128]{2,1,0:T(8,128)S(1)} async-done(((f32[16,32,128]{2,1,0:T(8,128)}), f32[16,32,128]{2,1,0:T(8,128)S(1)}, u32[]{:S(2)}, u32[]{:S(2)}) %all-to-all-start.2) | async-done | bytes 262176 | tf_op jit(solution)/shard_map/all_to_all | solution.py:1008
  92.6 1.3 %slice_bitcast_fusion = (f32[96]{0:T(128)}, f32[96]{0:T(128)}) fusion(f32[8,128]{1,0:T(8,128)} %get-tuple-element.110.norm_ref), kind=kLoop, calls=%fused_computation | loop fusion | bytes 1536 | tf_op jit(solution)/shard_map/squeeze | solution.py:1135
  94.2 0.9 shard_map.338
  (37 shorter events, 2.2 us)
Async XLA Ops:
  3.7 13.2 %collective-permute-start = (f32[16,24,384]{2,1,0:T(8,128)}, f32[16,24,384]{2,1,0:T(8,128)S(1)}, u32[]{:S(2)}, u32[]{:S(2)}) collective-permute-start(f32[16,24,384]{2,1,0:T(8,128)} %get-tuple-element.82), channel_id=1, source_target_pairs={{4,0},{8,4},{12,8},{0,12},{20,16},{24,20},{28,24},{16,28},{5,1},{9... | collective-permute-start | bytes 1769480 | tf_op jit(solution)/shard_map/ppermute | solution.py:1004
  6.1 10.8 %collective-permute-start.1 = (f32[16,8,384]{2,1,0:T(8,128)}, f32[16,8,384]{2,1,0:T(8,128)S(1)}, u32[]{:S(2)}, u32[]{:S(2)}) collective-permute-start(f32[16,8,384]{2,1,0:T(8,128)} %get-tuple-element.83), channel_id=1, source_target_pairs={{16,0},{20,4},{24,8},{28,12},{0,16},{4,20},{8,24},{12,28},{17,1},{... | collective-permute-start | bytes 589832 | tf_op jit(solution)/shard_map/ppermute | solution.py:1004
  7.6 9.3 %collective-permute-start.2 = (f32[16,8,384]{2,1,0:T(8,128)}, f32[16,8,384]{2,1,0:T(8,128)S(1)}, u32[]{:S(2)}, u32[]{:S(2)}) collective-permute-start(f32[16,8,384]{2,1,0:T(8,128)} %get-tuple-element.84), channel_id=1, source_target_pairs={{20,0},{24,4},{28,8},{16,12},{4,16},{8,20},{12,24},{0,28},{21,1},{... | collective-permute-start | bytes 589832 | tf_op jit(solution)/shard_map/ppermute | solution.py:1004
  8.0 12.5 %all-to-all-start = ((f32[32,1,256]{2,1,0:T(1,128)}), f32[32,1,256]{2,1,0:T(1,128)S(1)}, u32[]{:S(2)}, u32[]{:S(2)}) async-start(f32[32,1,256]{2,1,0:T(1,128)} %get-tuple-element.88), calls=%async_computation | async-start | bytes 65536 | tf_op jit(solution)/shard_map/all_to_all | solution.py:1008
  16.9 3.6 %copy-start.5 = (f32[16,8,384]{2,1,0:T(8,128)}, f32[16,8,384]{2,1,0:T(8,128)S(1)}, u32[]{:S(2)}) copy-start(f32[16,8,384]{2,1,0:T(8,128)S(1)} %collective-permute-done.1.x_down) | copy-start | bytes 589828
  16.9 3.6 %copy-start.6 = (f32[16,8,384]{2,1,0:T(8,128)}, f32[16,8,384]{2,1,0:T(8,128)S(1)}, u32[]{:S(2)}) copy-start(f32[16,8,384]{2,1,0:T(8,128)S(1)} %collective-permute-done.2.x_corner) | copy-start | bytes 589828
  16.9 3.6 %copy-start.1 = (f32[16,24,384]{2,1,0:T(8,128)}, f32[16,24,384]{2,1,0:T(8,128)S(1)}, u32[]{:S(2)}) copy-start(f32[16,24,384]{2,1,0:T(8,128)S(1)} %collective-permute-done.x_right) | copy-start | bytes 1769476
  16.9 22.7 %collective-permute-start.4 = (f32[16,8,384]{2,1,0:T(8,128)}, f32[16,8,384]{2,1,0:T(8,128)}, u32[]{:S(2)}, u32[]{:S(2)}) collective-permute-start(f32[16,8,384]{2,1,0:T(8,128)} %get-tuple-element.86), channel_id=1, source_target_pairs={{16,0},{20,4},{24,8},{28,12},{0,16},{4,20},{8,24},{12,28},{17,1},{... | collective-permute-start | bytes 589832 | tf_op jit(solution)/shard_map/ppermute | solution.py:1004
  18.7 21.6 %collective-permute-start.5 = (f32[16,8,384]{2,1,0:T(8,128)}, f32[16,8,384]{2,1,0:T(8,128)}, u32[]{:S(2)}, u32[]{:S(2)}) collective-permute-start(f32[16,8,384]{2,1,0:T(8,128)} %get-tuple-element.87), channel_id=1, source_target_pairs={{20,0},{24,4},{28,8},{16,12},{4,16},{8,20},{12,24},{0,28},{21,1},{... | collective-permute-start | bytes 589832 | tf_op jit(solution)/shard_map/ppermute | solution.py:1004
  19.7 20.7 %collective-permute-start.3 = (f32[16,24,384]{2,1,0:T(8,128)}, f32[16,24,384]{2,1,0:T(8,128)}, u32[]{:S(2)}, u32[]{:S(2)}) collective-permute-start(f32[16,24,384]{2,1,0:T(8,128)} %get-tuple-element.85), channel_id=1, source_target_pairs={{4,0},{8,4},{12,8},{0,12},{20,16},{24,20},{28,24},{16,28},{5,1},{9... | collective-permute-start | bytes 1769480 | tf_op jit(solution)/shard_map/ppermute | solution.py:1004
  38.1 19.7 %collective-permute-start.7 = (f32[16,8,384]{2,1,0:T(8,128)}, f32[16,8,384]{2,1,0:T(8,128)S(1)}, u32[]{:S(2)}, u32[]{:S(2)}) collective-permute-start(f32[16,8,384]{2,1,0:T(8,128)} %get-tuple-element.107), channel_id=1, source_target_pairs={{16,0},{20,4},{24,8},{28,12},{0,16},{4,20},{8,24},{12,28},{17,1},{... | collective-permute-start | bytes 589832 | tf_op jit(solution)/shard_map/ppermute | solution.py:1004
  39.7 18.2 %collective-permute-start.8 = (f32[16,8,384]{2,1,0:T(8,128)}, f32[16,8,384]{2,1,0:T(8,128)S(1)}, u32[]{:S(2)}, u32[]{:S(2)}) collective-permute-start(f32[16,8,384]{2,1,0:T(8,128)} %get-tuple-element.108), channel_id=1, source_target_pairs={{28,0},{16,4},{20,8},{24,12},{12,16},{0,20},{4,24},{8,28},{29,1},{... | collective-permute-start | bytes 589832 | tf_op jit(solution)/shard_map/ppermute | solution.py:1004
  39.7 18.2 %collective-permute-start.6 = (f32[16,24,384]{2,1,0:T(8,128)}, f32[16,24,384]{2,1,0:T(8,128)}, u32[]{:S(2)}, u32[]{:S(2)}) collective-permute-start(f32[16,24,384]{2,1,0:T(8,128)} %get-tuple-element.106), channel_id=1, source_target_pairs={{12,0},{0,4},{4,8},{8,12},{28,16},{16,20},{20,24},{24,28},{13,1},{... | collective-permute-start | bytes 1769480 | tf_op jit(solution)/shard_map/ppermute | solution.py:1004
  57.9 25.4 %copy-start.3 = (f32[16,8,384]{2,1,0:T(8,128)}, f32[16,8,384]{2,1,0:T(8,128)S(1)}, u32[]{:S(2)}) copy-start(f32[16,8,384]{2,1,0:T(8,128)S(1)} %collective-permute-done.7.refs_3_) | copy-start | bytes 589828
  57.9 25.4 %copy-start.4 = (f32[16,8,384]{2,1,0:T(8,128)}, f32[16,8,384]{2,1,0:T(8,128)S(1)}, u32[]{:S(2)}) copy-start(f32[16,8,384]{2,1,0:T(8,128)S(1)} %collective-permute-done.8.refs_4_) | copy-start | bytes 589828
  57.9 1.8 %collective-permute-start.9 = (f32[16,32,128]{2,1,0:T(8,128)}, f32[16,32,128]{2,1,0:T(8,128)S(1)}, u32[]{:S(2)}, u32[]{:S(2)}) collective-permute-start(f32[16,32,128]{2,1,0:T(8,128)} %get-tuple-element.109), channel_id=1, source_target_pairs={{0,4},{4,0},{1,5},{5,1},{2,6},{6,2},{3,7},{7,3},{8,12},{12,8},{9,1... | collective-permute-start | bytes 786440 | tf_op jit(solution)/shard_map/ppermute | solution.py:1012
  58.2 25.0 %collective-permute-start.10 = (f32[16,24,384]{2,1,0:T(8,128)}, f32[16,24,384]{2,1,0:T(8,128)S(1)}, u32[]{:S(2)}, u32[]{:S(2)}) collective-permute-start(f32[16,24,384]{2,1,0:T(8,128)} %get-tuple-element.118), channel_id=1, source_target_pairs={{12,0},{0,4},{4,8},{8,12},{28,16},{16,20},{20,24},{24,28},{13,1},{... | collective-permute-start | bytes 1769480 | tf_op jit(solution)/shard_map/ppermute | solution.py:1004
  61.4 17.5 %all-to-all-start.1 = ((f32[16,32,128]{2,1,0:T(8,128)}), f32[16,32,128]{2,1,0:T(8,128)S(1)}, u32[]{:S(2)}, u32[]{:S(2)}) async-start(f32[16,32,128]{2,1,0:T(8,128)} %add.3), calls=%async_computation.1 | async-start | bytes 524288 | tf_op jit(solution)/shard_map/all_to_all | solution.py:1008
  68.0 15.3 %collective-permute-start.11 = (f32[16,8,384]{2,1,0:T(8,128)}, f32[16,8,384]{2,1,0:T(8,128)S(1)}, u32[]{:S(2)}, u32[]{:S(2)}) collective-permute-start(f32[16,8,384]{2,1,0:T(8,128)} %get-tuple-element.119), channel_id=1, source_target_pairs={{16,0},{20,4},{24,8},{28,12},{0,16},{4,20},{8,24},{12,28},{17,1},{... | collective-permute-start | bytes 589832 | tf_op jit(solution)/shard_map/ppermute | solution.py:1004
  69.9 13.4 %collective-permute-start.12 = (f32[16,8,384]{2,1,0:T(8,128)}, f32[16,8,384]{2,1,0:T(8,128)S(1)}, u32[]{:S(2)}, u32[]{:S(2)}) collective-permute-start(f32[16,8,384]{2,1,0:T(8,128)} %get-tuple-element.120), channel_id=1, source_target_pairs={{28,0},{16,4},{20,8},{24,12},{12,16},{0,20},{4,24},{8,28},{29,1},{... | collective-permute-start | bytes 589832 | tf_op jit(solution)/shard_map/ppermute | solution.py:1004
  79.7 13.0 %all-to-all-start.2 = ((f32[16,32,128]{2,1,0:T(8,128)}), f32[16,32,128]{2,1,0:T(8,128)S(1)}, u32[]{:S(2)}, u32[]{:S(2)}) async-start(f32[16,32,128]{2,1,0:T(8,128)} %shard_map.336.sums_ref), calls=%async_computation.2 | async-start | bytes 524288 | tf_op jit(solution)/shard_map/all_to_all | solution.py:1008
  83.2 0.7 copy-start.8
  83.3 0.9 copy-start.2
  92.6 1.5 %collective-permute-start.13 = (f32[16,32,128]{2,1,0:T(8,128)S(1)}, f32[16,32,128]{2,1,0:T(8,128)S(1)}, u32[]{:S(2)}, u32[]{:S(2)}) collective-permute-start(f32[16,32,128]{2,1,0:T(8,128)S(1)} %all-to-all-done.2.mine_ref), channel_id=1, source_target_pairs={{0,4},{4,0},{1,5},{5,1},{2,6},{6,2},{3,7},{7,3},{8,12},{12,8},{9,1... | collective-permute-start | bytes 786440 | tf_op jit(solution)/shard_map/ppermute | solution.py:1012
  (2 other events, 1.3 us)

commit v6 on v5

--- a/solution.py
+++ b/solution.py
@@ -361,7 +361,9 @@
         own_ref, give_ref, norm_ref, affine_ref, flat_ref = refs[:5]
         refs = refs[5:]
     else:
-        affine_ref, refs = refs[-1], refs[:-1]
+        (affine_ref, sums_ref), refs = refs[-2:], refs[:-2]
+        passed_ref = refs[4]
+        refs = (*refs[:4], sums_ref, *refs[5:])
     g_qkv_ref, g_out_ref, g_up_ref, g_down_ref, sums_ref, dpos_ref, dcos_ref = refs
 
     @pl.when(step == 0)
@@ -389,7 +391,7 @@
             )
             norm_ref[4:8] = jnp.zeros((4, LANES), f32)
         for n, ref in enumerate(refs):
-            ref[...] = jnp.zeros_like(ref) if is_first else so_far[n][...]
+            ref[...] = jnp.zeros_like(ref) if is_first or n == 4 else so_far[n][...]
         qkv_f[...] = packed(w_qkv_ref[...].T)
         qkv_b[...] = packed(w_qkv_ref[...])
         out_f[...] = packed(w_out_ref[...].T)
@@ -663,10 +665,11 @@
     for m in range(step_items):
         scatter(of_item(d_normed, m), dn_keep, 1, m)
 
+    def row_sums():
+        rows = [jnp.sum(sums_ref[i].T, 0, keepdims=True) for i in range(11)]
+        return rows if is_first else [r + so_far[4][i : i + 1, :WIDTH] for i, r in enumerate(rows)]
+
     def finish():
-        def lane_sums(v):
-            return jnp.sum(v.T, 0, keepdims=True)
-
         flat_ref[...] = jnp.zeros_like(flat_ref)
         g = g_qkv_ref[...].T
         flat_ref[0:96, :] = g[:WIDTH, :LANES]
@@ -681,7 +684,7 @@
             flat_ref[288 + 96 * k : 384 + 96 * k, :] = g_up[:WIDTH, lanes]
             flat_ref[576 + 96 * k : 672 + 96 * k, :] = g_down[:WIDTH, lanes]
             flat_ref[876 + k : 877 + k, :] = g_up[WIDTH : WIDTH + 1, lanes]
-        totals = [lane_sums(sums_ref[i]) for i in range(11)]
+        totals = row_sums()
         for i in range(8):
             flat_ref[864 + i : 865 + i, :WIDTH] = totals[i]
         flat_ref[872:873, :WIDTH] = totals[8]
@@ -745,6 +748,9 @@
 
     if is_last:
         finish()
+    else:
+        for i, row in enumerate(row_sums()):
+            passed_ref[i : i + 1, :WIDTH] = row
 
 
 totals_shapes = [
@@ -790,6 +796,7 @@
     slot_rows = -(-PAYLOAD // slots)
     slot_rows = -(-(slot_rows + 2) // 8) * 8
     totals = [jax.ShapeDtypeStruct(s, f32) for s in totals_shapes]
+    totals[4] = jax.ShapeDtypeStruct((16, LANES), f32)
     scratch = [pltpu.VMEM((2, WIDTH, LANES), f32)]
     if is_last:
         tail = [
@@ -801,6 +808,7 @@
         scratch += [pltpu.VMEM(s, f32) for s in totals_shapes]
     else:
         tail = totals
+        scratch.append(pltpu.VMEM(totals_shapes[4], f32))
     scratch += [
         pltpu.VMEM((3 * WIDTH, 3 * WIDTH), bf16),
         pltpu.VMEM((WIDTH, 3 * WIDTH), bf16),

time: 95.7 us -> 95.3 us (level)
  transfers between devices with their start and end apart: 17 -> 17, of which waited for: 4 -> 4; matrix products, arithmetic and copies ran while one was open for 3% -> 3% of each run, Pallas kernels for 46% -> 45%
where the time goes in v6:
time: 95.3 us; the launch traced here: 94.8 us
  Pallas kernels  47 us (49%)
  starting transfers between devices  27.5 us (29%)
  waiting for transfers between devices  14.8 us (16%)
  local copies, waits for them, and re-layouts  2.81 us (3%)
  other arithmetic  1.7 us (2%)
  between operations  1.06 us (1%)
    pallas_call x2, Pallas kernels, run_block(): pl.pallas_call(partial(block_kernel, step_items, part * items, float(toke...  34.1 us
    all_to_all x3, starting transfers between devices, exchange(): return lax.all_to_all(slots, axes, 0, 0, tiled=True)  15 us
    all_to_all x3, waiting for transfers between devices, exchange(): return lax.all_to_all(slots, axes, 0, 0, tiled=True)  13.3 us
    ppermute x12, starting transfers between devices, take_from(): return lax.ppermute(block, axes_tiles, route)  12.1 us
    pallas_call x1, Pallas kernels, finish_fields(): pl.pallas_call(partial(final_kernel, float(token_count), part_steps), gri...  4.23 us
    pallas_call x1, Pallas kernels, prepare(): pl.pallas_call(partial(prepare_kernel, PARTS - 1), grid=(1,), in_specs=[p...  3.99 us
    pallas_call x1, Pallas kernels, pack(): pl.pallas_call(partial(pack_kernel, items, part_steps), grid=(steps,), in...  3.05 us
  transfers between devices with their start and end apart: 17, of which 4 were waited for; matrix products, arithmetic and copies ran while one was open for 3% of the time, Pallas kernels for 45%

profile of v6, /device:TPU:0, one launch (start us, length us, event | category | flops | bytes accessed | tf_op | source)
XLA Modules:
  0.0 94.8 jit_solution(10825646278947119932)
XLA Ops:
  0.7 3.0 %shard_map.333 = (f32[32,1,256]{2,1,0:T(1,128)}, f32[16,24,384]{2,1,0:T(8,128)}, f32[16,8,384]{2,1,0:T(8,128)}, f32[16,8,384]{2,1,0:T(8,128)}) custom-call(f32[32,16,768]{2,1,0:T(8,128)} %x_ref.3, f32[32,16,768]{2,1,0:T(8,128)} %ct_own.3, f32[32,16,768]{2,1,0:T(8,128)} %ct_own.3), custom_call_target="tpu_custom_call" | custom-call | flops 4000000000 | bytes 1000000 | tf_op jit(solution)/shard_map/pallas_call | solution.py:141
  3.7 2.4 %collective-permute-start = (f32[16,24,384]{2,1,0:T(8,128)}, f32[16,24,384]{2,1,0:T(8,128)S(1)}, u32[]{:S(2)}, u32[]{:S(2)}) collective-permute-start(f32[16,24,384]{2,1,0:T(8,128)} %get-tuple-element.82), channel_id=1, source_target_pairs={{4,0},{8,4},{12,8},{0,12},{20,16},{24,20},{28,24},{16,28},{5,1},{9... | collective-permute-start | bytes 1769480 | tf_op jit(solution)/shard_map/ppermute | solution.py:1012
  6.1 1.5 %collective-permute-start.1 = (f32[16,8,384]{2,1,0:T(8,128)}, f32[16,8,384]{2,1,0:T(8,128)S(1)}, u32[]{:S(2)}, u32[]{:S(2)}) collective-permute-start(f32[16,8,384]{2,1,0:T(8,128)} %get-tuple-element.83), channel_id=1, source_target_pairs={{16,0},{20,4},{24,8},{28,12},{0,16},{4,20},{8,24},{12,28},{17,1},{... | collective-permute-start | bytes 589832 | tf_op jit(solution)/shard_map/ppermute | solution.py:1012
  8.0 4.9 %all-to-all-start = ((f32[32,1,256]{2,1,0:T(1,128)}), f32[32,1,256]{2,1,0:T(1,128)S(1)}, u32[]{:S(2)}, u32[]{:S(2)}) async-start(f32[32,1,256]{2,1,0:T(1,128)} %get-tuple-element.88), calls=%async_computation | async-start | bytes 65536 | tf_op jit(solution)/shard_map/all_to_all | solution.py:1016
  12.9 4.0 %shard_map.332 = (s32[2,32]{1,0:T(2,128)}, f32[8,128]{1,0:T(8,128)}, f32[3,64,128]{2,1,0:T(8,128)}, f32[24,512]{1,0:T(8,128)}, f32[2,512,256]{2,1,0:T(8,128)}, /...) custom-call(f32[3]{0:T(128)} %log_scale_ref.1, ...), custom_call_target="tpu_custom_call" | custom-call | bytes 1000000 | tf_op jit(solution)/shard_map/pallas_call | solution.py:306
  16.9 1.8 %collective-permute-start.4 = (f32[16,8,384]{2,1,0:T(8,128)}, f32[16,8,384]{2,1,0:T(8,128)}, u32[]{:S(2)}, u32[]{:S(2)}) collective-permute-start(f32[16,8,384]{2,1,0:T(8,128)} %get-tuple-element.86), channel_id=1, source_target_pairs={{16,0},{20,4},{24,8},{28,12},{0,16},{4,20},{8,24},{12,28},{17,1},{... | collective-permute-start | bytes 589832 | tf_op jit(solution)/shard_map/ppermute | solution.py:1012
  18.8 0.9 collective-permute-start.5
  19.7 0.8 collective-permute-start.3
  20.5 0.6 copy-done
  21.1 16.8 %shard_map.334 = (f32[16,12,384]{2,1,0:T(8,128)}, f32[16,12,384]{2,1,0:T(8,128)}, f32[16,24,384]{2,1,0:T(8,128)}, f32[16,8,384]{2,1,0:T(8,128)}, f32[16,8,384]{2...) custom-call(s32[2,32]{1,0:T(2,128)} %get-tuple-element.78.flags_ref,, ...), custom_call_target="tpu_custom_call" | custom-call | flops 40000000000 | bytes 1000000 | tf_op jit(solution)/shard_map/pallas_call | solution.py:826
  37.9 1.5 %collective-permute-start.7 = (f32[16,8,384]{2,1,0:T(8,128)}, f32[16,8,384]{2,1,0:T(8,128)S(1)}, u32[]{:S(2)}, u32[]{:S(2)}) collective-permute-start(f32[16,8,384]{2,1,0:T(8,128)} %get-tuple-element.107), channel_id=1, source_target_pairs={{16,0},{20,4},{24,8},{28,12},{0,16},{4,20},{8,24},{12,28},{17,1},{... | collective-permute-start | bytes 589832 | tf_op jit(solution)/shard_map/ppermute | solution.py:1012
  39.4 0.7 collective-permute-start.6
  40.1 17.3 %shard_map.335 = (f32[16,12,384]{2,1,0:T(8,128)}, f32[16,12,384]{2,1,0:T(8,128)}, f32[16,24,384]{2,1,0:T(8,128)}, f32[16,8,384]{2,1,0:T(8,128)}, f32[16,8,384]{2...) custom-call(s32[2,32]{1,0:T(2,128)} %get-tuple-element.78.flags_ref, s32[32]{0:T(128)} %lead_ref.3, ...), custom_call_target="tpu_custom_call" | custom-call | flops 40000000000 | bytes 1000000 | tf_op jit(solution)/shard_map/pallas_call | solution.py:826
  58.1 1.2 %collective-permute-done.9 = f32[16,32,128]{2,1,0:T(8,128)S(1)} collective-permute-done((f32[16,32,128]{2,1,0:T(8,128)}, f32[16,32,128]{2,1,0:T(8,128)S(1)}, u32[]{:S(2)}, u32[]{:S(2)}) %collective-permute-start.9) | collective-permute-done | bytes 262176 | tf_op jit(solution)/shard_map/ppermute | solution.py:1020
  59.3 1.7 %add.3 = f32[16,32,128]{2,1,0:T(8,128)} add(f32[16,32,128]{2,1,0:T(8,128)} %get-tuple-element.104, f32[16,32,128]{2,1,0:T(8,128)S(1)} %collective-permute-done.9) | non-fusion elementwise | flops 65536 | bytes 786432 | tf_op jit(solution)/shard_map/add | solution.py:1100
  61.0 6.6 %all-to-all-start.1 = ((f32[16,32,128]{2,1,0:T(8,128)}), f32[16,32,128]{2,1,0:T(8,128)S(1)}, u32[]{:S(2)}, u32[]{:S(2)}) async-start(f32[16,32,128]{2,1,0:T(8,128)} %add.3), calls=%async_computation.1 | async-start | bytes 524288 | tf_op jit(solution)/shard_map/all_to_all | solution.py:1016
  67.6 1.9 %collective-permute-start.11 = (f32[16,8,384]{2,1,0:T(8,128)}, f32[16,8,384]{2,1,0:T(8,128)S(1)}, u32[]{:S(2)}, u32[]{:S(2)}) collective-permute-start(f32[16,8,384]{2,1,0:T(8,128)} %get-tuple-element.119), channel_id=1, source_target_pairs={{16,0},{20,4},{24,8},{28,12},{0,16},{4,20},{8,24},{12,28},{17,1},{... | collective-permute-start | bytes 589832 | tf_op jit(solution)/shard_map/ppermute | solution.py:1012
  69.5 9.0 %all-to-all-done.1.slots_ref = f32[16,32,128]{2,1,0:T(8,128)S(1)} async-done(((f32[16,32,128]{2,1,0:T(8,128)}), f32[16,32,128]{2,1,0:T(8,128)S(1)}, u32[]{:S(2)}, u32[]{:S(2)}) %all-to-all-start.1) | async-done | bytes 262176 | tf_op jit(solution)/shard_map/all_to_all | solution.py:1016
  78.5 0.7 shard_map.336.sums_ref
  79.3 3.5 %all-to-all-start.2 = ((f32[16,32,128]{2,1,0:T(8,128)}), f32[16,32,128]{2,1,0:T(8,128)S(1)}, u32[]{:S(2)}, u32[]{:S(2)}) async-start(f32[16,32,128]{2,1,0:T(8,128)} %shard_map.336.sums_ref), calls=%async_computation.2 | async-start | bytes 524288 | tf_op jit(solution)/shard_map/all_to_all | solution.py:1016
  83.8 4.2 %shard_map.337 = (f32[32,16,768]{2,1,0:T(8,128)}, f32[32,16,768]{2,1,0:T(8,128)}) custom-call(f32[32,16,768]{2,1,0:T(8,128)} %x_ref.3, f32[8,128]{1,0:T(8,128)} %get-tuple-element.110.norm_ref, f32[16,32,128]{2,1,0:T(8,128)} %shard_map.336.sums_ref, f32[16,12,384]{2,1,0:T(8,128)} %get-tuple-element.111.refs_0_, f32[16,12,384]{2,1,0:T(8,128)} %get-tuple-element.112.refs_1_, ...), custom_call_target="tpu_custom_call" | custom-call | flops 60000002048 | bytes 1000000 | tf_op jit(solution)/shard_map/pallas_call | solution.py:892
  88.0 4.2 %all-to-all-done.2.mine_ref = f32[16,32,128]{2,1,0:T(8,128)S(1)} async-done(((f32[16,32,128]{2,1,0:T(8,128)}), f32[16,32,128]{2,1,0:T(8,128)S(1)}, u32[]{:S(2)}, u32[]{:S(2)}) %all-to-all-start.2) | async-done | bytes 262176 | tf_op jit(solution)/shard_map/all_to_all | solution.py:1016
  92.3 1.3 %slice_bitcast_fusion = (f32[96]{0:T(128)}, f32[96]{0:T(128)}) fusion(f32[8,128]{1,0:T(8,128)} %get-tuple-element.110.norm_ref), kind=kLoop, calls=%fused_computation | loop fusion | bytes 1536 | tf_op jit(solution)/shard_map/squeeze | solution.py:1143
  93.8 0.9 shard_map.338
  (37 shorter events, 2.2 us)
Async XLA Ops:
  3.7 13.2 %collective-permute-start = (f32[16,24,384]{2,1,0:T(8,128)}, f32[16,24,384]{2,1,0:T(8,128)S(1)}, u32[]{:S(2)}, u32[]{:S(2)}) collective-permute-start(f32[16,24,384]{2,1,0:T(8,128)} %get-tuple-element.82), channel_id=1, source_target_pairs={{4,0},{8,4},{12,8},{0,12},{20,16},{24,20},{28,24},{16,28},{5,1},{9... | collective-permute-start | bytes 1769480 | tf_op jit(solution)/shard_map/ppermute | solution.py:1012
  6.1 10.8 %collective-permute-start.1 = (f32[16,8,384]{2,1,0:T(8,128)}, f32[16,8,384]{2,1,0:T(8,128)S(1)}, u32[]{:S(2)}, u32[]{:S(2)}) collective-permute-start(f32[16,8,384]{2,1,0:T(8,128)} %get-tuple-element.83), channel_id=1, source_target_pairs={{16,0},{20,4},{24,8},{28,12},{0,16},{4,20},{8,24},{12,28},{17,1},{... | collective-permute-start | bytes 589832 | tf_op jit(solution)/shard_map/ppermute | solution.py:1012
  7.6 9.3 %collective-permute-start.2 = (f32[16,8,384]{2,1,0:T(8,128)}, f32[16,8,384]{2,1,0:T(8,128)S(1)}, u32[]{:S(2)}, u32[]{:S(2)}) collective-permute-start(f32[16,8,384]{2,1,0:T(8,128)} %get-tuple-element.84), channel_id=1, source_target_pairs={{20,0},{24,4},{28,8},{16,12},{4,16},{8,20},{12,24},{0,28},{21,1},{... | collective-permute-start | bytes 589832 | tf_op jit(solution)/shard_map/ppermute | solution.py:1012
  8.0 12.5 %all-to-all-start = ((f32[32,1,256]{2,1,0:T(1,128)}), f32[32,1,256]{2,1,0:T(1,128)S(1)}, u32[]{:S(2)}, u32[]{:S(2)}) async-start(f32[32,1,256]{2,1,0:T(1,128)} %get-tuple-element.88), calls=%async_computation | async-start | bytes 65536 | tf_op jit(solution)/shard_map/all_to_all | solution.py:1016
  16.9 3.6 %copy-start.5 = (f32[16,8,384]{2,1,0:T(8,128)}, f32[16,8,384]{2,1,0:T(8,128)S(1)}, u32[]{:S(2)}) copy-start(f32[16,8,384]{2,1,0:T(8,128)S(1)} %collective-permute-done.1.x_down) | copy-start | bytes 589828
  16.9 3.6 %copy-start.6 = (f32[16,8,384]{2,1,0:T(8,128)}, f32[16,8,384]{2,1,0:T(8,128)S(1)}, u32[]{:S(2)}) copy-start(f32[16,8,384]{2,1,0:T(8,128)S(1)} %collective-permute-done.2.x_corner) | copy-start | bytes 589828
  16.9 3.6 %copy-start.1 = (f32[16,24,384]{2,1,0:T(8,128)}, f32[16,24,384]{2,1,0:T(8,128)S(1)}, u32[]{:S(2)}) copy-start(f32[16,24,384]{2,1,0:T(8,128)S(1)} %collective-permute-done.x_right) | copy-start | bytes 1769476
  16.9 22.5 %collective-permute-start.4 = (f32[16,8,384]{2,1,0:T(8,128)}, f32[16,8,384]{2,1,0:T(8,128)}, u32[]{:S(2)}, u32[]{:S(2)}) collective-permute-start(f32[16,8,384]{2,1,0:T(8,128)} %get-tuple-element.86), channel_id=1, source_target_pairs={{16,0},{20,4},{24,8},{28,12},{0,16},{4,20},{8,24},{12,28},{17,1},{... | collective-permute-start | bytes 589832 | tf_op jit(solution)/shard_map/ppermute | solution.py:1012
  18.8 21.3 %collective-permute-start.5 = (f32[16,8,384]{2,1,0:T(8,128)}, f32[16,8,384]{2,1,0:T(8,128)}, u32[]{:S(2)}, u32[]{:S(2)}) collective-permute-start(f32[16,8,384]{2,1,0:T(8,128)} %get-tuple-element.87), channel_id=1, source_target_pairs={{20,0},{24,4},{28,8},{16,12},{4,16},{8,20},{12,24},{0,28},{21,1},{... | collective-permute-start | bytes 589832 | tf_op jit(solution)/shard_map/ppermute | solution.py:1012
  19.7 20.4 %collective-permute-start.3 = (f32[16,24,384]{2,1,0:T(8,128)}, f32[16,24,384]{2,1,0:T(8,128)}, u32[]{:S(2)}, u32[]{:S(2)}) collective-permute-start(f32[16,24,384]{2,1,0:T(8,128)} %get-tuple-element.85), channel_id=1, source_target_pairs={{4,0},{8,4},{12,8},{0,12},{20,16},{24,20},{28,24},{16,28},{5,1},{9... | collective-permute-start | bytes 1769480 | tf_op jit(solution)/shard_map/ppermute | solution.py:1012
  37.9 19.5 %collective-permute-start.7 = (f32[16,8,384]{2,1,0:T(8,128)}, f32[16,8,384]{2,1,0:T(8,128)S(1)}, u32[]{:S(2)}, u32[]{:S(2)}) collective-permute-start(f32[16,8,384]{2,1,0:T(8,128)} %get-tuple-element.107), channel_id=1, source_target_pairs={{16,0},{20,4},{24,8},{28,12},{0,16},{4,20},{8,24},{12,28},{17,1},{... | collective-permute-start | bytes 589832 | tf_op jit(solution)/shard_map/ppermute | solution.py:1012
  39.4 18.0 %collective-permute-start.8 = (f32[16,8,384]{2,1,0:T(8,128)}, f32[16,8,384]{2,1,0:T(8,128)S(1)}, u32[]{:S(2)}, u32[]{:S(2)}) collective-permute-start(f32[16,8,384]{2,1,0:T(8,128)} %get-tuple-element.108), channel_id=1, source_target_pairs={{28,0},{16,4},{20,8},{24,12},{12,16},{0,20},{4,24},{8,28},{29,1},{... | collective-permute-start | bytes 589832 | tf_op jit(solution)/shard_map/ppermute | solution.py:1012
  39.4 18.0 %collective-permute-start.6 = (f32[16,24,384]{2,1,0:T(8,128)}, f32[16,24,384]{2,1,0:T(8,128)}, u32[]{:S(2)}, u32[]{:S(2)}) collective-permute-start(f32[16,24,384]{2,1,0:T(8,128)} %get-tuple-element.106), channel_id=1, source_target_pairs={{12,0},{0,4},{4,8},{8,12},{28,16},{16,20},{20,24},{24,28},{13,1},{... | collective-permute-start | bytes 1769480 | tf_op jit(solution)/shard_map/ppermute | solution.py:1012
  57.4 25.5 %copy-start.3 = (f32[16,8,384]{2,1,0:T(8,128)}, f32[16,8,384]{2,1,0:T(8,128)S(1)}, u32[]{:S(2)}) copy-start(f32[16,8,384]{2,1,0:T(8,128)S(1)} %collective-permute-done.7.refs_3_) | copy-start | bytes 589828
  57.5 25.4 %copy-start.4 = (f32[16,8,384]{2,1,0:T(8,128)}, f32[16,8,384]{2,1,0:T(8,128)S(1)}, u32[]{:S(2)}) copy-start(f32[16,8,384]{2,1,0:T(8,128)S(1)} %collective-permute-done.8.refs_4_) | copy-start | bytes 589828
  57.5 1.8 %collective-permute-start.9 = (f32[16,32,128]{2,1,0:T(8,128)}, f32[16,32,128]{2,1,0:T(8,128)S(1)}, u32[]{:S(2)}, u32[]{:S(2)}) collective-permute-start(f32[16,32,128]{2,1,0:T(8,128)} %get-tuple-element.109), channel_id=1, source_target_pairs={{0,4},{4,0},{1,5},{5,1},{2,6},{6,2},{3,7},{7,3},{8,12},{12,8},{9,1... | collective-permute-start | bytes 786440 | tf_op jit(solution)/shard_map/ppermute | solution.py:1020
  57.9 25.0 %collective-permute-start.10 = (f32[16,24,384]{2,1,0:T(8,128)}, f32[16,24,384]{2,1,0:T(8,128)S(1)}, u32[]{:S(2)}, u32[]{:S(2)}) collective-permute-start(f32[16,24,384]{2,1,0:T(8,128)} %get-tuple-element.118), channel_id=1, source_target_pairs={{12,0},{0,4},{4,8},{8,12},{28,16},{16,20},{20,24},{24,28},{13,1},{... | collective-permute-start | bytes 1769480 | tf_op jit(solution)/shard_map/ppermute | solution.py:1012
  61.0 17.6 %all-to-all-start.1 = ((f32[16,32,128]{2,1,0:T(8,128)}), f32[16,32,128]{2,1,0:T(8,128)S(1)}, u32[]{:S(2)}, u32[]{:S(2)}) async-start(f32[16,32,128]{2,1,0:T(8,128)} %add.3), calls=%async_computation.1 | async-start | bytes 524288 | tf_op jit(solution)/shard_map/all_to_all | solution.py:1016
  67.6 15.3 %collective-permute-start.11 = (f32[16,8,384]{2,1,0:T(8,128)}, f32[16,8,384]{2,1,0:T(8,128)S(1)}, u32[]{:S(2)}, u32[]{:S(2)}) collective-permute-start(f32[16,8,384]{2,1,0:T(8,128)} %get-tuple-element.119), channel_id=1, source_target_pairs={{16,0},{20,4},{24,8},{28,12},{0,16},{4,20},{8,24},{12,28},{17,1},{... | collective-permute-start | bytes 589832 | tf_op jit(solution)/shard_map/ppermute | solution.py:1012
  69.5 13.4 %collective-permute-start.12 = (f32[16,8,384]{2,1,0:T(8,128)}, f32[16,8,384]{2,1,0:T(8,128)S(1)}, u32[]{:S(2)}, u32[]{:S(2)}) collective-permute-start(f32[16,8,384]{2,1,0:T(8,128)} %get-tuple-element.120), channel_id=1, source_target_pairs={{28,0},{16,4},{20,8},{24,12},{12,16},{0,20},{4,24},{8,28},{29,1},{... | collective-permute-start | bytes 589832 | tf_op jit(solution)/shard_map/ppermute | solution.py:1012
  79.3 13.0 %all-to-all-start.2 = ((f32[16,32,128]{2,1,0:T(8,128)}), f32[16,32,128]{2,1,0:T(8,128)S(1)}, u32[]{:S(2)}, u32[]{:S(2)}) async-start(f32[16,32,128]{2,1,0:T(8,128)} %shard_map.336.sums_ref), calls=%async_computation.2 | async-start | bytes 524288 | tf_op jit(solution)/shard_map/all_to_all | solution.py:1016
  82.9 0.7 copy-start.8
  82.9 0.9 copy-start.2
  92.2 1.5 %collective-permute-start.13 = (f32[16,32,128]{2,1,0:T(8,128)S(1)}, f32[16,32,128]{2,1,0:T(8,128)S(1)}, u32[]{:S(2)}, u32[]{:S(2)}) collective-permute-start(f32[16,32,128]{2,1,0:T(8,128)S(1)} %all-to-all-done.2.mine_ref), channel_id=1, source_target_pairs={{0,4},{4,0},{1,5},{5,1},{2,6},{6,2},{3,7},{7,3},{8,12},{12,8},{9,1... | collective-permute-start | bytes 786440 | tf_op jit(solution)/shard_map/ppermute | solution.py:1020
  (2 other events, 1.3 us)

commit v7 on v6

--- a/solution.py
+++ b/solution.py
@@ -226,10 +226,10 @@
     target_ref,
     *refs,
 ):
-    given, (flags_ref, scale_ref, bias_ref, vec_ref, net_ref, gate_ref), sent = (
+    given, (flags_ref, scale_ref, bias_ref, vec_ref, gate_ref), sent = (
         refs[: 4 * part_refs],
-        refs[4 * part_refs : 4 * part_refs + 6],
-        refs[4 * part_refs + 6 :],
+        refs[4 * part_refs : 4 * part_refs + 5],
+        refs[4 * part_refs + 5 :],
     )
     for n in range(part_refs):
         x_ref, ct_ref, x_top_ref, ct_top_ref = given[4 * n : 4 * n + 4]
@@ -257,10 +257,8 @@
     net = jnp.concatenate([w1_ref[...], row(b1_ref), w2_ref[...], jnp.zeros((2, units), f32)], 0)
     vec_ref[16:24, :] = net
     lanes = lax.broadcasted_iota(jnp.int32, (1, LANES), 1)
-    hidden, slope = bias_net(net, coords_ref[...])
+    hidden, _ = bias_net(net, coords_ref[...])
     gate = 1.0 / (1.0 + jnp.exp(-exact(head_rows(net), hidden)))
-    net_ref[0] = hidden
-    net_ref[1] = slope
     gate_ref[...] = 16.0 * gate * (1.0 - gate)
     spots = one_hot(target_ref[...])
     tiles = add_parts(dot(three_parts(16.0 * gate), spots))
@@ -287,7 +285,6 @@
         (8, LANES),
         (HEADS, PLACES, LANES),
         (24, units),
-        (2, units, OFFSETS),
         (8, OFFSETS),
     ]
     shapes = [jax.ShapeDtypeStruct(a, f32) for a in shapes]
@@ -312,7 +309,7 @@
         cost_estimate=about(0),
         compiler_params=in_order,
     )(log_scale, *inputs, *([x, ct, x, ct] * (PARTS - 1)))
-    return made[:6], [made[6 + 3 * n : 9 + 3 * n] for n in range(PARTS - 1)]
+    return made[:5], [made[5 + 3 * n : 8 + 3 * n] for n in range(PARTS - 1)]
 
 
 def packed(w):
@@ -350,7 +347,7 @@
 ):
     step = pl.program_id(0)
     if is_last:
-        (net_ref, gate_ref, coords_ref, target_ref), refs = refs[:4], refs[4:]
+        (gate_ref, coords_ref, target_ref), refs = refs[:3], refs[3:]
     refs, scratch = refs[:-11], refs[-11:]
     qkv_f, out_f, up_f, down_f, down_b, up_b, out_b, qkv_b, cols_ref, up_cols_ref, bias_ref = scratch
     count = len(totals_shapes)
@@ -562,11 +559,14 @@
     f_hi, f_lo = split(first)
 
     up_bias = jnp.concatenate([up_cols_ref[...]] * step_items, 1)
-    u = product(up_f, f_hi, f_lo) + up_bias
-    phi, bell = normal_parts(u)
-    hidden = u * phi
-    slope = phi + bell
-    h_hi, h_lo = split(hidden)
+    size = HIDDEN // 2 if is_first else HIDDEN
+    slopes, h_parts = [], []
+    for c in range(0, HIDDEN, size):
+        u = product(up_f.at[c : c + size, :], f_hi, f_lo) + up_bias[c : c + size]
+        phi, bell = normal_parts(u)
+        slopes.append(phi + bell)
+        h_parts.append(split(u * phi))
+    h_hi, h_lo = (jnp.concatenate(p, 0) for p in zip(*h_parts))
     branch = product(down_f, h_hi, h_lo) + spread_cols(3)
     hat, rstd = layer_norm(branch)
     gain1 = gain(8)
@@ -607,8 +607,11 @@
     sums_ref[8] += add_items(d_branch)
     z_hi, z_lo = split(d_branch)
     g_down_ref[...] += outer(h_hi, h_lo, z_hi, z_lo)
-    d_pre = product(down_b, z_hi, z_lo) * slope
-    p_hi, p_lo = split(d_pre)
+    p_parts = [
+        split(product(down_b.at[c : c + size, :], z_hi, z_lo) * slopes[c // size])
+        for c in range(0, HIDDEN, size)
+    ]
+    p_hi, p_lo = (jnp.concatenate(p, 0) for p in zip(*p_parts))
     g_up_ref[...] += outer(p_hi, p_lo, f_hi, f_lo)
     d_first = cot + product(up_b, p_hi, p_lo)
     d_attn = norm_back(d_first, attn_hat, attn_rstd, gain0, 0)
@@ -718,10 +721,11 @@
             r = dot_rows(both, u_hi)
             return r[:8] + r[8:] + dot_rows(v_hi, u_lo)
 
-        g_w2 = against(d_logit, net_ref[0])
+        hidden_units, unit_slope = bias_net(vec_ref[16:24, :], coords_ref[...])
+        g_w2 = against(d_logit, hidden_units)
         column = net_columns(vec_ref[16:24, :])
         d_hidden = sum(column(3 + h) * d_logit[h : h + 1] for h in range(HEADS))
-        g_first = against(coords_ref[...], d_hidden * net_ref[1])
+        g_first = against(coords_ref[...], d_hidden * unit_slope)
         for i, row in enumerate(
             [g_first[0:1], g_first[1:2], g_first[2:3], g_w2[0:1], g_w2[1:2], g_w2[2:3]]
         ):
@@ -1064,7 +1068,7 @@
     coords, target = offset_constants()
     weights = (query_key_value_weight, output_weight, up_weight, down_weight)
     corners = regions.transpose(1, 2, 0)
-    (flags, *prepared, net, gate), sent_later = prepare(
+    (flags, *prepared, gate), sent_later = prepare(
         inputs, cotangent, log_cosine_scale, corners, vectors, coords, target
     )
     halos = []
@@ -1074,7 +1078,7 @@
                 ((right, down, corner), halos[-1])
             )
         halos.append((take_from(right, 0, 1), take_from(down, 1, 0), take_from(corner, 1, 1)))
-    bias_net_parts = (net, gate, coords, target)
+    bias_net_parts = (gate, coords, target)
     totals, out_parts, dn_parts, home = [], [], [], []
     for part in range(PARTS):
         out_keep, dn_keep, right, down, corner, *totals = run_block(

time: 95.3 us -> 95 us (level)
  transfers between devices with their start and end apart: 17 -> 17, of which waited for: 4 -> 5; matrix products, arithmetic and copies ran while one was open for 3% -> 3% of each run, Pallas kernels for 45% -> 45%
where the time goes in v7:
time: 95 us; the launch traced here: 94.5 us
  Pallas kernels  46.2 us (49%)
  starting transfers between devices  27.2 us (29%)
  waiting for transfers between devices  15.5 us (16%)
  local copies, waits for them, and re-layouts  2.84 us (3%)
  other arithmetic  1.69 us (2%)
  between operations  1.04 us (1%)
    pallas_call x2, Pallas kernels, run_block(): pl.pallas_call(partial(block_kernel, step_items, part * items, float(toke...  33.7 us
    all_to_all x3, starting transfers between devices, exchange(): return lax.all_to_all(slots, axes, 0, 0, tiled=True)  14.3 us
    all_to_all x3, waiting for transfers between devices, exchange(): return lax.all_to_all(slots, axes, 0, 0, tiled=True)  14 us
    ppermute x12, starting transfers between devices, take_from(): return lax.ppermute(block, axes_tiles, route)  12.2 us
    pallas_call x1, Pallas kernels, finish_fields(): pl.pallas_call(partial(final_kernel, float(token_count), part_steps), gri...  4.23 us
    pallas_call x1, Pallas kernels, prepare(): pl.pallas_call(partial(prepare_kernel, PARTS - 1), grid=(1,), in_specs=[p...  3.65 us
    pallas_call x1, Pallas kernels, pack(): pl.pallas_call(partial(pack_kernel, items, part_steps), grid=(steps,), in...  3.05 us
  transfers between devices with their start and end apart: 17, of which 5 were waited for; matrix products, arithmetic and copies ran while one was open for 3% of the time, Pallas kernels for 45%

profile of v7, /device:TPU:0, one launch (start us, length us, event | category | flops | bytes accessed | tf_op | source)
XLA Modules:
  0.0 94.5 jit_solution(6262705011402377384)
XLA Ops:
  0.7 3.0 %shard_map.333 = (f32[32,1,256]{2,1,0:T(1,128)}, f32[16,24,384]{2,1,0:T(8,128)}, f32[16,8,384]{2,1,0:T(8,128)}, f32[16,8,384]{2,1,0:T(8,128)}) custom-call(f32[32,16,768]{2,1,0:T(8,128)} %x_ref.3, f32[32,16,768]{2,1,0:T(8,128)} %ct_own.3, f32[32,16,768]{2,1,0:T(8,128)} %ct_own.3), custom_call_target="tpu_custom_call" | custom-call | flops 4000000000 | bytes 1000000 | tf_op jit(solution)/shard_map/pallas_call | solution.py:141
  3.7 2.4 %collective-permute-start = (f32[16,24,384]{2,1,0:T(8,128)}, f32[16,24,384]{2,1,0:T(8,128)S(1)}, u32[]{:S(2)}, u32[]{:S(2)}) collective-permute-start(f32[16,24,384]{2,1,0:T(8,128)} %get-tuple-element.81), channel_id=1, source_target_pairs={{4,0},{8,4},{12,8},{0,12},{20,16},{24,20},{28,24},{16,28},{5,1},{9... | collective-permute-start | bytes 1769480 | tf_op jit(solution)/shard_map/ppermute | solution.py:1016
  6.1 1.5 %collective-permute-start.1 = (f32[16,8,384]{2,1,0:T(8,128)}, f32[16,8,384]{2,1,0:T(8,128)S(1)}, u32[]{:S(2)}, u32[]{:S(2)}) collective-permute-start(f32[16,8,384]{2,1,0:T(8,128)} %get-tuple-element.82), channel_id=1, source_target_pairs={{16,0},{20,4},{24,8},{28,12},{0,16},{4,20},{8,24},{12,28},{17,1},{... | collective-permute-start | bytes 589832 | tf_op jit(solution)/shard_map/ppermute | solution.py:1016
  8.0 4.9 %all-to-all-start = ((f32[32,1,256]{2,1,0:T(1,128)}), f32[32,1,256]{2,1,0:T(1,128)S(1)}, u32[]{:S(2)}, u32[]{:S(2)}) async-start(f32[32,1,256]{2,1,0:T(1,128)} %get-tuple-element.87), calls=%async_computation | async-start | bytes 65536 | tf_op jit(solution)/shard_map/all_to_all | solution.py:1020
  12.9 3.6 %shard_map.332 = (s32[2,32]{1,0:T(2,128)}, f32[8,128]{1,0:T(8,128)}, f32[3,64,128]{2,1,0:T(8,128)}, f32[24,512]{1,0:T(8,128)}, f32[8,256]{1,0:T(8,128)}, /*index...) custom-call(f32[3]{0:T(128)} %log_scale_ref.1, s32[16,8,32]{2,1,0:T(8,128)} %bitcast.14, ...), custom_call_target="tpu_custom_call" | custom-call | bytes 1000000 | tf_op jit(solution)/shard_map/pallas_call | solution.py:303
  16.6 1.6 %collective-permute-start.3 = (f32[16,24,384]{2,1,0:T(8,128)}, f32[16,24,384]{2,1,0:T(8,128)}, u32[]{:S(2)}, u32[]{:S(2)}) collective-permute-start(f32[16,24,384]{2,1,0:T(8,128)} %get-tuple-element.84), channel_id=1, source_target_pairs={{4,0},{8,4},{12,8},{0,12},{20,16},{24,20},{28,24},{16,28},{5,1},{9... | collective-permute-start | bytes 1769480 | tf_op jit(solution)/shard_map/ppermute | solution.py:1016
  18.2 1.6 %collective-permute-start.4 = (f32[16,8,384]{2,1,0:T(8,128)}, f32[16,8,384]{2,1,0:T(8,128)}, u32[]{:S(2)}, u32[]{:S(2)}) collective-permute-start(f32[16,8,384]{2,1,0:T(8,128)} %get-tuple-element.85), channel_id=1, source_target_pairs={{16,0},{20,4},{24,8},{28,12},{0,16},{4,20},{8,24},{12,28},{17,1},{... | collective-permute-start | bytes 589832 | tf_op jit(solution)/shard_map/ppermute | solution.py:1016
  20.8 16.4 %shard_map.334 = (f32[16,12,384]{2,1,0:T(8,128)}, f32[16,12,384]{2,1,0:T(8,128)}, f32[16,24,384]{2,1,0:T(8,128)}, f32[16,8,384]{2,1,0:T(8,128)}, f32[16,8,384]{2...) custom-call(s32[2,32]{1,0:T(2,128)} %get-tuple-element.77.flags_ref,, ...), custom_call_target="tpu_custom_call" | custom-call | flops 40000000000 | bytes 1000000 | tf_op jit(solution)/shard_map/pallas_call | solution.py:830
  37.4 1.6 %collective-permute-start.7 = (f32[16,8,384]{2,1,0:T(8,128)}, f32[16,8,384]{2,1,0:T(8,128)S(1)}, u32[]{:S(2)}, u32[]{:S(2)}) collective-permute-start(f32[16,8,384]{2,1,0:T(8,128)} %get-tuple-element.105), channel_id=1, source_target_pairs={{16,0},{20,4},{24,8},{28,12},{0,16},{4,20},{8,24},{12,28},{17,1},{... | collective-permute-start | bytes 589832 | tf_op jit(solution)/shard_map/ppermute | solution.py:1016
  39.0 0.9 collective-permute-start.8
  39.9 17.3 %shard_map.335 = (f32[16,12,384]{2,1,0:T(8,128)}, f32[16,12,384]{2,1,0:T(8,128)}, f32[16,24,384]{2,1,0:T(8,128)}, f32[16,8,384]{2,1,0:T(8,128)}, f32[16,8,384]{2...) custom-call(s32[2,32]{1,0:T(2,128)} %get-tuple-element.77.flags_ref, s32[32]{0:T(128)} %lead_ref.3, ...), custom_call_target="tpu_custom_call" | custom-call | flops 40000000000 | bytes 1000000 | tf_op jit(solution)/shard_map/pallas_call | solution.py:830
  57.2 0.7 collective-permute-start.9
  58.0 1.3 %collective-permute-done.9 = f32[16,32,128]{2,1,0:T(8,128)S(1)} collective-permute-done((f32[16,32,128]{2,1,0:T(8,128)}, f32[16,32,128]{2,1,0:T(8,128)S(1)}, u32[]{:S(2)}, u32[]{:S(2)}) %collective-permute-start.9) | collective-permute-done | bytes 262176 | tf_op jit(solution)/shard_map/ppermute | solution.py:1024
  59.4 1.7 %add.3 = f32[16,32,128]{2,1,0:T(8,128)} add(f32[16,32,128]{2,1,0:T(8,128)} %get-tuple-element.102, f32[16,32,128]{2,1,0:T(8,128)S(1)} %collective-permute-done.9) | non-fusion elementwise | flops 65536 | bytes 786432 | tf_op jit(solution)/shard_map/add | solution.py:1104
  61.0 5.8 %all-to-all-start.1 = ((f32[16,32,128]{2,1,0:T(8,128)}), f32[16,32,128]{2,1,0:T(8,128)S(1)}, u32[]{:S(2)}, u32[]{:S(2)}) async-start(f32[16,32,128]{2,1,0:T(8,128)} %add.3), calls=%async_computation.1 | async-start | bytes 524288 | tf_op jit(solution)/shard_map/all_to_all | solution.py:1020
  66.9 1.9 %collective-permute-start.11 = (f32[16,8,384]{2,1,0:T(8,128)}, f32[16,8,384]{2,1,0:T(8,128)S(1)}, u32[]{:S(2)}, u32[]{:S(2)}) collective-permute-start(f32[16,8,384]{2,1,0:T(8,128)} %get-tuple-element.117), channel_id=1, source_target_pairs={{16,0},{20,4},{24,8},{28,12},{0,16},{4,20},{8,24},{12,28},{17,1},{... | collective-permute-start | bytes 589832 | tf_op jit(solution)/shard_map/ppermute | solution.py:1016
  68.8 9.3 %all-to-all-done.1.slots_ref = f32[16,32,128]{2,1,0:T(8,128)S(1)} async-done(((f32[16,32,128]{2,1,0:T(8,128)}), f32[16,32,128]{2,1,0:T(8,128)S(1)}, u32[]{:S(2)}, u32[]{:S(2)}) %all-to-all-start.1) | async-done | bytes 262176 | tf_op jit(solution)/shard_map/all_to_all | solution.py:1020
  78.1 0.7 shard_map.336.sums_ref
  78.8 3.5 %all-to-all-start.2 = ((f32[16,32,128]{2,1,0:T(8,128)}), f32[16,32,128]{2,1,0:T(8,128)S(1)}, u32[]{:S(2)}, u32[]{:S(2)}) async-start(f32[16,32,128]{2,1,0:T(8,128)} %shard_map.336.sums_ref), calls=%async_computation.2 | async-start | bytes 524288 | tf_op jit(solution)/shard_map/all_to_all | solution.py:1020
  82.5 0.6 copy-done.7
  83.4 4.2 %shard_map.337 = (f32[32,16,768]{2,1,0:T(8,128)}, f32[32,16,768]{2,1,0:T(8,128)}) custom-call(f32[32,16,768]{2,1,0:T(8,128)} %x_ref.3, f32[8,128]{1,0:T(8,128)} %get-tuple-element.108.norm_ref, f32[16,32,128]{2,1,0:T(8,128)} %shard_map.336.sums_ref, f32[16,12,384]{2,1,0:T(8,128)} %get-tuple-element.109.refs_0_, f32[16,12,384]{2,1,0:T(8,128)} %get-tuple-element.110.refs_1_, ...), custom_call_target="tpu_custom_call" | custom-call | flops 60000002048 | bytes 1000000 | tf_op jit(solution)/shard_map/pallas_call | solution.py:896
  87.6 4.3 %all-to-all-done.2.mine_ref = f32[16,32,128]{2,1,0:T(8,128)S(1)} async-done(((f32[16,32,128]{2,1,0:T(8,128)}), f32[16,32,128]{2,1,0:T(8,128)S(1)}, u32[]{:S(2)}, u32[]{:S(2)}) %all-to-all-start.2) | async-done | bytes 262176 | tf_op jit(solution)/shard_map/all_to_all | solution.py:1020
  92.0 1.3 %slice_bitcast_fusion = (f32[96]{0:T(128)}, f32[96]{0:T(128)}) fusion(f32[8,128]{1,0:T(8,128)} %get-tuple-element.108.norm_ref), kind=kLoop, calls=%fused_computation | loop fusion | bytes 1536 | tf_op jit(solution)/shard_map/squeeze | solution.py:1147
  93.5 0.9 shard_map.338
  (37 shorter events, 2.3 us)
Async XLA Ops:
  3.7 12.9 %collective-permute-start = (f32[16,24,384]{2,1,0:T(8,128)}, f32[16,24,384]{2,1,0:T(8,128)S(1)}, u32[]{:S(2)}, u32[]{:S(2)}) collective-permute-start(f32[16,24,384]{2,1,0:T(8,128)} %get-tuple-element.81), channel_id=1, source_target_pairs={{4,0},{8,4},{12,8},{0,12},{20,16},{24,20},{28,24},{16,28},{5,1},{9... | collective-permute-start | bytes 1769480 | tf_op jit(solution)/shard_map/ppermute | solution.py:1016
  6.1 10.4 %collective-permute-start.1 = (f32[16,8,384]{2,1,0:T(8,128)}, f32[16,8,384]{2,1,0:T(8,128)S(1)}, u32[]{:S(2)}, u32[]{:S(2)}) collective-permute-start(f32[16,8,384]{2,1,0:T(8,128)} %get-tuple-element.82), channel_id=1, source_target_pairs={{16,0},{20,4},{24,8},{28,12},{0,16},{4,20},{8,24},{12,28},{17,1},{... | collective-permute-start | bytes 589832 | tf_op jit(solution)/shard_map/ppermute | solution.py:1016
  7.6 8.9 %collective-permute-start.2 = (f32[16,8,384]{2,1,0:T(8,128)}, f32[16,8,384]{2,1,0:T(8,128)S(1)}, u32[]{:S(2)}, u32[]{:S(2)}) collective-permute-start(f32[16,8,384]{2,1,0:T(8,128)} %get-tuple-element.83), channel_id=1, source_target_pairs={{20,0},{24,4},{28,8},{16,12},{4,16},{8,20},{12,24},{0,28},{21,1},{... | collective-permute-start | bytes 589832 | tf_op jit(solution)/shard_map/ppermute | solution.py:1016
  8.0 12.2 %all-to-all-start = ((f32[32,1,256]{2,1,0:T(1,128)}), f32[32,1,256]{2,1,0:T(1,128)S(1)}, u32[]{:S(2)}, u32[]{:S(2)}) async-start(f32[32,1,256]{2,1,0:T(1,128)} %get-tuple-element.87), calls=%async_computation | async-start | bytes 65536 | tf_op jit(solution)/shard_map/all_to_all | solution.py:1020
  16.5 3.6 %copy-start.5 = (f32[16,8,384]{2,1,0:T(8,128)}, f32[16,8,384]{2,1,0:T(8,128)S(1)}, u32[]{:S(2)}) copy-start(f32[16,8,384]{2,1,0:T(8,128)S(1)} %collective-permute-done.1.x_down) | copy-start | bytes 589828
  16.5 3.6 %copy-start.6 = (f32[16,8,384]{2,1,0:T(8,128)}, f32[16,8,384]{2,1,0:T(8,128)S(1)}, u32[]{:S(2)}) copy-start(f32[16,8,384]{2,1,0:T(8,128)S(1)} %collective-permute-done.2.x_corner) | copy-start | bytes 589828
  16.6 3.6 %copy-start.1 = (f32[16,24,384]{2,1,0:T(8,128)}, f32[16,24,384]{2,1,0:T(8,128)S(1)}, u32[]{:S(2)}) copy-start(f32[16,24,384]{2,1,0:T(8,128)S(1)} %collective-permute-done.x_right) | copy-start | bytes 1769476
  16.6 23.3 %collective-permute-start.3 = (f32[16,24,384]{2,1,0:T(8,128)}, f32[16,24,384]{2,1,0:T(8,128)}, u32[]{:S(2)}, u32[]{:S(2)}) collective-permute-start(f32[16,24,384]{2,1,0:T(8,128)} %get-tuple-element.84), channel_id=1, source_target_pairs={{4,0},{8,4},{12,8},{0,12},{20,16},{24,20},{28,24},{16,28},{5,1},{9... | collective-permute-start | bytes 1769480 | tf_op jit(solution)/shard_map/ppermute | solution.py:1016
  18.2 20.9 %collective-permute-start.4 = (f32[16,8,384]{2,1,0:T(8,128)}, f32[16,8,384]{2,1,0:T(8,128)}, u32[]{:S(2)}, u32[]{:S(2)}) collective-permute-start(f32[16,8,384]{2,1,0:T(8,128)} %get-tuple-element.85), channel_id=1, source_target_pairs={{16,0},{20,4},{24,8},{28,12},{0,16},{4,20},{8,24},{12,28},{17,1},{... | collective-permute-start | bytes 589832 | tf_op jit(solution)/shard_map/ppermute | solution.py:1016
  19.8 20.1 %collective-permute-start.5 = (f32[16,8,384]{2,1,0:T(8,128)}, f32[16,8,384]{2,1,0:T(8,128)}, u32[]{:S(2)}, u32[]{:S(2)}) collective-permute-start(f32[16,8,384]{2,1,0:T(8,128)} %get-tuple-element.86), channel_id=1, source_target_pairs={{20,0},{24,4},{28,8},{16,12},{4,16},{8,20},{12,24},{0,28},{21,1},{... | collective-permute-start | bytes 589832 | tf_op jit(solution)/shard_map/ppermute | solution.py:1016
  37.2 20.0 %collective-permute-start.6 = (f32[16,24,384]{2,1,0:T(8,128)}, f32[16,24,384]{2,1,0:T(8,128)}, u32[]{:S(2)}, u32[]{:S(2)}) collective-permute-start(f32[16,24,384]{2,1,0:T(8,128)} %get-tuple-element.104), channel_id=1, source_target_pairs={{12,0},{0,4},{4,8},{8,12},{28,16},{16,20},{20,24},{24,28},{13,1},{... | collective-permute-start | bytes 1769480 | tf_op jit(solution)/shard_map/ppermute | solution.py:1016
  37.4 19.8 %collective-permute-start.7 = (f32[16,8,384]{2,1,0:T(8,128)}, f32[16,8,384]{2,1,0:T(8,128)S(1)}, u32[]{:S(2)}, u32[]{:S(2)}) collective-permute-start(f32[16,8,384]{2,1,0:T(8,128)} %get-tuple-element.105), channel_id=1, source_target_pairs={{16,0},{20,4},{24,8},{28,12},{0,16},{4,20},{8,24},{12,28},{17,1},{... | collective-permute-start | bytes 589832 | tf_op jit(solution)/shard_map/ppermute | solution.py:1016
  39.0 18.2 %collective-permute-start.8 = (f32[16,8,384]{2,1,0:T(8,128)}, f32[16,8,384]{2,1,0:T(8,128)S(1)}, u32[]{:S(2)}, u32[]{:S(2)}) collective-permute-start(f32[16,8,384]{2,1,0:T(8,128)} %get-tuple-element.106), channel_id=1, source_target_pairs={{28,0},{16,4},{20,8},{24,12},{12,16},{0,20},{4,24},{8,28},{29,1},{... | collective-permute-start | bytes 589832 | tf_op jit(solution)/shard_map/ppermute | solution.py:1016
  57.2 25.2 %copy-start.3 = (f32[16,8,384]{2,1,0:T(8,128)}, f32[16,8,384]{2,1,0:T(8,128)S(1)}, u32[]{:S(2)}) copy-start(f32[16,8,384]{2,1,0:T(8,128)S(1)} %collective-permute-done.7.refs_3_) | copy-start | bytes 589828
  57.2 25.2 %copy-start.4 = (f32[16,8,384]{2,1,0:T(8,128)}, f32[16,8,384]{2,1,0:T(8,128)S(1)}, u32[]{:S(2)}) copy-start(f32[16,8,384]{2,1,0:T(8,128)S(1)} %collective-permute-done.8.refs_4_) | copy-start | bytes 589828
  57.2 2.1 %collective-permute-start.9 = (f32[16,32,128]{2,1,0:T(8,128)}, f32[16,32,128]{2,1,0:T(8,128)S(1)}, u32[]{:S(2)}, u32[]{:S(2)}) collective-permute-start(f32[16,32,128]{2,1,0:T(8,128)} %get-tuple-element.107), channel_id=1, source_target_pairs={{0,4},{4,0},{1,5},{5,1},{2,6},{6,2},{3,7},{7,3},{8,12},{12,8},{9,1... | collective-permute-start | bytes 786440 | tf_op jit(solution)/shard_map/ppermute | solution.py:1024
  58.0 24.5 %collective-permute-start.10 = (f32[16,24,384]{2,1,0:T(8,128)}, f32[16,24,384]{2,1,0:T(8,128)S(1)}, u32[]{:S(2)}, u32[]{:S(2)}) collective-permute-start(f32[16,24,384]{2,1,0:T(8,128)} %get-tuple-element.116), channel_id=1, source_target_pairs={{12,0},{0,4},{4,8},{8,12},{28,16},{16,20},{20,24},{24,28},{13,1},{... | collective-permute-start | bytes 1769480 | tf_op jit(solution)/shard_map/ppermute | solution.py:1016
  61.0 17.1 %all-to-all-start.1 = ((f32[16,32,128]{2,1,0:T(8,128)}), f32[16,32,128]{2,1,0:T(8,128)S(1)}, u32[]{:S(2)}, u32[]{:S(2)}) async-start(f32[16,32,128]{2,1,0:T(8,128)} %add.3), calls=%async_computation.1 | async-start | bytes 524288 | tf_op jit(solution)/shard_map/all_to_all | solution.py:1020
  66.9 15.5 %collective-permute-start.11 = (f32[16,8,384]{2,1,0:T(8,128)}, f32[16,8,384]{2,1,0:T(8,128)S(1)}, u32[]{:S(2)}, u32[]{:S(2)}) collective-permute-start(f32[16,8,384]{2,1,0:T(8,128)} %get-tuple-element.117), channel_id=1, source_target_pairs={{16,0},{20,4},{24,8},{28,12},{0,16},{4,20},{8,24},{12,28},{17,1},{... | collective-permute-start | bytes 589832 | tf_op jit(solution)/shard_map/ppermute | solution.py:1016
  68.8 13.6 %collective-permute-start.12 = (f32[16,8,384]{2,1,0:T(8,128)}, f32[16,8,384]{2,1,0:T(8,128)S(1)}, u32[]{:S(2)}, u32[]{:S(2)}) collective-permute-start(f32[16,8,384]{2,1,0:T(8,128)} %get-tuple-element.118), channel_id=1, source_target_pairs={{28,0},{16,4},{20,8},{24,12},{12,16},{0,20},{4,24},{8,28},{29,1},{... | collective-permute-start | bytes 589832 | tf_op jit(solution)/shard_map/ppermute | solution.py:1016
  78.8 13.1 %all-to-all-start.2 = ((f32[16,32,128]{2,1,0:T(8,128)}), f32[16,32,128]{2,1,0:T(8,128)S(1)}, u32[]{:S(2)}, u32[]{:S(2)}) async-start(f32[16,32,128]{2,1,0:T(8,128)} %shard_map.336.sums_ref), calls=%async_computation.2 | async-start | bytes 524288 | tf_op jit(solution)/shard_map/all_to_all | solution.py:1020
  82.4 0.7 copy-start.8
  82.4 1.0 %copy-start.2 = (f32[16,24,384]{2,1,0:T(8,128)}, f32[16,24,384]{2,1,0:T(8,128)S(1)}, u32[]{:S(2)}) copy-start(f32[16,24,384]{2,1,0:T(8,128)S(1)} %collective-permute-done.10.refs_7_) | copy-start | bytes 1769476
  92.0 1.5 %collective-permute-start.13 = (f32[16,32,128]{2,1,0:T(8,128)S(1)}, f32[16,32,128]{2,1,0:T(8,128)S(1)}, u32[]{:S(2)}, u32[]{:S(2)}) collective-permute-start(f32[16,32,128]{2,1,0:T(8,128)S(1)} %all-to-all-done.2.mine_ref), channel_id=1, source_target_pairs={{0,4},{4,0},{1,5},{5,1},{2,6},{6,2},{3,7},{7,3},{8,12},{12,8},{9,1... | collective-permute-start | bytes 786440 | tf_op jit(solution)/shard_map/ppermute | solution.py:1024
  (2 other events, 1.3 us)
